TPU v7x, 128 devices: a whole 4x4x4 slice. The times are simulated.
128 devices in a mesh: sp: 16 (over x, y), wt: 8 (over z, core).
Axes of the slice: x: 4, y: 4, z: 4, core: 2. Of those that a mesh axis runs over, the one named last changes fastest.
Arguments:
- tokens: bfloat16 [8192, 1024], P('sp'), may hold values from -6 to 6
- norm_in: float32 [1024], replicated, may hold values from 0.5 to 1.5
- w_query: bfloat16 [1024, 1024], P(None, 'wt'), may hold values from -0.1875 to 0.1875
- w_key: bfloat16 [1024, 512], P(None, 'wt'), may hold values from -0.1875 to 0.1875
- w_value: bfloat16 [1024, 512], P(None, 'wt'), may hold values from -0.1875 to 0.1875
- query_gain: float32 [64], replicated, may hold values from 0.5 to 1.5
- key_gain: float32 [64], replicated, may hold values from 0.5 to 1.5
- w_out: bfloat16 [1024, 1024], P('wt'), may hold values from -1.5 to 1.5
- norm_mid: float32 [1024], replicated, may hold values from 0.5 to 1.5
- w_gate: bfloat16 [1024, 4608], P(None, 'wt'), may hold values from -0.1875 to 0.1875
- w_up: bfloat16 [1024, 4608], P(None, 'wt'), may hold values from -0.1875 to 0.1875
- w_down: bfloat16 [4608, 1024], P('wt'), may hold values from -0.09375 to 0.09375
- cotangent: bfloat16 [8192, 1024], P('sp'), may hold values from -6 to 6
- lengths: int32 [4], replicated, may hold values from 1 to 7936, as said below
Outputs:
- output: bfloat16 [8192, 1024], P('sp')
- grad_tokens: bfloat16 [8192, 1024], P('sp')
- grad_norm_in: float32 [1024], replicated
- grad_w_query: float32 [1024, 1024], P(None, 'wt')
- grad_w_key: float32 [1024, 512], P(None, 'wt')
- grad_w_value: float32 [1024, 512], P(None, 'wt')
- grad_query_gain: float32 [64], replicated
- grad_key_gain: float32 [64], replicated
- grad_w_out: float32 [1024, 1024], P('wt')
- grad_norm_mid: float32 [1024], replicated
- grad_w_gate: float32 [1024, 4608], P(None, 'wt')
- grad_w_up: float32 [1024, 4608], P(None, 'wt')
- grad_w_down: float32 [4608, 1024], P('wt')
Inputs may be any that keep to these rules, and one draw needn't show every extreme that they name: `lengths`: every length is at least 1, they sum to 8192, and exactly one is 7936.
All inputs are finite; a program needn't handle non-finite values.
Results may differ from a plain program's by a relative error of at most 0.028.
Values may be sent and summed in bfloat16 or wider, within the bound.
A program may use at most 128 MiB of HBM per device.

v0:
```python
import jax
import jax.numpy as jnp
from jax import lax
from jax.sharding import PartitionSpec as P

eps = 1e-05
theta = 1000000.0


def rms_scale(values):
    return lax.rsqrt(jnp.mean(values * values, axis=-1, keepdims=True) + eps)


def norm_back(values, scale, gain, grad):
    scaled = grad * gain
    inner = jnp.mean(scaled * values, axis=-1, keepdims=True)
    return scale * scaled - values * scale * scale * scale * inner


def rope_tables(positions, head_dim):
    freqs = theta ** (-(jnp.arange(head_dim // 2).astype(jnp.float32) * 2.0) / head_dim)
    angles = positions.astype(jnp.float32)[:, None] * freqs[None, :]
    angles = jnp.concatenate([angles, angles], axis=-1)
    return (jnp.cos(angles), jnp.sin(angles))


def rotate(values, cosine, sine):
    half = values.shape[-1] // 2
    turned = jnp.concatenate([-values[..., half:], values[..., :half]], axis=-1)
    return values * cosine + turned * sine


def rotate_back(grad, cosine, sine):
    half = grad.shape[-1] // 2
    turned = grad * sine
    return grad * cosine + jnp.concatenate([turned[..., half:], -turned[..., :half]], axis=-1)


def segments_of(token_ids, lengths):
    ends = jnp.cumsum(lengths)
    segment = jnp.sum((token_ids[:, None] >= ends[None, :]).astype(jnp.int32), axis=1)
    starts = ends - lengths
    which = segment[:, None] == jnp.arange(lengths.shape[0])[None, :]
    start_of = jnp.sum(jnp.where(which, starts[None, :], 0), axis=1)
    return (segment, token_ids - start_of)


def body(
    tokens,
    norm_in,
    w_query,
    w_key,
    w_value,
    query_gain,
    key_gain,
    w_out,
    norm_mid,
    w_gate,
    w_up,
    w_down,
    cotangent,
    lengths,
):
    f32 = jnp.float32
    bf16 = jnp.bfloat16
    rows = tokens.shape[0]
    parts = lax.axis_size("sp")
    block_id = lax.axis_index("sp")
    head_dim = query_gain.shape[0]
    q_width = w_query.shape[1]
    kv_width = w_key.shape[1]
    q_heads = q_width // head_dim
    kv_local = kv_width // head_dim
    group = q_heads // kv_local
    total = rows * parts
    piece = rows // parts
    scale = head_dim ** (-0.5)
    block = min(512, total)
    count = total // block
    own_ids = block_id * rows + jnp.arange(rows)
    own_seg, own_pos = segments_of(own_ids, lengths)
    cosine, sine = rope_tables(own_pos, head_dim)
    cosine = cosine[:, None, :]
    sine = sine[:, None, :]
    ranks = jnp.arange(parts)
    my_order = (ranks + block_id) % parts
    inverse = jnp.zeros((parts,), jnp.int32).at[my_order].set(ranks)
    my_column = (ranks + block_id) % parts
    unit_ids = (
        ranks[:, None] * rows + my_column[:, None] * piece + jnp.arange(piece)[None, :]
    ).reshape(rows)
    unit_seg, unused_pos = segments_of(unit_ids, lengths)
    key_ids_all = jnp.arange(total)
    key_seg_all, unused_key_pos = segments_of(key_ids_all, lengths)

    def to_units(array):
        return array.reshape(parts, piece, -1)[my_order].reshape(rows, -1)

    def from_units(array):
        return array.reshape(parts, piece, -1)[inverse].reshape(rows, -1)

    base = tokens.astype(f32)
    scale_in = rms_scale(base)
    normed = (base * scale_in * norm_in).astype(bf16)
    q_proj = jnp.dot(normed, w_query, preferred_element_type=f32).reshape(rows, q_heads, head_dim)
    q_scale = rms_scale(q_proj)
    queries = (
        rotate(q_proj * q_scale * query_gain, cosine, sine).astype(bf16).reshape(rows, q_width)
    )
    k_proj = jnp.dot(normed, w_key, preferred_element_type=f32).reshape(rows, kv_local, head_dim)
    k_scale = rms_scale(k_proj)
    keys = rotate(k_proj * k_scale * key_gain, cosine, sine).astype(bf16).reshape(rows, kv_width)
    values = jnp.dot(normed, w_value, preferred_element_type=f32).astype(bf16)
    unit_queries = lax.all_to_all(to_units(queries), "sp", split_axis=0, concat_axis=0, tiled=True)
    unit_q = unit_queries.reshape(rows, kv_local, group, head_dim)
    whole_keys, whole_values = (
        lax.all_gather(keys, "sp", axis=0, tiled=True),
        lax.all_gather(values, "sp", axis=0, tiled=True),
    )

    def block_scores(keys_all, index):
        start = index * block
        key_block = lax.dynamic_slice_in_dim(keys_all, start, block, 0).reshape(
            block, kv_local, head_dim
        )
        scores = jnp.einsum("tgjd,sgd->gjts", unit_q, key_block, preferred_element_type=f32) * scale
        key_ids = lax.dynamic_slice_in_dim(key_ids_all, start, block, 0)
        key_segs = lax.dynamic_slice_in_dim(key_seg_all, start, block, 0)
        allowed = (key_ids[None, :] <= unit_ids[:, None]) & (key_segs[None, :] == unit_seg[:, None])
        return (jnp.where(allowed[None, None], scores, -1e30), key_block)

    def value_slice(values_all, index):
        return lax.dynamic_slice_in_dim(values_all, index * block, block, 0).reshape(
            block, kv_local, head_dim
        )

    indices = jnp.arange(count)

    def lse_step(carry, index):
        largest, weight_sum = carry
        scores, unused_block = block_scores(whole_keys, index)
        new_max = jnp.maximum(largest, jnp.max(scores, axis=-1))
        weight_sum = weight_sum * jnp.exp(largest - new_max) + jnp.sum(
            jnp.exp(scores - new_max[..., None]), axis=-1
        )
        return ((new_max, weight_sum), None)

    start_max = jnp.full((kv_local, group, rows), -1e30, f32)
    start_sum = jnp.zeros((kv_local, group, rows), f32)
    (largest, weight_sum), unused_out = lax.scan(lse_step, (start_max, start_sum), indices)
    log_sum = largest + jnp.log(weight_sum)

    def out_step(running, index):
        scores, unused_block = block_scores(whole_keys, index)
        probs = jnp.exp(scores - log_sum[..., None]).astype(bf16)
        return (
            running
            + jnp.einsum(
                "gjts,sgd->tgjd",
                probs,
                value_slice(whole_values, index),
                preferred_element_type=f32,
            ),
            None,
        )

    unit_full, unused_out = lax.scan(
        out_step, jnp.zeros((rows, kv_local, group, head_dim), f32), indices
    )
    unit_out = unit_full.reshape(rows, q_width).astype(bf16)
    mixed = from_units(lax.all_to_all(unit_out, "sp", split_axis=0, concat_axis=0, tiled=True))
    attn = lax.psum(
        jnp.dot(mixed, w_out, preferred_element_type=f32).astype(jnp.bfloat16), "wt"
    ).astype(jnp.float32)
    middle = base + attn
    scale_mid = rms_scale(middle)
    normed_mid = (middle * scale_mid * norm_mid).astype(bf16)
    gate = jnp.dot(normed_mid, w_gate, preferred_element_type=f32)
    up_proj = jnp.dot(normed_mid, w_up, preferred_element_type=f32)
    sigmoid_gate = jax.nn.sigmoid(gate)
    act = (gate * sigmoid_gate * up_proj).astype(bf16)
    mlp = lax.psum(
        jnp.dot(act, w_down, preferred_element_type=f32).astype(jnp.bfloat16), "wt"
    ).astype(jnp.float32)
    output = (middle + mlp).astype(bf16)
    g_down = jnp.einsum("tf,td->fd", act, cotangent, preferred_element_type=f32)
    d_act = jnp.einsum("td,fd->tf", cotangent, w_down, preferred_element_type=f32)
    d_gate = (d_act * up_proj * sigmoid_gate * (1.0 + gate * (1.0 - sigmoid_gate))).astype(bf16)
    d_up = (d_act * gate * sigmoid_gate).astype(bf16)
    g_gate = jnp.einsum("td,tf->df", normed_mid, d_gate, preferred_element_type=f32)
    g_up = jnp.einsum("td,tf->df", normed_mid, d_up, preferred_element_type=f32)
    d_mid_part = jnp.einsum("tf,df->td", d_gate, w_gate, preferred_element_type=f32) + jnp.einsum(
        "tf,df->td", d_up, w_up, preferred_element_type=f32
    )
    d_mid = lax.psum(d_mid_part.astype(jnp.bfloat16), "wt").astype(jnp.float32)
    g_norm_mid = jnp.sum(d_mid * middle * scale_mid, axis=0)
    d_middle = cotangent.astype(f32) + norm_back(middle, scale_mid, norm_mid, d_mid)
    d_attn = d_middle.astype(bf16)
    g_out = jnp.einsum("tq,td->qd", mixed, d_attn, preferred_element_type=f32)
    d_mixed = jnp.einsum("td,qd->tq", d_attn, w_out, preferred_element_type=f32).astype(bf16)
    unit_grad = lax.all_to_all(
        to_units(d_mixed), "sp", split_axis=0, concat_axis=0, tiled=True
    ).reshape(rows, kv_local, group, head_dim)
    keys_back, values_back = (
        lax.all_gather(keys, "sp", axis=0, tiled=True),
        lax.all_gather(values, "sp", axis=0, tiled=True),
    )
    delta = jnp.einsum("tgjd,tgjd->gjt", unit_grad.astype(f32), unit_full)

    def grad_step(running, index):
        scores, key_block = block_scores(keys_back, index)
        probs = jnp.exp(scores - log_sum[..., None])
        d_probs = jnp.einsum(
            "tgjd,sgd->gjts", unit_grad, value_slice(values_back, index), preferred_element_type=f32
        )
        d_scores = (probs * (d_probs - delta[..., None])).astype(bf16)
        running = (
            running
            + jnp.einsum("gjts,sgd->tgjd", d_scores, key_block, preferred_element_type=f32) * scale
        )
        d_key_block = (
            jnp.einsum("gjts,tgjd->sgd", d_scores, unit_q, preferred_element_type=f32) * scale
        )
        d_value_block = jnp.einsum(
            "gjts,tgjd->sgd", probs.astype(bf16), unit_grad, preferred_element_type=f32
        )
        return (
            running,
            (d_key_block.reshape(block, kv_width), d_value_block.reshape(block, kv_width)),
        )

    unit_dq, (d_key_blocks, d_value_blocks) = lax.scan(
        grad_step, jnp.zeros((rows, kv_local, group, head_dim), f32), indices
    )
    d_keys_own, d_values_own = (
        lax.psum_scatter(
            d_key_blocks.reshape(total, kv_width).astype(jnp.bfloat16),
            "sp",
            scatter_dimension=0,
            tiled=True,
        ).astype(jnp.float32),
        lax.psum_scatter(
            d_value_blocks.reshape(total, kv_width).astype(jnp.bfloat16),
            "sp",
            scatter_dimension=0,
            tiled=True,
        ).astype(jnp.float32),
    )
    unit_dq = unit_dq.reshape(rows, q_width).astype(bf16)
    d_queries = (
        from_units(lax.all_to_all(unit_dq, "sp", split_axis=0, concat_axis=0, tiled=True))
        .astype(f32)
        .reshape(rows, q_heads, head_dim)
    )
    d_q_normed = rotate_back(d_queries, cosine, sine)
    gq_part = jnp.sum(d_q_normed * q_proj * q_scale, axis=(0, 1))
    d_q_proj = (
        norm_back(q_proj, q_scale, query_gain, d_q_normed).reshape(rows, q_width).astype(bf16)
    )
    d_k_rot = d_keys_own.astype(bf16).astype(f32).reshape(rows, kv_local, head_dim)
    d_k_normed = rotate_back(d_k_rot, cosine, sine)
    gk_part = jnp.sum(d_k_normed * k_proj * k_scale, axis=(0, 1))
    d_k_proj = norm_back(k_proj, k_scale, key_gain, d_k_normed).reshape(rows, kv_width).astype(bf16)
    d_vals = d_values_own.astype(bf16)
    g_query = jnp.einsum("td,tq->dq", normed, d_q_proj, preferred_element_type=f32)
    g_key = jnp.einsum("td,tq->dq", normed, d_k_proj, preferred_element_type=f32)
    g_value = jnp.einsum("td,tq->dq", normed, d_vals, preferred_element_type=f32)
    d_normed_part = jnp.einsum("tq,dq->td", d_q_proj, w_query, preferred_element_type=f32)
    d_normed_part = d_normed_part + jnp.einsum(
        "tq,dq->td", d_k_proj, w_key, preferred_element_type=f32
    )
    d_normed_part = d_normed_part + jnp.einsum(
        "tq,dq->td", d_vals, w_value, preferred_element_type=f32
    )
    d_normed, gq_sum, gk_sum = (
        lax.psum(d_normed_part.astype(jnp.bfloat16), "wt").astype(jnp.float32),
        lax.psum(gq_part.astype(jnp.bfloat16), "wt").astype(jnp.float32),
        lax.psum(gk_part.astype(jnp.bfloat16), "wt").astype(jnp.float32),
    )
    g_norm_in = jnp.sum(d_normed * base * scale_in, axis=0)
    grad_tokens = (d_middle + norm_back(base, scale_in, norm_in, d_normed)).astype(bf16)
    g_norm_in, g_query, g_key, g_value, gq_sum, gk_sum, g_out, g_norm_mid, g_gate, g_up, g_down = (
        lax.psum(g_norm_in.astype(jnp.bfloat16), "sp").astype(jnp.float32),
        lax.psum(g_query.astype(jnp.bfloat16), "sp").astype(jnp.float32),
        lax.psum(g_key.astype(jnp.bfloat16), "sp").astype(jnp.float32),
        lax.psum(g_value.astype(jnp.bfloat16), "sp").astype(jnp.float32),
        lax.psum(gq_sum.astype(jnp.bfloat16), "sp").astype(jnp.float32),
        lax.psum(gk_sum.astype(jnp.bfloat16), "sp").astype(jnp.float32),
        lax.psum(g_out.astype(jnp.bfloat16), "sp").astype(jnp.float32),
        lax.psum(g_norm_mid.astype(jnp.bfloat16), "sp").astype(jnp.float32),
        lax.psum(g_gate.astype(jnp.bfloat16), "sp").astype(jnp.float32),
        lax.psum(g_up.astype(jnp.bfloat16), "sp").astype(jnp.float32),
        lax.psum(g_down.astype(jnp.bfloat16), "sp").astype(jnp.float32),
    )
    return (
        output,
        grad_tokens,
        g_norm_in,
        g_query,
        g_key,
        g_value,
        gq_sum,
        gk_sum,
        g_out,
        g_norm_mid,
        g_gate,
        g_up,
        g_down,
    )


def solution(mesh):
    placed = (
        P("sp", None),
        P(),
        P(None, "wt"),
        P(None, "wt"),
        P(None, "wt"),
        P(),
        P(),
        P("wt", None),
        P(),
        P(None, "wt"),
        P(None, "wt"),
        P("wt", None),
        P("sp", None),
        P(),
    )
    return jax.shard_map(
        body,
        mesh=mesh,
        in_specs=placed,
        out_specs=(
            P("sp", None),
            P("sp", None),
            P(),
            P(None, "wt"),
            P(None, "wt"),
            P(None, "wt"),
            P(),
            P(),
            P("wt", None),
            P(),
            P(None, "wt"),
            P(None, "wt"),
            P("wt", None),
        ),
        check_vma=False,
    )
```

profile of v0, /device:TPU:1, one launch (start us, length us, event | category | flops | bytes accessed | tf_op | source)
XLA Modules:
  0.0 991.5 jit_solution(8828904695562201513)
XLA Ops:
  24.3 7.6 all-to-all-start
  35.9 2.9 all-to-all-done
  39.7 19.0 %all-gather.5.cloned.1.call-done = bf16[8192,64]{0,1:T(8,128)(2,1)} async-done(((bf16[512,64]{0,1:T(8,128)(2,1)}), bf16[8192,64]{0,1:T(8,128)(2,1)}) %all-gather.5.cloned.1.call-update) | async-done | bytes 1048592 | tf_op jit(solution)/shard_map/all_gather | solution.py:117
  59.8 115.5 %while.39 = (s32[]{:T(128)}, f32[1,2,512]{2,1,0:T(2,128)S(1)}, f32[1,2,512]{2,1,0:T(2,128)S(1)}, s32[16]{0:T(128)}, s32[8192]{0:T(1024)}, /*index=5*/s32[8192]{0...) while((s32[]{:T(128)}, f32[1,2,512]{2,1,0:T(2,128)S(1)}, ...), condition=%wide.region_11.12_spmd.clone, body=%wide.region_8.11_spmd.clone.sunk | while | flops 71570952 | bytes 5253398 | solution.py:150
  175.4 84.0 %while.40 = (s32[]{:T(128)}, f32[512,1,2,64]{0,3,2,1:T(8,128)}, s32[16]{0:T(128)S(1)}, bf16[8192,64]{0,1:T(8,128)(2,1)}, s32[8192]{0:T(1024)S(1)}, /*index=5*/s3...) while((s32[]{:T(128)}, f32[512,1,2,64]{0,3,2,1:T(8,128)}, ...), condition=%wide.region_13.14_spmd.clone, body=%wide.region_12.13_spmd.clone.sunk | while | flops 137232896 | bytes 1339160 | solution.py:167
  177.9 2.6 fusion.176
  183.0 2.7 fusion.176
  188.3 2.7 fusion.176
  193.5 2.7 fusion.176
  198.8 2.7 fusion.176
  204.1 2.7 fusion.176
  209.3 2.7 fusion.176
  214.6 2.7 fusion.176
  219.8 2.7 fusion.176
  225.1 2.7 fusion.176
  230.3 2.7 fusion.176
  235.6 2.7 fusion.176
  240.8 2.7 fusion.176
  246.1 2.7 fusion.176
  251.4 2.7 fusion.176
  256.6 2.7 fusion.176
  262.0 4.4 all-to-all-start.1
  266.5 6.6 all-to-all-done.1
  275.3 61.7 %all-reduce.9.cloned.1.call-done = bf16[512,1024]{1,0:T(8,128)(2,1)} async-done(((bf16[512,1024]{1,0:T(8,128)(2,1)}), bf16[512,1024]{1,0:T(8,128)(2,1)}) %all-reduce.9.cloned.1.call-update) | async-done | bytes 1048592 | tf_op jit(solution)/shard_map/psum | solution.py:172
  343.0 2.2 multiply_convert_fusion.1
  348.2 62.0 %all-reduce.11.cloned.1.call-done = bf16[512,1024]{1,0:T(8,128)(2,1)} async-done(((bf16[512,1024]{1,0:T(8,128)(2,1)}), bf16[512,1024]{1,0:T(8,128)(2,1)}) %all-reduce.11.cloned.1.call-update) | async-done | bytes 1048592 | tf_op jit(solution)/shard_map/psum | solution.py:195
  410.2 2.8 fusion.76
  413.0 2.2 fusion.73
  418.9 6.5 all-to-all-start.2
  425.7 6.4 all-to-all-done.2
  433.5 210.0 %while.41 = (s32[]{:T(128)}, f32[512,1,2,64]{0,3,2,1:T(8,128)}, bf16[16,512,64]{1,2,0:T(8,128)(2,1)}, bf16[16,512,64]{1,2,0:T(8,128)(2,1)}, s32[16]{0:T(128)}, /...) while((s32[]{:T(128)}, f32[512,1,2,64]{0,3,2,1:T(8,128)}, ...), condition=%wide.region_21.22_spmd.clone, body=%wide.region_20.21_spmd.clone.sunk | while | flops 340230656 | bytes 20151704 | solution.py:232
  443.8 2.7 fusion.191
  457.0 2.7 fusion.191
  470.1 2.7 fusion.191
  483.3 2.7 fusion.191
  496.4 2.7 fusion.191
  509.5 2.7 fusion.191
  522.7 2.7 fusion.191
  535.8 2.7 fusion.191
  548.9 2.7 fusion.191
  562.1 2.7 fusion.191
  575.2 2.7 fusion.191
  588.3 2.7 fusion.191
  601.5 2.7 fusion.191
  614.6 2.7 fusion.191
  627.8 2.7 fusion.191
  640.9 2.7 fusion.191
  643.6 2.3 copy.102
  647.7 3.2 convolution_convert_fusion
  650.9 3.3 convolution_convert_fusion.1
  657.1 3.5 all-to-all-start.3
  660.6 3.1 convolution_convert_fusion.4
  664.9 2.3 all-to-all-done.3
  673.7 2.7 fusion.108
  676.5 40.1 %reduce-scatter.3.cloned.1.call-done = bf16[512,64]{0,1:T(8,128)(2,1)} async-done(((bf16[8192,64]{0,1:T(8,128)(2,1)}), bf16[512,64]{0,1:T(8,128)(2,1)}) %reduce-scatter.3.cloned.1.call-update) | async-done | bytes 65552 | tf_op jit(solution)/shard_map/reduce_scatter | solution.py:236
  721.8 70.9 %reduce-scatter.5.cloned.1.call-done = bf16[512,64]{0,1:T(8,128)(2,1)} async-done(((bf16[8192,64]{0,1:T(8,128)(2,1)}), bf16[512,64]{0,1:T(8,128)(2,1)}) %reduce-scatter.5.cloned.1.call-update) | async-done | bytes 65552 | tf_op jit(solution)/shard_map/reduce_scatter | solution.py:242
  792.7 3.7 add_convert_fusion
  797.3 2.7 convolution_convert_fusion.5
  803.2 14.3 %all-reduce.2 = (bf16[64]{0:T(256)(128)(2,1)S(1)}, bf16[64]{0:T(256)(128)(2,1)S(1)}) all-reduce(bf16[64]{0:T(256)(128)(2,1)S(1)} %reduce_sum.177, bf16[64]{0:T(256)(128)(2,1)S(1)} %get-tuple-element.410), channel_id=1, replica_groups=mesh['sp'=16,'wt'=8] {'wt'}, use_global_device_ids=true, to_apply=%region_35.36 | all-reduce | flops 128 | bytes 512 | tf_op jit(solution)/shard_map/psum | solution.py:277
  817.5 44.3 %all-reduce.15.cloned.1.call-done = (bf16[512,1024]{1,0:T(8,128)(2,1)}, bf16[512,1024]{1,0:T(8,128)(2,1)}) async-done(((bf16[512,1024]{1,0:T(8,128)(2,1)}, bf16[512,1024]{1,0:T(8,128)(2,1)}), (bf16[512,1024]{1,0:T(8,128)(2,1)}, bf16[512,1024]{1,0:T(8,128)(2,1)})) %all-reduce.15.cloned.1.call-update) | async-done | bytes 2097168 | tf_op jit(solution)/shard_map/psum | solution.py:182
  864.0 34.7 %all-reduce = (bf16[1024]{0:T(1024)(128)(2,1)S(1)}, bf16[64]{0:T(256)(128)(2,1)S(1)}, bf16[64]{0:T(256)(128)(2,1)S(1)}, bf16[1024]{0:T(1024)(128)(2,1)S(1)}) all-reduce(bf16[1024]{0:T(1024)(128)(2,1)S(1)} %get-tuple-element.408, bf16[64]{0:T(256)(128)(2,1)S(1)} %get-tuple-element.497, ...), channel_id=1, replica_groups=mesh['sp'=16,'wt'=8] {'sp'}, use_global_device_ids=true, to_apply=%region_29.30 | all-reduce | flops 2176 | bytes 8704 | tf_op jit(solution)/shard_map/psum | solution.py:283
  900.8 4.5 fusion.71
  905.4 69.7 %all-reduce.13.cloned.1.call-done = (bf16[1024,128]{1,0:T(8,128)(2,1)}, bf16[1024,64]{0,1:T(8,128)(2,1)}, bf16[1024,64]{0,1:T(8,128)(2,1)}, bf16[128,1024]{1,0:T...) async-done(((bf16[1024,128]{1,0:T(8,128)(2,1)}, bf16[1024,64]{0,1:T(8,128)(2,1)}, bf16[1024,64]{0,1:T(8,128)(2,1)}, ...) | async-done | bytes 4325392 | tf_op jit(solution)/shard_map/psum | solution.py:284
  975.0 3.1 convert_element_type.283
  (818 shorter events, 364.1 us)
Async XLA Ops:
  7.2 335.4 %copy-start = (bf16[576,1024]{1,0:T(8,128)(2,1)S(1)}, bf16[576,1024]{1,0:T(8,128)(2,1)}, u32[]{:S(2)}) copy-start(bf16[576,1024]{1,0:T(8,128)(2,1)} %param.31) | copy-start | bytes 3538948
  7.2 51.5 %all-gather.5.cloned.1.call-start = ((), (), s32[]{:S(2)}) async-start(), calls=%async_computation.7 | async-start | bytes 1114112 | tf_op jit(solution)/shard_map/all_gather | solution.py:117
  7.3 4.3 copy-start.56
  11.1 20.9 %copy-start.3 = (bf16[512,1024]{1,0:T(8,128)(2,1)}, bf16[512,1024]{1,0:T(8,128)(2,1)S(1)}, u32[]{:S(2)}) copy-start(bf16[512,1024]{1,0:T(8,128)(2,1)S(1)} %fusion.66) | copy-start | bytes 3145732
  13.2 4.7 copy-start.16
  13.7 8.3 copy-start.11
  13.9 4.9 copy-start.9
  13.9 5.9 copy-start.46
  16.9 5.0 copy-start.64
  21.8 13.3 %copy-start.69 = (s32[4,1]{0,1:T(1,128)S(1)}, s32[4,1]{0,1:T(1,128)}, u32[]{:S(2)}) copy-start(s32[4,1]{0,1:T(1,128)} %copy-done.68) | copy-start | bytes 52
  22.0 12.0 %copy-start.66 = (f32[128]{0:T(128)}, f32[128]{0:T(128)S(1)}, u32[]{:S(2)}) copy-start(f32[128]{0:T(128)S(1)} %mul.543) | copy-start | bytes 1540
  22.0 11.9 %copy-start.59 = (s32[1024]{0:T(1024)}, s32[1024]{0:T(1024)S(1)}, u32[]{:S(2)}) copy-start(s32[1024]{0:T(1024)S(1)} %pad_clamp_fusion.1) | copy-start | bytes 12292
  24.3 14.5 %all-to-all-start = ((bf16[16,32,128]{2,1,0:T(8,128)(2,1)}), bf16[16,32,128]{2,1,0:T(8,128)(2,1)S(1)}, u32[]{:S(2)}, u32[]{:S(2)}) async-start(bf16[16,32,128]{2,1,0:T(8,128)(2,1)} %gather_fusion), calls=%async_computation | async-start | bytes 262144 | tf_op jit(solution)/shard_map/all_to_all | solution.py:114
  31.9 143.4 %all-gather.3.cloned.1.call-start = ((), (), s32[]{:S(2)}) async-start(), calls=%async_computation.6 | async-start | bytes 1114112 | tf_op jit(solution)/shard_map/all_gather | solution.py:118
  175.3 91.1 %copy-start.73 = (s32[16]{0:T(128)S(1)}, s32[16]{0:T(128)}, u32[]{:S(2)}) copy-start(s32[16]{0:T(128)} %scatter_custom_fusion) | copy-start | bytes 196
  175.3 98.3 %copy-start.29 = (bf16[128,1024]{1,0:T(8,128)(2,1)S(1)}, bf16[128,1024]{1,0:T(8,128)(2,1)}, u32[]{:S(2)}) copy-start(bf16[128,1024]{1,0:T(8,128)(2,1)} %param.27) | copy-start | bytes 786436
  259.9 77.1 %copy-start.2 = (bf16[512,1024]{1,0:T(8,128)(2,1)S(1)}, bf16[512,1024]{1,0:T(8,128)(2,1)}, u32[]{:S(2)}) copy-start(bf16[512,1024]{1,0:T(8,128)(2,1)} %param.20) | copy-start | bytes 3145732
  262.0 11.1 %all-to-all-start.1 = ((bf16[16,32,128]{2,1,0:T(8,128)(2,1)}), bf16[16,32,128]{2,1,0:T(8,128)(2,1)S(1)}, u32[]{:S(2)}, u32[]{:S(2)}) async-start(bf16[16,32,128]{2,1,0:T(8,128)(2,1)} %convert_element_type.235), calls=%async_computation.1 | async-start | bytes 262144 | tf_op jit(solution)/shard_map/all_to_all | solution.py:171
  266.4 70.7 %all-reduce.9.cloned.1.call-start = ((), (), s32[]{:S(2)}) async-start(), calls=%async_computation.8 | async-start | bytes 2097152 | tf_op jit(solution)/shard_map/psum | solution.py:172
  266.5 7.2 copy-start.60
  273.7 65.2 %copy-start.53 = (f32[1024]{0:T(1024)S(1)}, f32[1024]{0:T(1024)}, u32[]{:S(2)}) copy-start(f32[1024]{0:T(1024)} %param.28) | copy-start | bytes 12292
  275.1 135.1 %all-reduce.11.cloned.1.call-start = ((), (), s32[]{:S(2)}) async-start(), calls=%async_computation.9 | async-start | bytes 2097152 | tf_op jit(solution)/shard_map/psum | solution.py:195
  415.3 17.3 %copy-start.31 = (f32[512,1,2,64]{0,3,2,1:T(8,128)S(1)}, f32[512,1,2,64]{0,3,2,1:T(8,128)}, u32[]{:S(2)}) copy-start(f32[512,1,2,64]{0,3,2,1:T(8,128)} %get-tuple-element.204) | copy-start | bytes 786436
  417.4 16.1 %copy-start.8 = (bf16[512,1,2,64]{0,3,2,1:T(8,128)(2,1)S(1)}, bf16[512,1,2,64]{0,3,2,1:T(8,128)(2,1)}, u32[]{:S(2)}) copy-start(bf16[512,1,2,64]{0,3,2,1:T(8,128)(2,1)} %get-tuple-element.918) | copy-start | bytes 393220
  417.4 16.1 %copy-start.62 = (f32[1,2,512]{2,1,0:T(2,128)S(1)}, f32[1,2,512]{2,1,0:T(2,128)}, u32[]{:S(2)}) copy-start(f32[1,2,512]{2,1,0:T(2,128)} %copy-done.61) | copy-start | bytes 12292
  418.9 13.2 %all-to-all-start.2 = ((bf16[16,32,128]{2,1,0:T(8,128)(2,1)}), bf16[16,32,128]{2,1,0:T(8,128)(2,1)S(1)}, u32[]{:S(2)}, u32[]{:S(2)}) async-start(bf16[16,32,128]{2,1,0:T(8,128)(2,1)} %gather_fusion.2), calls=%async_computation.2 | async-start | bytes 262144 | tf_op jit(solution)/shard_map/all_to_all | solution.py:201
  425.4 291.1 %reduce-scatter.3.cloned.1.call-start = ((), (), s32[]{:S(2)}) async-start(), calls=%async_computation.10 | async-start | bytes 1114112 | tf_op jit(solution)/shard_map/reduce_scatter | solution.py:236
  433.5 4.8 copy-start.48
  446.5 4.8 copy-start.48
  459.7 4.8 copy-start.48
  472.8 4.8 copy-start.48
  485.9 4.8 copy-start.48
  499.1 4.8 copy-start.48
  512.2 4.8 copy-start.48
  525.3 4.8 copy-start.48
  538.5 4.8 copy-start.48
  551.6 4.8 copy-start.48
  564.7 4.8 copy-start.48
  577.9 4.8 copy-start.48
  591.0 4.8 copy-start.48
  604.2 4.8 copy-start.48
  617.3 4.8 copy-start.48
  630.4 4.8 copy-start.48
  657.1 10.2 %all-to-all-start.3 = ((bf16[16,32,128]{2,1,0:T(8,128)(2,1)}), bf16[16,32,128]{2,1,0:T(8,128)(2,1)S(1)}, u32[]{:S(2)}, u32[]{:S(2)}) async-start(bf16[16,32,128]{2,1,0:T(8,128)(2,1)} %convert_element_type.251), calls=%async_computation.3 | async-start | bytes 262144 | tf_op jit(solution)/shard_map/all_to_all | solution.py:251
  660.6 132.2 %reduce-scatter.5.cloned.1.call-start = ((), (), s32[]{:S(2)}) async-start(), calls=%async_computation.11 | async-start | bytes 1114112 | tf_op jit(solution)/shard_map/reduce_scatter | solution.py:242
  663.8 6.6 copy-start.23
  664.8 5.6 copy-start.10
  664.8 5.6 copy-start.65
  664.9 197.0 %all-reduce.15.cloned.1.call-start = ((), (), s32[]{:S(2)}) async-start(), calls=%async_computation.13 | async-start | bytes 4194304 | tf_op jit(solution)/shard_map/psum | solution.py:182
  672.4 44.1 %copy-start.19 = (f32[512,32]{0,1:T(8,128)S(1)}, f32[512,32]{0,1:T(8,128)}, u32[]{:S(2)}) copy-start(f32[512,32]{0,1:T(8,128)} %copy-done.18) | copy-start | bytes 196612
  672.5 45.2 %copy-start.15 = (f32[512,64]{0,1:T(8,128)S(1)}, f32[512,64]{0,1:T(8,128)}, u32[]{:S(2)}) copy-start(f32[512,64]{0,1:T(8,128)} %copy-done.14) | copy-start | bytes 393220
  672.5 45.2 %copy-start.51 = (f32[512]{0:T(512)S(1)}, f32[512]{0:T(512)}, u32[]{:S(2)}) copy-start(f32[512]{0:T(512)} %copy-done.50) | copy-start | bytes 6148
  672.5 45.2 %copy-start.57 = (f32[64]{0:T(128)S(1)}, f32[64]{0:T(128)}, u32[]{:S(2)}) copy-start(f32[64]{0:T(128)} %param.26) | copy-start | bytes 772
  673.7 46.3 %copy-start.39 = (bf16[1024,64]{0,1:T(8,128)(2,1)S(1)}, bf16[1024,64]{0,1:T(8,128)(2,1)}, u32[]{:S(2)}) copy-start(bf16[1024,64]{0,1:T(8,128)(2,1)} %param.23) | copy-start | bytes 393220
  676.5 116.3 %copy-start.40 = (bf16[1024,64]{0,1:T(8,128)(2,1)S(1)}, bf16[1024,64]{0,1:T(8,128)(2,1)}, u32[]{:S(2)}) copy-start(bf16[1024,64]{0,1:T(8,128)(2,1)} %param.24) | copy-start | bytes 393220
  720.0 72.7 %copy-start.36 = (bf16[512,64]{0,1:T(8,128)(2,1)}, bf16[512,64]{0,1:T(8,128)(2,1)S(1)}, u32[]{:S(2)}) copy-start(bf16[512,64]{0,1:T(8,128)(2,1)S(1)} %subtract_convert_fusion) | copy-start | bytes 196612
  796.4 178.6 %all-reduce.13.cloned.1.call-start = ((), (), s32[]{:S(2)}) async-start(), calls=%async_computation.12 | async-start | bytes 8650752 | tf_op jit(solution)/shard_map/psum | solution.py:284
  797.3 3.9 copy-start.37
  797.3 4.8 copy-start.41
  803.1 58.8 %copy-start.52 = (f32[1024]{0:T(1024)S(1)}, f32[1024]{0:T(1024)}, u32[]{:S(2)}) copy-start(f32[1024]{0:T(1024)} %param.21) | copy-start | bytes 12292
  803.1 58.8 %copy-start.55 = (f32[512]{0:T(512)S(1)}, f32[512]{0:T(512)}, u32[]{:S(2)}) copy-start(f32[512]{0:T(512)} %copy-done.54) | copy-start | bytes 6148
  803.1 60.8 %copy-start.58 = (bf16[1024]{0:T(1024)(128)(2,1)S(1)}, bf16[1024]{0:T(1024)(128)(2,1)}, u32[]{:S(2)}) copy-start(bf16[1024]{0:T(1024)(128)(2,1)} %get-tuple-element.406) | copy-start | bytes 6148
  803.1 97.7 %copy-start.6 = (bf16[512,1024]{1,0:T(8,128)(2,1)S(1)}, bf16[512,1024]{1,0:T(8,128)(2,1)}, u32[]{:S(2)}) copy-start(bf16[512,1024]{1,0:T(8,128)(2,1)} %all-reduce.9.cloned.1.call-done) | copy-start | bytes 3145732
  979.8 4.1 copy-start.44
  (70 other events, 150.8 us)
Sparse Core Ops, SparseCore 0:
  13.4 45.2 all-gather.4
  61.4 42.7 all-gather.2
  275.2 61.8 all-reduce.8
  348.3 61.8 all-reduce.10
  646.0 70.4 reduce-scatter.2
  720.5 72.1 reduce-scatter.4
  796.6 65.2 all-reduce.14
  867.2 107.7 all-reduce.12
where the time goes:
time: 999 us; the launch traced here: 991 us
  waiting for transfers between devices  386 us (39%)
  matrix products  254 us (25%)
  local copies, waits for them, and re-layouts  156 us (16%)
  other arithmetic  75.9 us (8%)
  blocking collectives  48.9 us (5%)
  loops' own time  33 us (3%)
  starting transfers between devices  22.7 us (2%)
  between operations  15.2 us (2%)
    reduce_scatter x1, waiting for transfers between devices, body(): lax.psum_scatter(d_value_blocks.reshape(total, kv_width).astype(jnp.bfloa...  70.9 us
    psum x1, waiting for transfers between devices, body(): lax.psum(g_query.astype(jnp.bfloat16), 'sp').astype(jnp.float32)  69.7 us
    psum x1, waiting for transfers between devices, body(): d_mid = lax.psum(d_mid_part.astype(jnp.bfloat16), 'wt').astype(jnp.float32)  62 us
    psum x1, waiting for transfers between devices, body(): lax.psum(jnp.dot(mixed, w_out, preferred_element_type=f32).astype(jnp.bfl...  61.7 us
    dot_general x32, matrix products, block_scores(): jnp.einsum('tgjd,sgd->gjts', unit_q, key_block, preferred_element_type=f32)  59.1 us
    dynamic_slice x48, local copies, waits for them, and re-layouts, body(): lax.scan(lse_step, (start_max, start_sum), indices)  49.2 us
    psum x1, waiting for transfers between devices, body(): lax.psum(jnp.dot(act, w_down, preferred_element_type=f32).astype(jnp.bflo...  44.3 us
    dot_general x16, matrix products, out_step(): jnp.einsum('gjts,sgd->tgjd', probs, value_slice(whole_values, index), pre...  43.6 us
  transfers between devices with their start and end apart: 12, of which 11 were waited for; matrix products, arithmetic and copies ran while one was open for 17% of the time, Pallas kernels for 0%

commit v1 on v0

v1 whole, which is shorter than its diff:
```python
import functools, math
import jax
import jax.numpy as jnp
from jax import lax
from jax.experimental import pallas as pl
from jax.experimental.pallas import tpu as pltpu
from jax.sharding import PartitionSpec as P

f32 = jnp.float32
bf16 = jnp.bfloat16
CH = 512
HALF = 256
SCALE = 0.125
C2 = SCALE * math.log2(math.e)


def starts_of(ids, len_ref):
    end = jnp.int32(0)
    start = jnp.zeros_like(ids)
    for j in range(4):
        end = end + len_ref[j]
        start = start + jnp.where(ids >= end, len_ref[j], 0)
    return start


def scalar_start(row, len_ref):
    end = jnp.int32(0)
    start = jnp.int32(0)
    for j in range(4):
        end = end + len_ref[j]
        start = start + jnp.where(row >= end, len_ref[j], 0)
    return start


def key_ranges(r0, len_ref, ch):
    low = scalar_start(r0, len_ref)
    high = scalar_start(r0 + HALF - 1, len_ref)
    first = low // ch
    last = (r0 + HALF - 1) // ch + 1
    free = jnp.clip((high + ch - 1) // ch, first, last)
    diag = jnp.clip((r0 + 1) // ch, free, last)
    return first, free, diag, last


def lanes(shape):
    return lax.broadcasted_iota(jnp.int32, shape, len(shape) - 1)


def split3(value, lane):
    hi = value.astype(bf16).astype(f32)
    rest = value - hi
    mid = rest.astype(bf16).astype(f32)
    low = rest - mid
    return jnp.where(lane == 0, hi, jnp.where(lane == 1, mid, jnp.where(lane == 2, low, 0.0)))


def tile_row(me, t, parts):
    return me * 512 if t == 0 else (parts - 1 - me) * 512 + HALF


def fwd_kernel(parts, me_ref, len_ref, q_ref, kv_ref, mix_ref, out_ref, qa_ref, qs_ref, acc_ref):
    me = me_ref[0]
    lane = lanes((HALF, 128))
    lane2 = lanes((2 * HALF, 128))
    lanek = lanes((CH, 128))
    for t in range(2):
        r0 = tile_row(me, t, parts)
        q = q_ref[t * HALF:(t + 1) * HALF, :].astype(f32)
        qs_ref[0:HALF, :] = jnp.where(lane < 64, q, 0.0).astype(bf16)
        qs_ref[HALF:, :] = jnp.where(lane < 64, pltpu.roll(q, 64, 1), 0.0).astype(bf16)
        acc_ref[...] = jnp.zeros_like(acc_ref)

        def step(c, masked):
            k0 = pl.multiple_of(c * CH, CH)
            kv = kv_ref[pl.ds(k0, CH), :]
            s = lax.dot_general(qs_ref[...], kv, (((1,), (1,)), ((), ())), preferred_element_type=f32)
            p = jnp.exp2(s * C2)
            if masked:
                rows = r0 + lax.rem(lax.broadcasted_iota(jnp.int32, (2 * HALF, 1), 0), HALF)
                keys = k0 + lax.broadcasted_iota(jnp.int32, (2 * HALF, CH), 1)
                p = jnp.where((keys <= rows) & (keys >= starts_of(rows, len_ref)), p, 0.0)
            ones = jnp.where(lanek < 64, jnp.ones_like(kv), kv)
            acc_ref[...] += jnp.dot(p.astype(bf16), ones, preferred_element_type=f32)

        first, free, diag, last = key_ranges(r0, len_ref, CH)
        pl.loop(first, free)(lambda c: step(c, True))
        pl.loop(free, diag)(lambda c: step(c, False))
        pl.loop(diag, last)(lambda c: step(c, True))

        acc = acc_ref[...]
        swapped = pltpu.roll(acc, 64, 1)
        o = swapped / acc
        m = jnp.where(lane < 64, o[:HALF], pltpu.roll(o[HALF:], 64, 1))
        mix_ref[t * HALF:(t + 1) * HALF, :] = m.astype(bf16)
        out_ref[t * HALF:(t + 1) * HALF, :] = m
        total = jnp.where(lane2 < 64, acc, swapped)
        qa_ref[t, :, 0:128] = qs_ref[...]
        qa_ref[t, :, 128:256] = split3(jnp.log(total) * (-1.0 / SCALE), lane2).astype(bf16)


def bwd_kernel(parts, me_ref, len_ref, qa_ref, out_ref, do_ref, kv_ref, dq_ref, dkv_ref, da_ref, acc_ref, dqt_ref):
    me = me_ref[0]
    lane = lanes((HALF, 128))
    ones3 = jnp.where(lanes((CH, 128)) < 3, 1.0, 0.0).astype(bf16)
    acc_ref[...] = jnp.zeros_like(acc_ref)
    for t in range(2):
        r0 = tile_row(me, t, parts)
        rows_t = slice(t * HALF, (t + 1) * HALF)
        do = do_ref[rows_t, :].astype(f32)
        prod = do * out_ref[rows_t, :]
        d0 = -jnp.sum(jnp.where(lane < 64, prod, 0.0), axis=1, keepdims=True)
        d1 = -jnp.sum(jnp.where(lane < 64, 0.0, prod), axis=1, keepdims=True)
        da_ref[0:HALF, 0:128] = jnp.where(lane < 64, 0.0, pltpu.roll(do, 64, 1)).astype(bf16)
        da_ref[HALF:, 0:128] = jnp.where(lane < 64, 0.0, do).astype(bf16)
        da_ref[0:HALF, 128:256] = split3(jnp.broadcast_to(d0, (HALF, 128)), lane).astype(bf16)
        da_ref[HALF:, 128:256] = split3(jnp.broadcast_to(d1, (HALF, 128)), lane).astype(bf16)
        dqt_ref[...] = jnp.zeros_like(dqt_ref)

        def step(c, masked):
            k0 = pl.multiple_of(c * CH, CH)
            kv = kv_ref[pl.ds(k0, CH), :]
            kva = jnp.concatenate([kv, ones3], axis=1)
            qa = qa_ref[t]
            da = da_ref[...]
            s = lax.dot_general(kva, qa, (((1,), (1,)), ((), ())), preferred_element_type=f32)
            p = jnp.exp2(s * C2)
            if masked:
                rows = r0 + lax.rem(lax.broadcasted_iota(jnp.int32, (1, 2 * HALF), 1), HALF)
                keys = k0 + lax.broadcasted_iota(jnp.int32, (CH, 2 * HALF), 0)
                p = jnp.where((keys <= rows) & (keys >= starts_of(rows, len_ref)), p, 0.0)
            dp = lax.dot_general(kva, da, (((1,), (1,)), ((), ())), preferred_element_type=f32)
            ds = (p * dp).astype(bf16)
            acc_ref[pl.ds(k0, CH), :] += jnp.dot(
                p.astype(bf16), da[:, 0:128], preferred_element_type=f32
            ) + jnp.dot(ds, qa[:, 0:128], preferred_element_type=f32)
            kt = kv.T[0:64, :]
            dqt_ref[...] += jnp.dot(kt, ds, preferred_element_type=f32)

        first, free, diag, last = key_ranges(r0, len_ref, CH)
        pl.loop(first, free)(lambda c: step(c, True))
        pl.loop(free, diag)(lambda c: step(c, False))
        pl.loop(diag, last)(lambda c: step(c, True))
        dqt = dqt_ref[...]
        both = jnp.concatenate([dqt[:, :HALF], dqt[:, HALF:]], axis=0)
        dq_ref[rows_t, :] = (both.T * SCALE).astype(bf16)
    weight = jnp.where(lanes((512, 128)) < 64, SCALE, 1.0)

    @pl.loop(0, parts)
    def _(b):
        rows = pl.ds(pl.multiple_of(b * 512, 512), 512)
        dkv_ref[rows, :] = (acc_ref[rows, :] * weight).astype(bf16)


smem = pl.BlockSpec(memory_space=pltpu.SMEM)
vmem = pl.BlockSpec(memory_space=pltpu.VMEM)


def attend(parts, me, lengths, q, kv):
    rows = 2 * HALF
    sds = jax.ShapeDtypeStruct
    return pl.pallas_call(
        functools.partial(fwd_kernel, parts),
        out_shape=(sds((rows, 128), bf16), sds((rows, 128), f32), sds((2, rows, 256), bf16)),
        in_specs=[smem, smem, vmem, vmem],
        out_specs=(vmem, vmem, vmem),
        scratch_shapes=[pltpu.VMEM((rows, 128), bf16), pltpu.VMEM((rows, 128), f32)],
        compiler_params=pltpu.CompilerParams(vmem_limit_bytes=48 << 20),
        cost_estimate=pl.CostEstimate(flops=3 << 30, bytes_accessed=4 << 20, transcendentals=5 << 20),
        name="attend",
    )(me, lengths, q, kv)


def attend_back(parts, me, lengths, qa, out, do, kv):
    rows = 2 * HALF
    sds = jax.ShapeDtypeStruct
    return pl.pallas_call(
        functools.partial(bwd_kernel, parts),
        out_shape=(sds((rows, 128), bf16), sds(kv.shape, bf16)),
        in_specs=[smem, smem, vmem, vmem, vmem, vmem],
        out_specs=(vmem, vmem),
        scratch_shapes=[pltpu.VMEM((rows, 256), bf16), pltpu.VMEM(kv.shape, f32), pltpu.VMEM((64, rows), f32)],
        compiler_params=pltpu.CompilerParams(vmem_limit_bytes=48 << 20),
        cost_estimate=pl.CostEstimate(flops=10 << 30, bytes_accessed=8 << 20, transcendentals=5 << 20),
        name="attend_back",
    )(me, lengths, qa, out, do, kv)
MESH = pl.DeviceIdType.MESH
eps = 1e-05


def rcopy(src, dst, send, recv, device):
    return pltpu.make_async_remote_copy(
        src_ref=src, dst_ref=dst, send_sem=send, recv_sem=recv, device_id=device, device_id_type=MESH
    )


def meet(devices):
    barrier = pltpu.get_barrier_semaphore()
    for device in devices:
        pl.semaphore_signal(barrier, inc=1, device_id=device, device_id_type=MESH)
    pl.semaphore_wait(barrier, len(devices))


class Place:
    def __init__(self):
        self.sp = lax.axis_index("sp")
        self.wt = lax.axis_index("wt")
        self.x, self.y = lax.div(self.sp, 4), lax.rem(self.sp, 4)
        self.z, self.c = lax.div(self.wt, 2), lax.rem(self.wt, 2)
        self.mirror = (15 - self.sp, self.wt)
        self.sibling = (self.sp, self.z * 2 + 1 - self.c)

    def along_x(self, d):
        return (lax.rem(self.x + d, 4) * 4 + self.y, self.wt)

    def along_y(self, d):
        return (self.x * 4 + lax.rem(self.y + d, 4), self.wt)

    def along_z(self, d):
        return (self.sp, lax.rem(self.z + d, 4) * 2 + self.c)

    def along_z_other(self, d):
        return (self.sp, lax.rem(self.z + d, 4) * 2 + 1 - self.c)

    def first(self, h, d):
        return self.along_x(d) if h == 0 else self.along_y(d)

    def second(self, h, d):
        return self.along_y(d) if h == 0 else self.along_x(d)

    def fsp(self, h):
        return self.x if h == 0 else self.y

    def ssp(self, h):
        return self.y if h == 0 else self.x


def spot(h, first, second):
    return (first, second) if h == 0 else (second, first)


ORDER = (2, 1, 3)


def gather_kernel(q_ref, kv_ref, qz_ref, all_ref, ms, mr, fs, fr, ss, sr):
    p = Place()
    meet([p.along_x(d) for d in ORDER] + [p.along_y(d) for d in ORDER] + [p.mirror])
    all_ref[p.x, p.y] = kv_ref[...]
    mirror = rcopy(q_ref.at[1], qz_ref.at[1], ms, mr, p.mirror)
    first, second = {}, {}
    for d in ORDER:
        for h in range(2):
            first[h, d] = rcopy(
                kv_ref.at[h], all_ref.at[p.x, p.y, h], fs.at[h, d - 1], fr.at[h, d - 1], p.first(h, d)
            )
            first[h, d].start()
    mirror.start()

    def forward(h, slot):
        a = lax.rem(p.fsp(h) + 4 - slot, 4)
        at = spot(h, a, p.ssp(h))
        for e in ORDER:
            src = kv_ref.at[h] if slot == 0 else all_ref.at[at[0], at[1], h]
            second[h, slot, e] = rcopy(
                src, all_ref.at[at[0], at[1], h], ss.at[h, slot, e - 1], sr.at[h, slot, e - 1], p.second(h, e)
            )
            second[h, slot, e].start()

    for h in range(2):
        forward(h, 0)
    qz_ref[0] = q_ref[0]
    for d in (1, 3, 2):
        for h in range(2):
            first[h, d].wait_recv()
            forward(h, d)
    mirror.wait()
    for copy in first.values():
        copy.wait_send()
    for copy in second.values():
        copy.wait()


def scatter_kernel(dkv_ref, dqz_ref, own_ref, dq_ref, r1, send, r2, ms, mr, fs, fr, ss, sr):
    p = Place()
    meet([p.along_x(d) for d in ORDER] + [p.along_y(d) for d in ORDER] + [p.mirror])
    first, second = {}, {}
    for d in ORDER:
        for h in range(2):
            to = lax.rem(p.fsp(h) + d, 4)
            src = dkv_ref.at[to, :, 0] if h == 0 else dkv_ref.at[:, to, 1]
            first[h, d] = rcopy(src, r1.at[h, d - 1], fs.at[h, d - 1], fr.at[h, d - 1], p.first(h, d))
            first[h, d].start()
    mirror = rcopy(dqz_ref.at[1], dq_ref.at[1], ms, mr, p.mirror)
    mirror.start()
    dq_ref[0] = dqz_ref[0]

    def total(h, b):
        at = spot(h, p.fsp(h), b)
        value = dkv_ref[at[0], at[1], h].astype(f32)
        for d in range(3):
            value = value + r1[h, d, b].astype(f32)
        return value

    for h in range(2):
        for d in ORDER:
            first[h, d].wait_recv()
        for e in ORDER:
            b = lax.rem(p.ssp(h) + e, 4)
            send[h, e - 1] = total(h, b).astype(bf16)
            second[h, e] = rcopy(
                send.at[h, e - 1], r2.at[h, e - 1], ss.at[h, e - 1], sr.at[h, e - 1], p.second(h, e)
            )
            second[h, e].start()
    for h in range(2):
        value = total(h, p.ssp(h))
        for e in ORDER:
            second[h, e].wait_recv()
            value = value + r2[h, e - 1].astype(f32)
        own_ref[h] = value.astype(bf16)
    mirror.wait()
    for copy in list(first.values()) + list(second.values()):
        copy.wait_send()


class WtSum:
    def __init__(self, p, part, sib, send, rz, sems):
        self.p, self.part, self.sib, self.send, self.rz = p, part, sib, send, rz
        self.cs, self.cr, self.zs, self.zr = sems
        self.second = {}

    def core(self, zz):
        return rcopy(
            self.part.at[zz * 2 + 1 - self.p.c], self.sib.at[zz], self.cs.at[zz], self.cr.at[zz], self.p.sibling
        )

    def start_core(self, zz):
        self.core(zz).start()

    def pair(self, zz):
        return self.part[zz * 2 + self.p.c].astype(f32) + self.sib[zz].astype(f32)

    def send_z(self, d):
        zz = lax.rem(self.p.z + d, 4)
        self.core(zz).wait_recv()
        self.send[d - 1] = self.pair(zz).astype(bf16)
        copy = rcopy(
            self.send.at[d - 1], self.rz.at[d - 1], self.zs.at[d - 1], self.zr.at[d - 1], self.p.along_z(d)
        )
        copy.start()
        self.second[d] = copy

    def own(self):
        self.core(self.p.z).wait_recv()
        value = self.pair(self.p.z)
        for d in (1, 3, 2):
            self.second[d].wait_recv()
            value = value + self.rz[d - 1].astype(f32)
        return value

    def finish(self):
        for zz in range(4):
            self.core(zz).wait_send()
        for copy in self.second.values():
            copy.wait_send()


class WtGather:
    def __init__(self, p, out, sems):
        self.p, self.out = p, out
        self.zs, self.zr, self.gs, self.gr = sems
        self.far, self.near = {}, {}

    def start(self):
        p = self.p
        for d in ORDER:
            self.far[d] = rcopy(
                self.out.at[p.wt], self.out.at[p.wt], self.zs.at[d - 1], self.zr.at[d - 1], p.along_z(d)
            )
            self.far[d].start()
        self.pass_on(0)

    def pass_on(self, slot):
        p = self.p
        row = lax.rem(p.z + 4 - slot, 4) * 2 + p.c
        self.near[slot] = rcopy(
            self.out.at[row], self.out.at[row], self.gs.at[slot], self.gr.at[slot], p.sibling
        )
        self.near[slot].start()

    def forward(self):
        for d in (1, 3, 2):
            self.far[d].wait_recv()
            self.pass_on(d)

    def arrived(self):
        for slot in (0, 1, 3, 2):
            self.near[slot].wait_recv()

    def finish(self):
        for copy in list(self.far.values()) + list(self.near.values()):
            copy.wait_send()


def rms_of(value):
    return lax.rsqrt(jnp.mean(value * value, axis=-1, keepdims=True) + eps)


def norm_back(values, scale, gain, grad):
    scaled = grad * gain
    inner = jnp.mean(scaled * values, axis=-1, keepdims=True)
    return scale * scaled - values * scale * scale * scale * inner


def wt_peers(p):
    return [p.sibling] + [p.along_z(d) for d in ORDER]


def middle_kernel(mix_ref, w_ref, tok_ref, gain_ref, nm_ref, mid_ref, mixo_ref, part, sib, send, rz, ms, mr, cs, cr, zs, zr, az, bz, ag, bg):
    p = Place()
    meet(wt_peers(p) + [p.mirror])
    mirror = rcopy(mix_ref.at[1], mixo_ref.at[1], ms, mr, p.mirror)
    mirror.start()
    mixo_ref[0] = mix_ref[0]
    total = WtSum(p, part, sib, send, rz, (cs, cr, zs, zr))
    for half in range(2):
        if half == 1:
            mirror.wait()
        both = jnp.dot(mixo_ref[half], w_ref[...], preferred_element_type=f32).astype(bf16)
        part[half * 4:half * 4 + 4] = both.reshape(4, 64, 1024)
        for zz in (half * 2, half * 2 + 1):
            total.start_core(zz)
    for d in ORDER:
        total.send_z(d)
    middle = tok_ref[p.wt].astype(f32) + total.own()
    mid_ref[...] = middle
    nm_ref[p.wt] = (middle * rms_of(middle) * gain_ref[...]).astype(bf16)
    spread = WtGather(p, nm_ref, (az, bz, ag, bg))
    spread.start()
    spread.forward()
    spread.arrived()
    spread.finish()
    total.finish()


def turn_kernel(dm_ref, mlp_ref, mid_ref, cot_ref, gain_ref, w_ref, out_ref, da_ref, dmid_ref, gn_ref, dz_ref, up, sib, send, rz, ms, mr, cs, cr, zs, zr, az, bz, ag, bg):
    p = Place()
    meet(wt_peers(p) + [p.mirror])
    totals = [
        WtSum(p, ref, sib.at[i], send.at[i], rz.at[i], (cs.at[i], cr.at[i], zs.at[i], zr.at[i]))
        for i, ref in enumerate((dm_ref, mlp_ref))
    ]
    for total in totals:
        for zz in range(4):
            total.start_core(zz)
    for total in totals:
        for d in ORDER:
            total.send_z(d)
    middle = mid_ref[...]
    scale = rms_of(middle)
    d_mid = totals[0].own()
    gn_ref[...] = jnp.sum(d_mid * middle * scale, axis=0, keepdims=True)
    d_middle = cot_ref[p.wt].astype(f32) + norm_back(middle, scale, gain_ref[...], d_mid)
    dmid_ref[...] = d_middle
    da_ref[p.wt] = d_middle.astype(bf16)
    spreads = [
        WtGather(p, ref, (az.at[i], bz.at[i], ag.at[i], bg.at[i])) for i, ref in enumerate((da_ref, out_ref))
    ]
    spreads[0].start()
    out_ref[p.wt] = (middle + totals[1].own()).astype(bf16)
    spreads[1].start()
    spreads[0].forward()
    spreads[0].arrived()
    mirror = rcopy(up, dz_ref.at[1], ms, mr, p.mirror)
    for half in (1, 0):
        rows = da_ref[half * 4:half * 4 + 4].reshape(256, 1024)
        d_mixed = lax.dot_general(rows, w_ref[...], (((1,), (1,)), ((), ())), preferred_element_type=f32).astype(bf16)
        if half == 1:
            up[...] = d_mixed
            mirror.start()
        else:
            dz_ref[0] = d_mixed
    spreads[1].forward()
    spreads[1].arrived()
    mirror.wait()
    for part in spreads + totals:
        part.finish()


def last_kernel(dn_ref, g_ref, tok_ref, dmid_ref, gain_ref, gn_ref, gg_ref, gt_ref, gq_ref, gkv_ref, vec_ref,
                sib, send, rz, cs, cr, zs, zr, az, bz, ag, bg,
                r1, s2, r2, gb, f1s, f1r, f2s, f2r, f3s, f3r, f4s, f4r,
                vw, vx, vy, vr, vs1, vr1, vs2, vr2, vs3, vr3):
    p = Place()
    meet(wt_peers(p) + [p.along_z_other(d) for d in ORDER] + [p.along_x(d) for d in ORDER] + [p.along_y(d) for d in ORDER])
    total = WtSum(p, dn_ref, sib, send, rz, (cs, cr, zs, zr))
    for zz in range(4):
        total.start_core(zz)
    first, second, third, fourth = {}, {}, {}, {}
    for d in ORDER:
        for h in range(2):
            to = lax.rem(p.fsp(h) + d, 4)
            src = g_ref.at[h, to] if h == 0 else g_ref.at[h, :, to]
            first[h, d] = rcopy(src, r1.at[h, d - 1], f1s.at[h, d - 1], f1r.at[h, d - 1], p.first(h, d))
            first[h, d].start()
    for d in ORDER:
        total.send_z(d)

    def part_of(h, b):
        at = spot(h, p.fsp(h), b)
        value = g_ref[h, at[0], at[1]].astype(f32)
        for d in range(3):
            value = value + r1[h, d, b].astype(f32)
        return value

    for h in range(2):
        for d in ORDER:
            first[h, d].wait_recv()
        for e in ORDER:
            s2[h, e - 1] = part_of(h, lax.rem(p.ssp(h) + e, 4)).astype(bf16)
            second[h, e] = rcopy(s2.at[h, e - 1], r2.at[h, e - 1], f2s.at[h, e - 1], f2r.at[h, e - 1], p.second(h, e))
            second[h, e].start()

    base = tok_ref[p.wt].astype(f32)
    scale = rms_of(base)
    d_normed = total.own()
    gt_ref[p.wt] = (dmid_ref[...] + norm_back(base, scale, gain_ref[...], d_normed)).astype(bf16)
    spread = WtGather(p, gt_ref, (az, bz, ag, bg))
    spread.start()
    vw[0, 0:1] = jnp.sum(d_normed * base * scale, axis=0, keepdims=True)
    vw[0, 1:2] = gn_ref[...]
    vw[0, 2:3] = gg_ref[...]
    vw[0, 3:8] = jnp.zeros((5, 1024), f32)

    def vec_round(buf, devices, sends, recvs):
        copies = []
        for i, device in enumerate(devices):
            copies.append(rcopy(buf.at[0], buf.at[i + 1], sends.at[i], recvs.at[i], device))
            copies[-1].start()
        return copies

    def vec_total(buf, copies):
        value = buf[0]
        for i, copy in enumerate(copies):
            copy.wait_recv()
            value = value + buf[i + 1]
        return value

    round1 = vec_round(vw, [p.along_z(d) for d in ORDER] + [p.along_z_other(d) for d in ORDER] + [p.sibling], vs1, vr1)

    for h in range(2):
        value = part_of(h, p.ssp(h))
        for e in ORDER:
            second[h, e].wait_recv()
            value = value + r2[h, e - 1].astype(f32)
        gb[h, p.x, p.y] = value.astype(bf16)
        for e in ORDER:
            third[h, e] = rcopy(gb.at[h, p.x, p.y], gb.at[h, p.x, p.y], f3s.at[h, e - 1], f3r.at[h, e - 1], p.second(h, e))
            third[h, e].start()

    vx[0] = vec_total(vw, round1)
    round2 = vec_round(vx, [p.along_x(d) for d in ORDER], vs2, vr2)
    for h in range(2):
        for e in ORDER:
            third[h, e].wait_recv()
        mine = gb.at[h, p.x] if h == 0 else gb.at[h, :, p.y]
        for d in ORDER:
            fourth[h, d] = rcopy(mine, mine, f4s.at[h, d - 1], f4r.at[h, d - 1], p.first(h, d))
            fourth[h, d].start()
    spread.forward()
    vy[0] = vec_total(vx, round2)
    round3 = vec_round(vy, [p.along_y(d) for d in ORDER], vs3, vr3)
    for copy in fourth.values():
        copy.wait_recv()
    gq_ref[...] = gb[0].astype(f32)
    gkv_ref[...] = gb[1].astype(f32)
    vec_ref[...] = vec_total(vy, round3)
    spread.arrived()
    spread.finish()
    total.finish()
    for group in (first, second, third, fourth):
        for copy in group.values():
            copy.wait_send()
    for copy in round1 + round2 + round3:
        copy.wait_send()


DMA = pltpu.SemaphoreType.DMA
sds = jax.ShapeDtypeStruct


def comm_call(kernel, number, out_shape, args, scratch, name):
    return pl.pallas_call(
        kernel,
        out_shape=out_shape,
        in_specs=[vmem] * len(args),
        out_specs=tuple(vmem for _ in out_shape),
        scratch_shapes=scratch,
        compiler_params=pltpu.CompilerParams(
            collective_id=number, has_side_effects=True, vmem_limit_bytes=24 << 20
        ),
        cost_estimate=pl.CostEstimate(flops=8 << 30, bytes_accessed=32 << 20, transcendentals=0),
        name=name,
    )(*args)


def gather_keys(q, kv):
    return comm_call(
        gather_kernel, 1,
        (sds((2, 256, 128), bf16), sds((4, 4, 2, 256, 128), bf16)),
        (q.reshape(2, 256, 128), kv.reshape(2, 256, 128)),
        [DMA, DMA, DMA((2, 3)), DMA((2, 3)), DMA((2, 4, 3)), DMA((2, 4, 3))],
        "gather_keys",
    )


def scatter_keys(dkv, dq):
    return comm_call(
        scatter_kernel, 2,
        (sds((2, 256, 128), bf16), sds((2, 256, 128), bf16)),
        (dkv.reshape(4, 4, 2, 256, 128), dq.reshape(2, 256, 128)),
        [pltpu.VMEM((2, 3, 4, 256, 128), bf16), pltpu.VMEM((2, 3, 256, 128), bf16), pltpu.VMEM((2, 3, 256, 128), bf16),
         DMA, DMA, DMA((2, 3)), DMA((2, 3)), DMA((2, 3)), DMA((2, 3))],
        "scatter_keys",
    )


def make_middle(mix, w_out, tokens, gain):
    rows = pltpu.VMEM
    return comm_call(
        middle_kernel, 3,
        (sds((8, 64, 1024), bf16), sds((64, 1024), f32), sds((2, 256, 128), bf16)),
        (mix.reshape(2, 256, 128), w_out, tokens.reshape(8, 64, 1024), gain.reshape(1, 1024)),
        [rows((8, 64, 1024), bf16), rows((4, 64, 1024), bf16), rows((3, 64, 1024), bf16), rows((3, 64, 1024), bf16),
         DMA, DMA, DMA((4,)), DMA((4,)), DMA((3,)), DMA((3,)), DMA((3,)), DMA((3,)), DMA((4,)), DMA((4,))],
        "make_middle",
    )


def turn_back(dm, mlp, mid, cot, gain, w_out):
    rows = pltpu.VMEM
    return comm_call(
        turn_kernel, 4,
        (sds((8, 64, 1024), bf16), sds((8, 64, 1024), bf16), sds((64, 1024), f32), sds((1, 1024), f32), sds((2, 256, 128), bf16)),
        (dm.reshape(8, 64, 1024), mlp.reshape(8, 64, 1024), mid, cot.reshape(8, 64, 1024), gain.reshape(1, 1024), w_out),
        [rows((256, 128), bf16), rows((2, 4, 64, 1024), bf16), rows((2, 3, 64, 1024), bf16), rows((2, 3, 64, 1024), bf16),
         DMA, DMA, DMA((2, 4)), DMA((2, 4)), DMA((2, 3)), DMA((2, 3)), DMA((2, 3)), DMA((2, 3)), DMA((2, 4)), DMA((2, 4))],
        "turn_back",
    )


def last_sums(dn, g, tokens, dmid, gain, gn, gg):
    rows = pltpu.VMEM
    return comm_call(
        last_kernel, 5,
        (sds((8, 64, 1024), bf16), sds((4, 4, 64, 128), f32), sds((4, 4, 64, 128), f32), sds((8, 1024), f32)),
        (dn.reshape(8, 64, 1024), g.reshape(2, 4, 4, 64, 128), tokens.reshape(8, 64, 1024), dmid, gain.reshape(1, 1024), gn, gg),
        [rows((4, 64, 1024), bf16), rows((3, 64, 1024), bf16), rows((3, 64, 1024), bf16),
         DMA((4,)), DMA((4,)), DMA((3,)), DMA((3,)), DMA((3,)), DMA((3,)), DMA((4,)), DMA((4,)),
         rows((2, 3, 4, 64, 128), bf16), rows((2, 3, 64, 128), bf16), rows((2, 3, 64, 128), bf16), rows((2, 4, 4, 64, 128), bf16),
         DMA((2, 3)), DMA((2, 3)), DMA((2, 3)), DMA((2, 3)), DMA((2, 3)), DMA((2, 3)), DMA((2, 3)), DMA((2, 3)),
         rows((8, 8, 1024), f32), rows((4, 8, 1024), f32), rows((4, 8, 1024), f32), rows((8, 1024), f32),
         DMA((7,)), DMA((7,)), DMA((3,)), DMA((3,)), DMA((3,)), DMA((3,))],
        "last_sums",
    )
def turned(value, lane):
    return jnp.where(lax.rem(lane, 64) < 32, pltpu.roll(value, 96, 1), pltpu.roll(value, 32, 1))


def head_sums(value, lane):
    s0 = jnp.sum(jnp.where(lane < 64, value, 0.0), axis=1, keepdims=True)
    s1 = jnp.sum(jnp.where(lane < 64, 0.0, value), axis=1, keepdims=True)
    return jnp.where(lane < 64, s0, s1)


def twice(gain):
    return jnp.concatenate([gain, gain], axis=1)


def proj_kernel(tok_ref, gain_ref, wq_ref, wk_ref, wv_ref, qg_ref, kg_ref, cos_ref, sin_ref, n_ref, qp_ref, kvp_ref, q_ref, kv_ref):
    lane = lanes((512, 128))
    base = tok_ref[...].astype(f32)
    normed = (base * rms_of(base) * gain_ref[...]).astype(bf16)
    n_ref[...] = normed
    wkv = jnp.concatenate([wk_ref[...], wv_ref[...]], axis=1)
    cosine, sine = cos_ref[...], sin_ref[...]
    q = jnp.dot(normed, wq_ref[...], preferred_element_type=f32)
    qp_ref[...] = q
    q = q * lax.rsqrt(head_sums(q * q, lane) * (1.0 / 64) + eps) * twice(qg_ref[...])
    q_ref[...] = (q * cosine + turned(q, lane) * sine).astype(bf16)
    kv = jnp.dot(normed, wkv, preferred_element_type=f32)
    kvp_ref[...] = kv
    k = kv * lax.rsqrt(head_sums(kv * kv, lane) * (1.0 / 64) + eps) * twice(kg_ref[...])
    k = k * cosine + turned(k, lane) * sine
    kv_ref[...] = jnp.where(lane < 64, k, kv).astype(bf16)


def proj_back_kernel(dq_ref, dkv_ref, qp_ref, kvp_ref, n_ref, wq_ref, wk_ref, wv_ref, qg_ref, kg_ref, cos_ref, sin_ref, dn_ref, g_ref, gg_ref):
    lane = lanes((512, 128))
    cosine, sine = cos_ref[...], sin_ref[...]

    def back(grad, proj, gain):
        grad = grad * cosine - turned(grad, lane) * sine
        scale = lax.rsqrt(head_sums(proj * proj, lane) * (1.0 / 64) + eps)
        scaled = grad * gain
        inner = head_sums(scaled * proj, lane) * (1.0 / 64)
        gains = jnp.sum(grad * proj * scale, axis=0, keepdims=True)
        return scale * scaled - proj * scale * scale * scale * inner, gains

    dq, gq = back(dq_ref[...].astype(f32), qp_ref[...], twice(qg_ref[...]))
    dkv_in = dkv_ref[...].astype(f32)
    dk, gk = back(dkv_in, kvp_ref[...], twice(kg_ref[...]))
    dq = dq.astype(bf16)
    dkv = jnp.where(lane < 64, dk, dkv_in).astype(bf16)
    wkv = jnp.concatenate([wk_ref[...], wv_ref[...]], axis=1)
    dn = lax.dot_general(dq, wq_ref[...], (((1,), (1,)), ((), ())), preferred_element_type=f32)
    dn = dn + lax.dot_general(dkv, wkv, (((1,), (1,)), ((), ())), preferred_element_type=f32)
    dn_ref[...] = dn.astype(bf16)
    normed = n_ref[...]
    g_ref[0] = lax.dot_general(normed, dq, (((0,), (0,)), ((), ())), preferred_element_type=f32).astype(bf16)
    g_ref[1] = lax.dot_general(normed, dkv, (((0,), (0,)), ((), ())), preferred_element_type=f32).astype(bf16)
    gg_ref[...] = jnp.concatenate([gq, gk, jnp.zeros((1, 768), f32)], axis=1)


def local_call(kernel, out_shape, args, name):
    return pl.pallas_call(
        kernel,
        out_shape=out_shape,
        in_specs=[vmem] * len(args),
        out_specs=tuple(vmem for _ in out_shape),
        compiler_params=pltpu.CompilerParams(vmem_limit_bytes=32 << 20),
        cost_estimate=pl.CostEstimate(flops=3 << 30, bytes_accessed=16 << 20, transcendentals=0),
        name=name,
    )(*args)


theta = 1000000.0


def body(tokens, norm_in, w_query, w_key, w_value, query_gain, key_gain, w_out, norm_mid, w_gate, w_up, w_down, cotangent, lengths):
    parts = lax.axis_size("sp")
    sp = lax.axis_index("sp")
    me = sp.reshape(1).astype(jnp.int32)
    ids = sp * 512 + jnp.arange(512)
    positions = ids - starts_of(ids, lengths)
    index = jnp.arange(128)
    freqs = theta ** (-((index % 32).astype(f32) * 2.0) / 64)
    angles = positions.astype(f32)[:, None] * freqs[None, :]
    cosine = jnp.cos(angles)
    sine = jnp.sin(angles) * jnp.where(index % 64 < 32, -1.0, 1.0)[None, :]
    qg, kg = query_gain.reshape(1, 64), key_gain.reshape(1, 64)
    gain_in = norm_in.reshape(1, 1024)

    normed, q_proj, kv_proj, q, kv = local_call(
        proj_kernel,
        (sds((512, 1024), bf16), sds((512, 128), f32), sds((512, 128), f32), sds((512, 128), bf16), sds((512, 128), bf16)),
        (tokens, gain_in, w_query, w_key, w_value, qg, kg, cosine, sine),
        "project",
    )
    qz, kv_all = gather_keys(q, kv)
    kv_all = kv_all.reshape(8192, 128)
    mix_z, mix_f, qa = attend(parts, me, lengths, qz.reshape(512, 128), kv_all)
    normed_mid, mid_own, mixed = make_middle(mix_z, w_out, tokens, norm_mid)
    normed_mid = normed_mid.reshape(512, 1024)
    mixed = mixed.reshape(512, 128)

    gate = jnp.dot(normed_mid, w_gate, preferred_element_type=f32)
    up_proj = jnp.dot(normed_mid, w_up, preferred_element_type=f32)
    sigmoid_gate = jax.nn.sigmoid(gate)
    act = (gate * sigmoid_gate * up_proj).astype(bf16)
    mlp_part = jnp.dot(act, w_down, preferred_element_type=f32).astype(bf16)
    d_act = jnp.einsum("td,fd->tf", cotangent, w_down, preferred_element_type=f32)
    d_gate = (d_act * up_proj * sigmoid_gate * (1.0 + gate * (1.0 - sigmoid_gate))).astype(bf16)
    d_up = (d_act * gate * sigmoid_gate).astype(bf16)
    d_mid_part = (
        jnp.einsum("tf,df->td", d_gate, w_gate, preferred_element_type=f32)
        + jnp.einsum("tf,df->td", d_up, w_up, preferred_element_type=f32)
    ).astype(bf16)
    g_down = jnp.einsum("tf,td->fd", act, cotangent, preferred_element_type=f32)
    g_gate = jnp.einsum("td,tf->df", normed_mid, d_gate, preferred_element_type=f32)
    g_up = jnp.einsum("td,tf->df", normed_mid, d_up, preferred_element_type=f32)

    output, d_attn, d_middle_own, gn, d_mix_z = turn_back(d_mid_part, mlp_part, mid_own, cotangent, norm_mid, w_out)
    g_out = jnp.einsum("tq,td->qd", mixed, d_attn.reshape(512, 1024), preferred_element_type=f32)
    g_gate, g_up, g_down, g_out = (
        lax.psum(g.astype(bf16), "sp").astype(f32) for g in (g_gate, g_up, g_down, g_out)
    )
    dq_z, dkv_all = attend_back(parts, me, lengths, qa, mix_f, d_mix_z.reshape(512, 128), kv_all)
    dkv, dq = scatter_keys(dkv_all, dq_z)
    dn_part, g_qkv, gg = local_call(
        proj_back_kernel,
        (sds((512, 1024), bf16), sds((2, 1024, 128), bf16), sds((1, 1024), f32)),
        (dq.reshape(512, 128), dkv.reshape(512, 128), q_proj, kv_proj, normed, w_query, w_key, w_value, qg, kg, cosine, sine),
        "project_back",
    )
    grad_tokens, g_query, g_kv, vec = last_sums(dn_part, g_qkv, tokens, d_middle_own, norm_in, gn, gg)
    g_query = g_query.reshape(1024, 128)
    g_kv = g_kv.reshape(1024, 128)
    return (
        output.reshape(512, 1024),
        grad_tokens.reshape(512, 1024),
        vec[0],
        g_query,
        g_kv[:, :64],
        g_kv[:, 64:],
        vec[2, :64] + vec[2, 64:128],
        vec[2, 128:192],
        g_out,
        vec[1],
        g_gate,
        g_up,
        g_down,
    )


def solution(mesh):
    placed = (
        P("sp", None), P(), P(None, "wt"), P(None, "wt"), P(None, "wt"), P(), P(), P("wt", None), P(),
        P(None, "wt"), P(None, "wt"), P("wt", None), P("sp", None), P(),
    )
    return jax.shard_map(
        body,
        mesh=mesh,
        in_specs=placed,
        out_specs=(
            P("sp", None), P("sp", None), P(), P(None, "wt"), P(None, "wt"), P(None, "wt"), P(), P(),
            P("wt", None), P(), P(None, "wt"), P(None, "wt"), P("wt", None),
        ),
        check_vma=False,
    )
```

time: 999 us -> 257 us (0.26)
  waiting for transfers between devices: 386 us -> 25.7 us
  matrix products: 254 us -> 12.5 us
  Pallas kernels: 0 us -> 168 us
  local copies, waits for them, and re-layouts: 156 us -> 19.6 us
  other arithmetic: 75.9 us -> 13.6 us
  blocking collectives: 48.9 us -> 0 us
  loops' own time: 33 us -> 0 us
  starting transfers between devices: 22.7 us -> 0.04 us
    dot_general x125 -> x2, matrix products: 239 us -> 2.03 us  [the longest x1 1.03 us: body(): jnp.einsum('tq,td->qd', mixed, d_attn.reshape(512, 1024), preferred_eleme...]
    psum x4 -> x1, waiting for transfers between devices: 238 us -> 25.7 us  [body(): lax.psum(g.astype(bf16), 'sp').astype(f32)]
    pallas_call x0 -> x9, Pallas kernels: none -> 168 us  [the longest x5 135 us: comm_call(): pl.pallas_call(kernel, out_shape=out_shape, in_specs=[vmem] * len(args),...]
    reduce_scatter x2 -> x0, waiting for transfers between devices: 111 us -> none  [the longest x1 70.9 us: body(): lax.psum_scatter(d_value_blocks.reshape(total, kv_width).astype(jnp.bfloa...]
    dynamic_slice x144 -> x0, local copies, waits for them, and re-layouts: 100 us -> none  [the longest x48 49.2 us: body(): lax.scan(lse_step, (start_max, start_sum), indices)]
    psum x2 -> x0, blocking collectives: 48.9 us -> none  [the longest x1 34.7 us: body(): lax.psum(g_norm_in.astype(jnp.bfloat16), 'sp').astype(jnp.float32)]
    another operation x3 -> x0, loops' own time: 33 us -> none  [the longest x1 11.2 us: body(): lax.scan(grad_step, jnp.zeros((rows, kv_local, group, head_dim), f32), in...]
    all_to_all x4 -> x0, starting transfers between devices: 22 us -> none  [the longest x1 7.58 us: body(): lax.all_to_all(to_units(queries), 'sp', split_axis=0, concat_axis=0, tile...]
  transfers between devices with their start and end apart: 12 -> 1, of which waited for: 11 -> 1; matrix products, arithmetic and copies ran while one was open for 17% -> 2% of each run, Pallas kernels for 0% -> 28%
where the time goes in v1:
time: 257 us; the launch traced here: 256 us
  Pallas kernels  168 us (65%)
  waiting for transfers between devices  25.7 us (10%)
  local copies, waits for them, and re-layouts  19.6 us (8%)
  between operations  17.2 us (7%)
  other arithmetic  13.6 us (5%)
  matrix products  12.5 us (5%)
    pallas_call x5, Pallas kernels, comm_call(): pl.pallas_call(kernel, out_shape=out_shape, in_specs=[vmem] * len(args),...  135 us
    psum x1, waiting for transfers between devices, body(): lax.psum(g.astype(bf16), 'sp').astype(f32)  25.7 us
    unnamed x77, local copies, waits for them, and re-layouts  16.4 us
    pallas_call x1, Pallas kernels, attend_back(): pl.pallas_call(functools.partial(bwd_kernel, parts), out_shape=(sds((rows...  16.3 us
    pallas_call x1, Pallas kernels, attend(): pl.pallas_call(functools.partial(fwd_kernel, parts), out_shape=(sds((rows...  11 us
    convert_element_type x4, other arithmetic, body(): lax.psum(g.astype(bf16), 'sp').astype(f32)  8.22 us
  transfers between devices with their start and end apart: 1, of which 1 were waited for; matrix products, arithmetic and copies ran while one was open for 2% of the time, Pallas kernels for 28%

profile of v1, /device:TPU:1, one launch (start us, length us, event | category | flops | bytes accessed | tf_op | source)
XLA Modules:
  0.0 256.3 jit_solution(4092124603938248260)
XLA Ops:
  7.2 0.0 copy-start
  7.2 0.0 copy-start.5
  7.2 0.0 all-reduce.3.cloned.1.call-start
  7.3 0.5 compare_select_fusion
  7.8 1.1 copy.27.wk_ref
  8.9 1.1 copy.28.wv_ref
  10.0 1.4 fusion.12
  14.0 2.6 %subtract_convert_fusion = f32[512]{0:T(512)S(1)} fusion(s32[]{:T(128)} %bitcast.7, s32[]{:T(128)S(6)} %add.87, s32[]{:T(128)} %bitcast.6, s32[]{:T(128)S(6)} %add.85, s32[]{:T(128)} %bitcast.5, s32[]{:T(128)S(6)} %add.83, s32[]{:T(128)} %bitcast.4, s32[]{:T(128)S(6)} %mul.58), kind=kLoop, calls=%fused_computation.13 | loop fusion | flops 7168 | bytes 2080 | tf_op jit(solution)/shard_map/convert_element_type | solution.py:746
  16.6 1.7 fusion
  18.3 2.0 project.1
  20.3 0.0 copy-start.17
  20.4 0.0 copy-start.21
  20.4 0.0 copy-start.23
  20.4 0.0 copy-start.3
  20.4 23.3 %gather_keys.1 = (bf16[2,256,128]{2,1,0:T(8,128)(2,1)S(1)}, bf16[4,4,2,256,128]{4,3,2,1,0:T(8,128)(2,1)S(1)}) custom-call(bf16[2,256,128]{2,1,0:T(8,128)(2,1)S(1)} %bitcast.90, bf16[2,256,128]{2,1,0:T(8,128)(2,1)S(1)} %bitcast.91), custom_call_target="tpu_custom_call" | custom-call | flops 8589934592 | bytes 33554432 | tf_op jit(solution)/shard_map/gather_keys/pallas_call | solution.py:591
  43.7 0.0 copy-start.13
  43.7 0.0 copy-start.7
  43.7 0.0 copy-start.9
  43.7 11.0 %attend.1 = (bf16[512,128]{1,0:T(8,128)(2,1)S(1)}, f32[512,128]{1,0:T(8,128)S(1)}, bf16[2,512,256]{2,1,0:T(8,128)(2,1)S(1)}) custom-call(s32[1]{0:T(128)} %bitcast.me_ref, s32[4]{0:T(128)S(1)} %copy-done.3, bf16[512,128]{1,0:T(8,128)(2,1)S(1)} %bitcast.92, bf16[8192,128]{1,0:T(8,128)(2,1)S(1)} %bitcast.75), custom_call_target="tpu_custom_call" | custom-call | flops 3221225472 | bytes 4194304 | tf_op jit(solution)/shard_map/attend/pallas_call | solution.py:161
  54.7 0.0 copy-start.25
  54.8 0.0 copy-start.33
  54.8 27.3 %make_middle.1 = (bf16[8,64,1024]{2,1,0:T(8,128)(2,1)S(1)}, f32[64,1024]{1,0:T(8,128)S(1)}, bf16[2,256,128]{2,1,0:T(8,128)(2,1)S(1)}) custom-call(bf16[2,256,128]{2,1,0:T(8,128)(2,1)S(1)} %bitcast.93, bf16[128,1024]{1,0:T(8,128)(2,1)S(1)} %copy-done.7, bf16[8,64,1024]{2,1,0:T(8,128)(2,1)S(1)} %bitcast.65, f32[1,1024]{1,0:T(1,128)S(1)} %bitcast.67), custom_call_target="tpu_custom_call" | custom-call | flops 8589934592 | bytes 33554432 | tf_op jit(solution)/shard_map/make_middle/pallas_call | solution.py:591
  82.1 0.9 fusion.14
  83.0 0.3 copy-done.4
  83.3 0.4 copy-done.34
  83.7 0.8 fusion.13
  84.5 1.3 multiply_convert_fusion
  85.8 1.0 fusion.15
  86.8 1.8 convolution_convert_fusion.1
  88.6 1.0 convolution_convert_fusion.3
  89.6 1.9 convolution_convert_fusion.2
  91.5 1.8 convolution_convert_fusion
  93.3 1.0 add_convert_fusion
  94.3 31.6 %turn_back.1 = (bf16[8,64,1024]{2,1,0:T(8,128)(2,1)S(1)}, bf16[8,64,1024]{2,1,0:T(8,128)(2,1)S(1)}, f32[64,1024]{1,0:T(8,128)S(1)}, f32[1,1024]{1,0:T(1,128)S(1)}, bf16[2,256,128]{2,1,0:T(8,128)(2,1)S(1)}) custom-call(bf16[8,64,1024]{2,1,0:T(8,128)(2,1)S(1)} %bitcast.84, bf16[8,64,1024]{2,1,0:T(8,128)(2,1)S(1)} %bitcast.83, ...), custom_call_target="tpu_custom_call" | custom-call | flops 8589934592 | bytes 33554432 | tf_op jit(solution)/shard_map/turn_back/pallas_call | solution.py:591
  126.0 0.6 copy-done.15
  126.6 0.7 copy-done.27
  127.3 0.6 copy-done.29
  127.9 1.0 convolution_convert_fusion.4
  128.9 0.0 all-reduce.3.cloned.1.call-update
  129.0 1.6 copy-done.14
  130.6 0.9 copy-done.16
  131.5 1.0 copy-done.20
  132.5 0.9 copy-done.26
  133.5 16.3 %attend_back.1 = (bf16[512,128]{1,0:T(8,128)(2,1)S(1)}, bf16[8192,128]{1,0:T(8,128)(2,1)S(1)}) custom-call(s32[1]{0:T(128)} %bitcast.me_ref, s32[4]{0:T(128)S(1)} %copy-done.3, bf16[2,512,256]{2,1,0:T(8,128)(2,1)S(1)} %copy-done.20, f32[512,128]{1,0:T(8,128)S(1)} %copy-done.26, bf16[512,128]{1,0:T(8,128)(2,1)S(1)} %bitcast.86, bf16[8192,128]{1,0:T(8,128)(2,1)S(1)} %bitcast.76), custom_call_target="tpu_custom_call" | custom-call | flops 10737418240 | bytes 8388608 | tf_op jit(solution)/shard_map/attend_back/pallas_call | solution.py:176
  149.8 0.0 copy-start.22
  149.8 0.0 copy-start.24
  149.8 20.5 %scatter_keys.1 = (bf16[2,256,128]{2,1,0:T(8,128)(2,1)S(1)}, bf16[2,256,128]{2,1,0:T(8,128)(2,1)S(1)}) custom-call(bf16[4,4,2,256,128]{4,3,2,1,0:T(8,128)(2,1)S(1)} %bitcast.77, bf16[2,256,128]{2,1,0:T(8,128)(2,1)S(1)} %bitcast.89), custom_call_target="tpu_custom_call" | custom-call | flops 8589934592 | bytes 33554432 | tf_op jit(solution)/shard_map/scatter_keys/pallas_call | solution.py:591
  170.4 0.0 copy-start.30
  170.4 3.0 %project_back.1 = (bf16[512,1024]{1,0:T(8,128)(2,1)S(1)}, bf16[2,1024,128]{2,1,0:T(8,128)(2,1)S(1)}, f32[1,1024]{1,0:T(1,128)S(1)}) custom-call(bf16[512,128]{1,0:T(8,128)(2,1)S(1)} %bitcast.88, bf16[512,128]{1,0:T(8,128)(2,1)S(1)} %bitcast.87, f32[512,128]{1,0:T(8,128)S(1)} %copy-done.22, f32[512,128]{1,0:T(8,128)S(1)} %copy-done.24, ...), custom_call_target="tpu_custom_call" | custom-call | flops 3221225472 | bytes 16777216 | tf_op jit(solution)/shard_map/project_back/pallas_call | solution.py:724
  173.4 32.7 %last_sums.1 = (bf16[8,64,1024]{2,1,0:T(8,128)(2,1)S(1)}, f32[4,4,64,128]{3,2,1,0:T(8,128)S(1)}, f32[4,4,64,128]{3,2,1,0:T(8,128)S(1)}, f32[8,1024]{1,0:T(8,128)S(1)}) custom-call(bf16[8,64,1024]{2,1,0:T(8,128)(2,1)S(1)} %bitcast.82, bf16[2,4,4,64,128]{4,3,2,1,0:T(8,128)(2,1)S(1)} %bitcast.85, bf16[8,64,1024]{2,1,0:T(8,128)(2,1)S(1)} %bitcast.66, ...), custom_call_target="tpu_custom_call" | custom-call | flops 8589934592 | bytes 33554432 | tf_op jit(solution)/shard_map/last_sums/pallas_call | solution.py:591
  206.2 1.1 fusion.10
  207.3 1.9 copy.33
  209.3 1.9 copy.34
  211.2 0.6 slice_bitcast_fusion
  211.8 0.6 fusion.11
  212.4 25.7 %all-reduce.3.cloned.1.call-done = (bf16[128,1024]{1,0:T(8,128)(2,1)}, bf16[1024,576]{0,1:T(8,128)(2,1)}, bf16[1024,576]{0,1:T(8,128)(2,1)}, bf16[576,1024]{1,0:T(8,128)(2,1)}) async-done(((bf16[128,1024]{1,0:T(8,128)(2,1)}, bf16[1024,576]{0,1:T(8,128)(2,1)}, bf16[1024,576]{0,1:T(8,128)(2,1)}, bf16[576,1024]{1,0:T(8,128)(2,1)}), (bf16[128,1024]{1,0:T(8,128)(2,1)}, bf16[1024,576]{0,1:T(8,128)(2,1)}, ...) | async-done | bytes 3801104 | tf_op jit(solution)/shard_map/psum | solution.py:784
  238.1 1.8 convert_element_type.61
  239.9 3.1 %convert_element_type.63 = f32[1024,576]{0,1:T(8,128)} convert(bf16[1024,576]{0,1:T(8,128)(2,1)} %get-tuple-element.72) | non-fusion elementwise | flops 589824 | bytes 3538944 | tf_op jit(solution)/shard_map/convert_element_type | solution.py:784
  242.9 1.7 convert_element_type.65
  244.6 1.7 convert_element_type.67
  246.3 1.0 copy.42
  247.3 1.0 copy.43
  248.3 0.4 copy-done.2
  248.7 0.8 copy.44
  (46 shorter events, 0.1 us)
Async XLA Ops:
  7.2 77.3 %copy-start = (bf16[1024,576]{0,1:T(8,128)(2,1)S(1)}, bf16[1024,576]{0,1:T(8,128)(2,1)}, u32[]{:S(2)}) copy-start(bf16[1024,576]{0,1:T(8,128)(2,1)} %param.24) | copy-start | bytes 3538948
  7.2 11.1 %copy-start.5 = (bf16[512,1024]{1,0:T(8,128)(2,1)S(1)}, bf16[512,1024]{1,0:T(8,128)(2,1)}, u32[]{:S(2)}) copy-start(bf16[512,1024]{1,0:T(8,128)(2,1)} %tok_ref.1) | copy-start | bytes 3145732
  7.2 11.1 %copy-start.10 = (f32[1024]{0:T(1024)S(1)}, f32[1024]{0:T(1024)}, u32[]{:S(2)}) copy-start(f32[1024]{0:T(1024)} %param.15) | copy-start | bytes 12292
  7.2 11.1 %copy-start.8 = (bf16[1024,128]{1,0:T(8,128)(2,1)S(1)}, bf16[1024,128]{1,0:T(8,128)(2,1)}, u32[]{:S(2)}) copy-start(bf16[1024,128]{1,0:T(8,128)(2,1)} %wq_ref.3) | copy-start | bytes 786436
  7.2 11.1 %copy-start.11 = (f32[64]{0:T(128)S(1)}, f32[64]{0:T(128)}, u32[]{:S(2)}) copy-start(f32[64]{0:T(128)} %param.19) | copy-start | bytes 772
  7.2 11.1 %copy-start.12 = (f32[64]{0:T(128)S(1)}, f32[64]{0:T(128)}, u32[]{:S(2)}) copy-start(f32[64]{0:T(128)} %param.20) | copy-start | bytes 772
  7.2 230.8 %all-reduce.3.cloned.1.call-start = ((), (), s32[]{:S(2)}) async-start(), calls=%async_computation | async-start | bytes 7602176 | tf_op jit(solution)/shard_map/psum | solution.py:784
  20.3 23.3 %copy-start.17 = (bf16[512,1024]{1,0:T(8,128)(2,1)}, bf16[512,1024]{1,0:T(8,128)(2,1)S(1)}, u32[]{:S(2)}) copy-start(bf16[512,1024]{1,0:T(8,128)(2,1)S(1)} %get-tuple-element.59.n_ref) | copy-start | bytes 3145732
  20.4 23.3 %copy-start.21 = (f32[512,128]{1,0:T(8,128)}, f32[512,128]{1,0:T(8,128)S(1)}, u32[]{:S(2)}) copy-start(f32[512,128]{1,0:T(8,128)S(1)} %get-tuple-element.57.qp_ref) | copy-start | bytes 786436
  20.4 23.3 %copy-start.23 = (f32[512,128]{1,0:T(8,128)}, f32[512,128]{1,0:T(8,128)S(1)}, u32[]{:S(2)}) copy-start(f32[512,128]{1,0:T(8,128)S(1)} %get-tuple-element.58.kvp_ref) | copy-start | bytes 786436
  20.4 23.3 %copy-start.3 = (s32[4]{0:T(128)S(1)}, s32[4]{0:T(128)}, u32[]{:S(2)}) copy-start(s32[4]{0:T(128)} %len_ref.3) | copy-start | bytes 52
  43.7 11.0 %copy-start.13 = (bf16[4,4,2,256,128]{4,3,2,1,0:T(8,128)(2,1)}, bf16[4,4,2,256,128]{4,3,2,1,0:T(8,128)(2,1)S(1)}, u32[]{:S(2)}) copy-start(bf16[4,4,2,256,128]{4,3,2,1,0:T(8,128)(2,1)S(1)} %get-tuple-element.45) | copy-start | bytes 6291460
  43.7 11.0 %copy-start.7 = (bf16[128,1024]{1,0:T(8,128)(2,1)S(1)}, bf16[128,1024]{1,0:T(8,128)(2,1)}, u32[]{:S(2)}) copy-start(bf16[128,1024]{1,0:T(8,128)(2,1)} %w_ref.3) | copy-start | bytes 786436
  43.7 11.0 %copy-start.9 = (f32[1024]{0:T(1024)S(1)}, f32[1024]{0:T(1024)}, u32[]{:S(2)}) copy-start(f32[1024]{0:T(1024)} %param.22) | copy-start | bytes 12292
  54.7 27.4 %copy-start.19 = (bf16[2,512,256]{2,1,0:T(8,128)(2,1)}, bf16[2,512,256]{2,1,0:T(8,128)(2,1)S(1)}, u32[]{:S(2)}) copy-start(bf16[2,512,256]{2,1,0:T(8,128)(2,1)S(1)} %get-tuple-element.50.qa_ref) | copy-start | bytes 1572868
  54.7 27.4 %copy-start.25 = (f32[512,128]{1,0:T(8,128)}, f32[512,128]{1,0:T(8,128)S(1)}, u32[]{:S(2)}) copy-start(f32[512,128]{1,0:T(8,128)S(1)} %get-tuple-element.51.out_ref) | copy-start | bytes 786436
  54.8 27.3 %copy-start.33 = (bf16[1024,576]{0,1:T(8,128)(2,1)S(1)}, bf16[1024,576]{0,1:T(8,128)(2,1)}, u32[]{:S(2)}) copy-start(bf16[1024,576]{0,1:T(8,128)(2,1)} %param.23) | copy-start | bytes 3538948
  82.1 1.2 copy-start.4
  82.1 1.6 copy-start.34
  126.0 0.7 copy-start.15
  126.6 0.7 copy-start.27
  127.3 0.6 copy-start.29
  129.0 1.6 copy-start.14
  130.6 0.9 copy-start.16
  131.5 1.0 copy-start.20
  132.5 0.9 copy-start.26
  149.8 20.6 %copy-start.18 = (bf16[512,1024]{1,0:T(8,128)(2,1)S(1)}, bf16[512,1024]{1,0:T(8,128)(2,1)}, u32[]{:S(2)}) copy-start(bf16[512,1024]{1,0:T(8,128)(2,1)} %copy-done.17) | copy-start | bytes 3145732
  149.8 20.6 %copy-start.22 = (f32[512,128]{1,0:T(8,128)S(1)}, f32[512,128]{1,0:T(8,128)}, u32[]{:S(2)}) copy-start(f32[512,128]{1,0:T(8,128)} %copy-done.21) | copy-start | bytes 786436
  149.8 20.6 %copy-start.24 = (f32[512,128]{1,0:T(8,128)S(1)}, f32[512,128]{1,0:T(8,128)}, u32[]{:S(2)}) copy-start(f32[512,128]{1,0:T(8,128)} %copy-done.23) | copy-start | bytes 786436
  170.4 3.0 %copy-start.6 = (bf16[512,1024]{1,0:T(8,128)(2,1)S(1)}, bf16[512,1024]{1,0:T(8,128)(2,1)}, u32[]{:S(2)}) copy-start(bf16[512,1024]{1,0:T(8,128)(2,1)} %tok_ref.1) | copy-start | bytes 3145732
  170.4 3.0 %copy-start.28 = (f32[64,1024]{1,0:T(8,128)S(1)}, f32[64,1024]{1,0:T(8,128)}, u32[]{:S(2)}) copy-start(f32[64,1024]{1,0:T(8,128)} %copy-done.27) | copy-start | bytes 786436
  170.4 3.0 %copy-start.30 = (f32[1,1024]{1,0:T(1,128)S(1)}, f32[1,1024]{1,0:T(1,128)}, u32[]{:S(2)}) copy-start(f32[1,1024]{1,0:T(1,128)} %copy-done.29) | copy-start | bytes 12292
  206.2 1.1 copy-start.1
  239.9 3.1 %copy-start.32 = (bf16[1024,576]{0,1:T(8,128)(2,1)S(1)}, bf16[1024,576]{0,1:T(8,128)(2,1)}, u32[]{:S(2)}) copy-start(bf16[1024,576]{0,1:T(8,128)(2,1)} %get-tuple-element.73) | copy-start | bytes 3538948
  242.9 1.7 copy-start.31
  247.3 1.4 copy-start.2
Sparse Core Ops, SparseCore 0:
  129.1 108.9 all-reduce.2

commit v2 on v1

--- a/solution.py
+++ b/solution.py
@@ -1,6 +1,7 @@
 import functools, math
 import jax
 import jax.numpy as jnp
+import numpy as np
 from jax import lax
 from jax.experimental import pallas as pl
 from jax.experimental.pallas import tpu as pltpu
@@ -8,6 +9,8 @@
 
 f32 = jnp.float32
 bf16 = jnp.bfloat16
+sds = jax.ShapeDtypeStruct
+DMA = pltpu.SemaphoreType.DMA
 CH = 512
 HALF = 256
 SCALE = 0.125
@@ -32,16 +35,6 @@
     return start
 
 
-def key_ranges(r0, len_ref, ch):
-    low = scalar_start(r0, len_ref)
-    high = scalar_start(r0 + HALF - 1, len_ref)
-    first = low // ch
-    last = (r0 + HALF - 1) // ch + 1
-    free = jnp.clip((high + ch - 1) // ch, first, last)
-    diag = jnp.clip((r0 + 1) // ch, free, last)
-    return first, free, diag, last
-
-
 def lanes(shape):
     return lax.broadcasted_iota(jnp.int32, shape, len(shape) - 1)
 
@@ -58,34 +51,69 @@
     return me * 512 if t == 0 else (parts - 1 - me) * 512 + HALF
 
 
-def fwd_kernel(parts, me_ref, len_ref, q_ref, kv_ref, mix_ref, out_ref, qa_ref, qs_ref, acc_ref):
-    me = me_ref[0]
+FAR = 8192.0
+
+
+def segment_bounds(len_ref, lane):
+    begin = jnp.zeros_like(lane)
+    end = jnp.zeros_like(lane)
+    at = jnp.int32(0)
+    for j in range(4):
+        begin = jnp.where(lane == 3 + j, at, begin)
+        at = at + len_ref[j]
+        end = jnp.where(lane == 3 + j, at, end)
+    return begin, end
+
+
+def inside(ids, len_ref, shape):
+    lane = lanes(shape)
+    begin, end = segment_bounds(len_ref, lane)
+    return (ids >= begin) & (ids < end), lane
+
+
+def key_columns(k0, len_ref, rows):
+    ids = k0 + lax.broadcasted_iota(jnp.int32, (rows, 128), 0)
+    within, lane = inside(ids, len_ref, (rows, 128))
+    return jnp.where(lane < 3, 1.0, jnp.where(within, 1.0, 0.0)).astype(bf16)
+
+
+def query_columns(r0, len_ref, rows):
+    ids = r0 + lax.broadcasted_iota(jnp.int32, (rows, 128), 0)
+    within, lane = inside(ids, len_ref, (rows, 128))
+    return jnp.where((lane < 3) | (lane > 6) | within, 0.0, -FAR)
+
+
+def fwd_kernel(parts, len_ref, q_ref, kv_ref, ext_ref, mix_ref, out_ref, qa_ref, acc_ref):
+    me = lax.axis_index("sp")
     lane = lanes((HALF, 128))
     lane2 = lanes((2 * HALF, 128))
     lanek = lanes((CH, 128))
     for t in range(2):
         r0 = tile_row(me, t, parts)
         q = q_ref[t * HALF:(t + 1) * HALF, :].astype(f32)
-        qs_ref[0:HALF, :] = jnp.where(lane < 64, q, 0.0).astype(bf16)
-        qs_ref[HALF:, :] = jnp.where(lane < 64, pltpu.roll(q, 64, 1), 0.0).astype(bf16)
+        qa_ref[t, 0:HALF, 0:128] = jnp.where(lane < 64, q, 0.0).astype(bf16)
+        qa_ref[t, HALF:, 0:128] = jnp.where(lane < 64, pltpu.roll(q, 64, 1), 0.0).astype(bf16)
+        columns = query_columns(r0, len_ref, HALF)
+        columns = jnp.concatenate([columns, columns], axis=0)
+        qa_ref[t, :, 128:256] = columns.astype(bf16)
         acc_ref[...] = jnp.zeros_like(acc_ref)
 
         def step(c, masked):
             k0 = pl.multiple_of(c * CH, CH)
             kv = kv_ref[pl.ds(k0, CH), :]
-            s = lax.dot_general(qs_ref[...], kv, (((1,), (1,)), ((), ())), preferred_element_type=f32)
+            kva = jnp.concatenate([kv, ext_ref[pl.ds(k0, CH), :]], axis=1)
+            s = lax.dot_general(qa_ref[t], kva, (((1,), (1,)), ((), ())), preferred_element_type=f32)
             p = jnp.exp2(s * C2)
             if masked:
                 rows = r0 + lax.rem(lax.broadcasted_iota(jnp.int32, (2 * HALF, 1), 0), HALF)
                 keys = k0 + lax.broadcasted_iota(jnp.int32, (2 * HALF, CH), 1)
-                p = jnp.where((keys <= rows) & (keys >= starts_of(rows, len_ref)), p, 0.0)
+                p = jnp.where(keys <= rows, p, 0.0)
             ones = jnp.where(lanek < 64, jnp.ones_like(kv), kv)
             acc_ref[...] += jnp.dot(p.astype(bf16), ones, preferred_element_type=f32)
 
-        first, free, diag, last = key_ranges(r0, len_ref, CH)
-        pl.loop(first, free)(lambda c: step(c, True))
-        pl.loop(free, diag)(lambda c: step(c, False))
-        pl.loop(diag, last)(lambda c: step(c, True))
+        block = me if t == 0 else parts - 1 - me
+        pl.loop(0, block)(lambda c: step(c, False))
+        step(block, True)
 
         acc = acc_ref[...]
         swapped = pltpu.roll(acc, 64, 1)
@@ -94,14 +122,19 @@
         mix_ref[t * HALF:(t + 1) * HALF, :] = m.astype(bf16)
         out_ref[t * HALF:(t + 1) * HALF, :] = m
         total = jnp.where(lane2 < 64, acc, swapped)
-        qa_ref[t, :, 0:128] = qs_ref[...]
-        qa_ref[t, :, 128:256] = split3(jnp.log(total) * (-1.0 / SCALE), lane2).astype(bf16)
-
-
-def bwd_kernel(parts, me_ref, len_ref, qa_ref, out_ref, do_ref, kv_ref, dq_ref, dkv_ref, da_ref, acc_ref, dqt_ref):
-    me = me_ref[0]
+        qa_ref[t, :, 128:256] = (split3(jnp.log(total) * (-1.0 / SCALE), lane2) + columns).astype(bf16)
+
+
+def bwd_kernel(parts, qa_ref, out_ref, do_ref, kv_ref, ext_ref, red_ref, dq_ref, dkv_ref, grads_ref, da_ref, acc_ref, dqt_ref, *sems):
+    me = lax.axis_index("sp")
+    p = Place()
+    meet([p.along_x(d) for d in ORDER] + [p.along_y(d) for d in ORDER])
+    spread = SpGather(p, grads_ref, 144, sems)
+    for i in range(2):
+        for h in range(2):
+            spread.put(i, h, red_ref[i, h])
+            spread.first(i, h)
     lane = lanes((HALF, 128))
-    ones3 = jnp.where(lanes((CH, 128)) < 3, 1.0, 0.0).astype(bf16)
     acc_ref[...] = jnp.zeros_like(acc_ref)
     for t in range(2):
         r0 = tile_row(me, t, parts)
@@ -119,7 +152,7 @@
         def step(c, masked):
             k0 = pl.multiple_of(c * CH, CH)
             kv = kv_ref[pl.ds(k0, CH), :]
-            kva = jnp.concatenate([kv, ones3], axis=1)
+            kva = jnp.concatenate([kv, ext_ref[pl.ds(k0, CH), :]], axis=1)
             qa = qa_ref[t]
             da = da_ref[...]
             s = lax.dot_general(kva, qa, (((1,), (1,)), ((), ())), preferred_element_type=f32)
@@ -127,7 +160,7 @@
             if masked:
                 rows = r0 + lax.rem(lax.broadcasted_iota(jnp.int32, (1, 2 * HALF), 1), HALF)
                 keys = k0 + lax.broadcasted_iota(jnp.int32, (CH, 2 * HALF), 0)
-                p = jnp.where((keys <= rows) & (keys >= starts_of(rows, len_ref)), p, 0.0)
+                p = jnp.where(keys <= rows, p, 0.0)
             dp = lax.dot_general(kva, da, (((1,), (1,)), ((), ())), preferred_element_type=f32)
             ds = (p * dp).astype(bf16)
             acc_ref[pl.ds(k0, CH), :] += jnp.dot(
@@ -136,11 +169,14 @@
             kt = kv.T[0:64, :]
             dqt_ref[...] += jnp.dot(kt, ds, preferred_element_type=f32)
 
-        first, free, diag, last = key_ranges(r0, len_ref, CH)
-        pl.loop(first, free)(lambda c: step(c, True))
-        pl.loop(free, diag)(lambda c: step(c, False))
-        pl.loop(diag, last)(lambda c: step(c, True))
+        block = me if t == 0 else parts - 1 - me
+        pl.loop(0, block)(lambda c: step(c, False))
+        step(block, True)
         dqt = dqt_ref[...]
+        if t == 0:
+            for i in range(2):
+                for h in range(2):
+                    spread.second(i, h)
         both = jnp.concatenate([dqt[:, :HALF], dqt[:, HALF:]], axis=0)
         dq_ref[rows_t, :] = (both.T * SCALE).astype(bf16)
     weight = jnp.where(lanes((512, 128)) < 64, SCALE, 1.0)
@@ -150,39 +186,42 @@
         rows = pl.ds(pl.multiple_of(b * 512, 512), 512)
         dkv_ref[rows, :] = (acc_ref[rows, :] * weight).astype(bf16)
 
+    spread.finish()
+
 
 smem = pl.BlockSpec(memory_space=pltpu.SMEM)
 vmem = pl.BlockSpec(memory_space=pltpu.VMEM)
 
 
-def attend(parts, me, lengths, q, kv):
+def attend(parts, lengths, q, kv, ext):
     rows = 2 * HALF
-    sds = jax.ShapeDtypeStruct
     return pl.pallas_call(
         functools.partial(fwd_kernel, parts),
         out_shape=(sds((rows, 128), bf16), sds((rows, 128), f32), sds((2, rows, 256), bf16)),
-        in_specs=[smem, smem, vmem, vmem],
+        in_specs=[smem, vmem, vmem, vmem],
         out_specs=(vmem, vmem, vmem),
-        scratch_shapes=[pltpu.VMEM((rows, 128), bf16), pltpu.VMEM((rows, 128), f32)],
-        compiler_params=pltpu.CompilerParams(vmem_limit_bytes=48 << 20),
+        scratch_shapes=[pltpu.VMEM((rows, 128), f32)],
+        compiler_params=pltpu.CompilerParams(vmem_limit_bytes=12 << 20),
         cost_estimate=pl.CostEstimate(flops=3 << 30, bytes_accessed=4 << 20, transcendentals=5 << 20),
         name="attend",
-    )(me, lengths, q, kv)
-
-
-def attend_back(parts, me, lengths, qa, out, do, kv):
+    )(lengths, q, kv, ext)
+
+
+def attend_back(parts, qa, out, do, kv, ext, red):
     rows = 2 * HALF
-    sds = jax.ShapeDtypeStruct
     return pl.pallas_call(
         functools.partial(bwd_kernel, parts),
-        out_shape=(sds((rows, 128), bf16), sds(kv.shape, bf16)),
-        in_specs=[smem, smem, vmem, vmem, vmem, vmem],
-        out_specs=(vmem, vmem),
-        scratch_shapes=[pltpu.VMEM((rows, 256), bf16), pltpu.VMEM(kv.shape, f32), pltpu.VMEM((64, rows), f32)],
-        compiler_params=pltpu.CompilerParams(vmem_limit_bytes=48 << 20),
+        out_shape=(sds((rows, 128), bf16), sds(kv.shape, bf16), sds((2, 4, 144, 1024), bf16)),
+        in_specs=[vmem] * 6,
+        out_specs=(vmem, vmem, vmem),
+        scratch_shapes=[pltpu.VMEM((rows, 256), bf16), pltpu.VMEM(kv.shape, f32), pltpu.VMEM((64, rows), f32)]
+        + SpGather.sems(2),
+        compiler_params=pltpu.CompilerParams(collective_id=6, has_side_effects=True, vmem_limit_bytes=20 << 20),
         cost_estimate=pl.CostEstimate(flops=10 << 30, bytes_accessed=8 << 20, transcendentals=5 << 20),
         name="attend_back",
-    )(me, lengths, qa, out, do, kv)
+    )(qa, out, do, kv, ext, red)
+
+
 MESH = pl.DeviceIdType.MESH
 eps = 1e-05
 
@@ -241,7 +280,7 @@
 ORDER = (2, 1, 3)
 
 
-def gather_kernel(q_ref, kv_ref, qz_ref, all_ref, ms, mr, fs, fr, ss, sr):
+def gather_kernel(len_ref, q_ref, kv_ref, qz_ref, all_ref, ext_ref, ms, mr, fs, fr, ss, sr):
     p = Place()
     meet([p.along_x(d) for d in ORDER] + [p.along_y(d) for d in ORDER] + [p.mirror])
     all_ref[p.x, p.y] = kv_ref[...]
@@ -268,6 +307,11 @@
     for h in range(2):
         forward(h, 0)
     qz_ref[0] = q_ref[0]
+    @pl.loop(0, 8)
+    def _(b):
+        rows = pl.ds(pl.multiple_of(b * 1024, 1024), 1024)
+        ext_ref[rows, :] = key_columns(b * 1024, len_ref, 1024)
+
     for d in (1, 3, 2):
         for h in range(2):
             first[h, d].wait_recv()
@@ -319,6 +363,127 @@
     mirror.wait()
     for copy in list(first.values()) + list(second.values()):
         copy.wait_send()
+
+
+class SpScatter:
+    def __init__(self, p, srcs, rows, refs):
+        self.p, self.srcs, self.rows = p, srcs, rows
+        self.ra, self.rb, self.send, self.r2, self.fs, self.fr, self.ss, self.sr = refs
+        self.one, self.two = {}, {}
+
+    @staticmethod
+    def scratch(n, rows):
+        return [
+            pltpu.VMEM((n, 3, rows, 512), bf16), pltpu.VMEM((n, 3, 4, rows, 128), bf16),
+            pltpu.VMEM((n, 2, 3, rows, 128), bf16), pltpu.VMEM((n, 2, 3, rows, 128), bf16),
+            DMA((n, 2, 3)), DMA((n, 2, 3)), DMA((n, 2, 3)), DMA((n, 2, 3)),
+        ]
+
+    def first(self, i):
+        p = self.p
+        for d in ORDER:
+            to = lax.rem(p.x + d, 4)
+            self.one[i, 0, d] = rcopy(
+                self.srcs[i].at[to, :, pl.ds(0, 512)], self.ra.at[i, d - 1],
+                self.fs.at[i, 0, d - 1], self.fr.at[i, 0, d - 1], p.along_x(d),
+            )
+            self.one[i, 0, d].start()
+            to = lax.rem(p.y + d, 4)
+            self.one[i, 1, d] = rcopy(
+                self.srcs[i].at[:, :, pl.ds(columns_at(1, to), 128)], self.rb.at[i, d - 1],
+                self.fs.at[i, 1, d - 1], self.fr.at[i, 1, d - 1], p.along_y(d),
+            )
+            self.one[i, 1, d].start()
+
+    def part(self, i, h, b):
+        p = self.p
+        if h == 0:
+            value = self.srcs[i][p.x, :, pl.ds(columns_at(0, b), 128)].astype(f32)
+            for d in range(3):
+                value = value + self.ra[i, d, :, pl.ds(columns_at(0, b), 128)].astype(f32)
+            return value
+        value = self.srcs[i][b, :, pl.ds(columns_at(1, p.y), 128)].astype(f32)
+        for d in range(3):
+            value = value + self.rb[i, d, b].astype(f32)
+        return value
+
+    def second(self, i):
+        p = self.p
+        for h in range(2):
+            for d in ORDER:
+                self.one[i, h, d].wait_recv()
+            for e in ORDER:
+                self.send[i, h, e - 1] = self.part(i, h, lax.rem(p.ssp(h) + e, 4)).astype(bf16)
+                self.two[i, h, e] = rcopy(
+                    self.send.at[i, h, e - 1], self.r2.at[i, h, e - 1],
+                    self.ss.at[i, h, e - 1], self.sr.at[i, h, e - 1], p.second(h, e),
+                )
+                self.two[i, h, e].start()
+
+    def own(self, i, h):
+        value = self.part(i, h, self.p.ssp(h))
+        for e in ORDER:
+            self.two[i, h, e].wait_recv()
+            value = value + self.r2[i, h, e - 1].astype(f32)
+        return value
+
+    def finish(self):
+        for copy in list(self.one.values()) + list(self.two.values()):
+            copy.wait_send()
+
+
+def columns_at(h, b):
+    return pl.multiple_of(h * 512 + b * 128, 128)
+
+
+class SpGather:
+    def __init__(self, p, out, rows, sems):
+        self.p, self.out, self.rows = p, out, rows
+        self.fs, self.fr, self.ss, self.sr = sems
+        self.one, self.two = {}, {}
+
+    @staticmethod
+    def sems(n):
+        return [DMA((n, 2, 3)) for _ in range(4)]
+
+    def spot(self, h):
+        p = self.p
+        return p.x, pl.ds(columns_at(h, p.y), 128)
+
+    def put(self, i, h, value):
+        x, columns = self.spot(h)
+        self.out[i, x, :, columns] = value
+
+    def first(self, i, h):
+        x, columns = self.spot(h)
+        block = self.out.at[i, x, :, columns]
+        for e in ORDER:
+            self.one[i, h, e] = rcopy(
+                block, block, self.fs.at[i, h, e - 1], self.fr.at[i, h, e - 1], self.p.second(h, e)
+            )
+            self.one[i, h, e].start()
+
+    def second(self, i, h):
+        x, columns = self.spot(h)
+        for e in ORDER:
+            self.one[i, h, e].wait_recv()
+        block = self.out.at[i, x, :, pl.ds(0, 512)] if h == 0 else self.out.at[i, :, :, columns]
+        for d in ORDER:
+            self.two[i, h, d] = rcopy(
+                block, block, self.ss.at[i, h, d - 1], self.sr.at[i, h, d - 1], self.p.first(h, d)
+            )
+            self.two[i, h, d].start()
+
+    def arrived(self, i):
+        for h in range(2):
+            for d in ORDER:
+                self.two[i, h, d].wait_recv()
+
+    def finish(self):
+        for copy in self.one.values():
+            copy.wait_send()
+        for copy in self.two.values():
+            copy.wait()
 
 
 class WtSum:
@@ -441,16 +606,22 @@
     total.finish()
 
 
-def turn_kernel(dm_ref, mlp_ref, mid_ref, cot_ref, gain_ref, w_ref, out_ref, da_ref, dmid_ref, gn_ref, dz_ref, up, sib, send, rz, ms, mr, cs, cr, zs, zr, az, bz, ag, bg):
+def turn_kernel(dm_ref, mlp_ref, mid_ref, cot_ref, gain_ref, w_ref, g0_ref, g1_ref, g2_ref,
+                out_ref, da_ref, dmid_ref, gn_ref, dz_ref, red_ref,
+                up, sib, send, rz, ms, mr, cs, cr, zs, zr, az, bz, ag, bg, *grad_refs):
     p = Place()
-    meet(wt_peers(p) + [p.mirror])
+    meet(wt_peers(p) + [p.mirror] + [p.along_x(d) for d in ORDER] + [p.along_y(d) for d in ORDER])
     totals = [
         WtSum(p, ref, sib.at[i], send.at[i], rz.at[i], (cs.at[i], cr.at[i], zs.at[i], zr.at[i]))
         for i, ref in enumerate((dm_ref, mlp_ref))
     ]
-    for total in totals:
-        for zz in range(4):
-            total.start_core(zz)
+    grads = SpScatter(p, (g0_ref, g1_ref, g2_ref), 144, grad_refs)
+    for zz in range(4):
+        totals[0].start_core(zz)
+    for i in range(3):
+        grads.first(i)
+    for zz in range(4):
+        totals[1].start_core(zz)
     for total in totals:
         for d in ORDER:
             total.send_z(d)
@@ -465,8 +636,10 @@
         WtGather(p, ref, (az.at[i], bz.at[i], ag.at[i], bg.at[i])) for i, ref in enumerate((da_ref, out_ref))
     ]
     spreads[0].start()
+    grads.second(0)
     out_ref[p.wt] = (middle + totals[1].own()).astype(bf16)
     spreads[1].start()
+    grads.second(1)
     spreads[0].forward()
     spreads[0].arrived()
     mirror = rcopy(up, dz_ref.at[1], ms, mr, p.mirror)
@@ -478,57 +651,45 @@
             mirror.start()
         else:
             dz_ref[0] = d_mixed
+    grads.second(2)
     spreads[1].forward()
+    for i in range(3):
+        for h in range(2):
+            red_ref[i, h] = grads.own(i, h).astype(bf16)
     spreads[1].arrived()
     mirror.wait()
-    for part in spreads + totals:
+    for part in spreads + totals + [grads]:
         part.finish()
 
 
-def last_kernel(dn_ref, g_ref, tok_ref, dmid_ref, gain_ref, gn_ref, gg_ref, gt_ref, gq_ref, gkv_ref, vec_ref,
+def last_kernel(dn_ref, gq_ref, go_ref, red_ref, tok_ref, dmid_ref, gain_ref, gn_ref, gg_ref,
+                gt_ref, sums_ref, gd_ref, vec_ref,
                 sib, send, rz, cs, cr, zs, zr, az, bz, ag, bg,
-                r1, s2, r2, gb, f1s, f1r, f2s, f2r, f3s, f3r, f4s, f4r,
-                vw, vx, vy, vr, vs1, vr1, vs2, vr2, vs3, vr3):
+                vw, vx, vy, vs1, vr1, vs2, vr2, vs3, vr3, *more):
     p = Place()
     meet(wt_peers(p) + [p.along_z_other(d) for d in ORDER] + [p.along_x(d) for d in ORDER] + [p.along_y(d) for d in ORDER])
     total = WtSum(p, dn_ref, sib, send, rz, (cs, cr, zs, zr))
     for zz in range(4):
         total.start_core(zz)
-    first, second, third, fourth = {}, {}, {}, {}
-    for d in ORDER:
-        for h in range(2):
-            to = lax.rem(p.fsp(h) + d, 4)
-            src = g_ref.at[h, to] if h == 0 else g_ref.at[h, :, to]
-            first[h, d] = rcopy(src, r1.at[h, d - 1], f1s.at[h, d - 1], f1r.at[h, d - 1], p.first(h, d))
-            first[h, d].start()
+    grads = SpScatter(p, (gq_ref.at[0], gq_ref.at[1], go_ref), 32, more[:8])
+    back = SpGather(p, sums_ref, 32, more[8:12])
+    down = SpGather(p, gd_ref, 144, more[12:16])
+    for h in range(2):
+        down.put(0, h, red_ref[h])
+        down.first(0, h)
+    for i in range(3):
+        grads.first(i)
     for d in ORDER:
         total.send_z(d)
 
-    def part_of(h, b):
-        at = spot(h, p.fsp(h), b)
-        value = g_ref[h, at[0], at[1]].astype(f32)
-        for d in range(3):
-            value = value + r1[h, d, b].astype(f32)
-        return value
-
-    for h in range(2):
-        for d in ORDER:
-            first[h, d].wait_recv()
-        for e in ORDER:
-            s2[h, e - 1] = part_of(h, lax.rem(p.ssp(h) + e, 4)).astype(bf16)
-            second[h, e] = rcopy(s2.at[h, e - 1], r2.at[h, e - 1], f2s.at[h, e - 1], f2r.at[h, e - 1], p.second(h, e))
-            second[h, e].start()
-
-    base = tok_ref[p.wt].astype(f32)
-    scale = rms_of(base)
-    d_normed = total.own()
-    gt_ref[p.wt] = (dmid_ref[...] + norm_back(base, scale, gain_ref[...], d_normed)).astype(bf16)
-    spread = WtGather(p, gt_ref, (az, bz, ag, bg))
-    spread.start()
-    vw[0, 0:1] = jnp.sum(d_normed * base * scale, axis=0, keepdims=True)
+    vw[0] = jnp.zeros((8, 1024), f32)
+    gains = jnp.zeros((1, 1024), f32)
+    for w in range(8):
+        base = tok_ref[w].astype(f32)
+        gains = gains + jnp.sum(dn_ref[w].astype(f32) * base * rms_of(base), axis=0, keepdims=True)
+    vw[0, 0:1] = gains
     vw[0, 1:2] = gn_ref[...]
     vw[0, 2:3] = gg_ref[...]
-    vw[0, 3:8] = jnp.zeros((5, 1024), f32)
 
     def vec_round(buf, devices, sends, recvs):
         copies = []
@@ -545,70 +706,60 @@
         return value
 
     round1 = vec_round(vw, [p.along_z(d) for d in ORDER] + [p.along_z_other(d) for d in ORDER] + [p.sibling], vs1, vr1)
-
-    for h in range(2):
-        value = part_of(h, p.ssp(h))
-        for e in ORDER:
-            second[h, e].wait_recv()
-            value = value + r2[h, e - 1].astype(f32)
-        gb[h, p.x, p.y] = value.astype(bf16)
-        for e in ORDER:
-            third[h, e] = rcopy(gb.at[h, p.x, p.y], gb.at[h, p.x, p.y], f3s.at[h, e - 1], f3r.at[h, e - 1], p.second(h, e))
-            third[h, e].start()
-
+    for i in range(3):
+        grads.second(i)
+    base = tok_ref[p.wt].astype(f32)
+    d_normed = total.own()
+    gt_ref[p.wt] = (dmid_ref[...] + norm_back(base, rms_of(base), gain_ref[...], d_normed)).astype(bf16)
+    spread = WtGather(p, gt_ref, (az, bz, ag, bg))
+    spread.start()
+    for i in range(3):
+        for h in range(2):
+            back.put(i, h, grads.own(i, h).astype(bf16))
+            back.first(i, h)
     vx[0] = vec_total(vw, round1)
     round2 = vec_round(vx, [p.along_x(d) for d in ORDER], vs2, vr2)
     for h in range(2):
-        for e in ORDER:
-            third[h, e].wait_recv()
-        mine = gb.at[h, p.x] if h == 0 else gb.at[h, :, p.y]
-        for d in ORDER:
-            fourth[h, d] = rcopy(mine, mine, f4s.at[h, d - 1], f4r.at[h, d - 1], p.first(h, d))
-            fourth[h, d].start()
-    spread.forward()
+        down.second(0, h)
+    for i in range(3):
+        for h in range(2):
+            back.second(i, h)
     vy[0] = vec_total(vx, round2)
     round3 = vec_round(vy, [p.along_y(d) for d in ORDER], vs3, vr3)
-    for copy in fourth.values():
-        copy.wait_recv()
-    gq_ref[...] = gb[0].astype(f32)
-    gkv_ref[...] = gb[1].astype(f32)
+    spread.forward()
     vec_ref[...] = vec_total(vy, round3)
     spread.arrived()
     spread.finish()
     total.finish()
-    for group in (first, second, third, fourth):
-        for copy in group.values():
-            copy.wait_send()
+    grads.finish()
+    back.finish()
+    down.finish()
     for copy in round1 + round2 + round3:
         copy.wait_send()
 
 
-DMA = pltpu.SemaphoreType.DMA
-sds = jax.ShapeDtypeStruct
-
-
-def comm_call(kernel, number, out_shape, args, scratch, name):
+def comm_call(kernel, number, out_shape, args, scratch, name, limit=10, first=None):
     return pl.pallas_call(
         kernel,
         out_shape=out_shape,
-        in_specs=[vmem] * len(args),
+        in_specs=[first or vmem] + [vmem] * (len(args) - 1),
         out_specs=tuple(vmem for _ in out_shape),
         scratch_shapes=scratch,
         compiler_params=pltpu.CompilerParams(
-            collective_id=number, has_side_effects=True, vmem_limit_bytes=24 << 20
+            collective_id=number, has_side_effects=True, vmem_limit_bytes=limit << 20
         ),
         cost_estimate=pl.CostEstimate(flops=8 << 30, bytes_accessed=32 << 20, transcendentals=0),
         name=name,
     )(*args)
 
 
-def gather_keys(q, kv):
+def gather_keys(lengths, q, kv):
     return comm_call(
         gather_kernel, 1,
-        (sds((2, 256, 128), bf16), sds((4, 4, 2, 256, 128), bf16)),
-        (q.reshape(2, 256, 128), kv.reshape(2, 256, 128)),
+        (sds((2, 256, 128), bf16), sds((4, 4, 2, 256, 128), bf16), sds((8192, 128), bf16)),
+        (lengths, q.reshape(2, 256, 128), kv.reshape(2, 256, 128)),
         [DMA, DMA, DMA((2, 3)), DMA((2, 3)), DMA((2, 4, 3)), DMA((2, 4, 3))],
-        "gather_keys",
+        "gather_keys", 4, smem,
     )
 
 
@@ -635,32 +786,37 @@
     )
 
 
-def turn_back(dm, mlp, mid, cot, gain, w_out):
+def turn_back(dm, mlp, mid, cot, gain, w_out, grads):
     rows = pltpu.VMEM
     return comm_call(
         turn_kernel, 4,
-        (sds((8, 64, 1024), bf16), sds((8, 64, 1024), bf16), sds((64, 1024), f32), sds((1, 1024), f32), sds((2, 256, 128), bf16)),
-        (dm.reshape(8, 64, 1024), mlp.reshape(8, 64, 1024), mid, cot.reshape(8, 64, 1024), gain.reshape(1, 1024), w_out),
+        (sds((8, 64, 1024), bf16), sds((8, 64, 1024), bf16), sds((64, 1024), f32), sds((1, 1024), f32),
+         sds((2, 256, 128), bf16), sds((3, 2, 144, 128), bf16)),
+        (dm.reshape(8, 64, 1024), mlp.reshape(8, 64, 1024), mid, cot.reshape(8, 64, 1024), gain.reshape(1, 1024), w_out)
+        + tuple(g.reshape(4, 144, 1024) for g in grads),
         [rows((256, 128), bf16), rows((2, 4, 64, 1024), bf16), rows((2, 3, 64, 1024), bf16), rows((2, 3, 64, 1024), bf16),
-         DMA, DMA, DMA((2, 4)), DMA((2, 4)), DMA((2, 3)), DMA((2, 3)), DMA((2, 3)), DMA((2, 3)), DMA((2, 4)), DMA((2, 4))],
-        "turn_back",
-    )
-
-
-def last_sums(dn, g, tokens, dmid, gain, gn, gg):
+         DMA, DMA, DMA((2, 4)), DMA((2, 4)), DMA((2, 3)), DMA((2, 3)), DMA((2, 3)), DMA((2, 3)), DMA((2, 4)), DMA((2, 4))]
+        + SpScatter.scratch(3, 144),
+        "turn_back", 16,
+    )
+
+
+def last_sums(dn, gq, go, red, tokens, dmid, gain, gn, gg):
     rows = pltpu.VMEM
     return comm_call(
         last_kernel, 5,
-        (sds((8, 64, 1024), bf16), sds((4, 4, 64, 128), f32), sds((4, 4, 64, 128), f32), sds((8, 1024), f32)),
-        (dn.reshape(8, 64, 1024), g.reshape(2, 4, 4, 64, 128), tokens.reshape(8, 64, 1024), dmid, gain.reshape(1, 1024), gn, gg),
+        (sds((8, 64, 1024), bf16), sds((3, 4, 32, 1024), bf16), sds((1, 4, 144, 1024), bf16), sds((8, 1024), f32)),
+        (dn.reshape(8, 64, 1024), gq.reshape(2, 4, 32, 1024), go.reshape(4, 32, 1024), red, tokens.reshape(8, 64, 1024),
+         dmid, gain.reshape(1, 1024), gn, gg),
         [rows((4, 64, 1024), bf16), rows((3, 64, 1024), bf16), rows((3, 64, 1024), bf16),
          DMA((4,)), DMA((4,)), DMA((3,)), DMA((3,)), DMA((3,)), DMA((3,)), DMA((4,)), DMA((4,)),
-         rows((2, 3, 4, 64, 128), bf16), rows((2, 3, 64, 128), bf16), rows((2, 3, 64, 128), bf16), rows((2, 4, 4, 64, 128), bf16),
-         DMA((2, 3)), DMA((2, 3)), DMA((2, 3)), DMA((2, 3)), DMA((2, 3)), DMA((2, 3)), DMA((2, 3)), DMA((2, 3)),
-         rows((8, 8, 1024), f32), rows((4, 8, 1024), f32), rows((4, 8, 1024), f32), rows((8, 1024), f32),
-         DMA((7,)), DMA((7,)), DMA((3,)), DMA((3,)), DMA((3,)), DMA((3,))],
-        "last_sums",
-    )
+         rows((8, 8, 1024), f32), rows((4, 8, 1024), f32), rows((4, 8, 1024), f32),
+         DMA((7,)), DMA((7,)), DMA((3,)), DMA((3,)), DMA((3,)), DMA((3,))]
+        + SpScatter.scratch(3, 32) + SpGather.sems(3) + SpGather.sems(1),
+        "last_sums", 10,
+    )
+
+
 def turned(value, lane):
     return jnp.where(lax.rem(lane, 64) < 32, pltpu.roll(value, 96, 1), pltpu.roll(value, 32, 1))
 
@@ -675,18 +831,34 @@
     return jnp.concatenate([gain, gain], axis=1)
 
 
-def proj_kernel(tok_ref, gain_ref, wq_ref, wk_ref, wv_ref, qg_ref, kg_ref, cos_ref, sin_ref, n_ref, qp_ref, kvp_ref, q_ref, kv_ref):
+def nt(a, b):
+    return lax.dot_general(a, b, (((1,), (1,)), ((), ())), preferred_element_type=f32)
+
+
+def tn(a, b):
+    return lax.dot_general(a, b, (((0,), (0,)), ((), ())), preferred_element_type=f32)
+
+
+def proj_kernel(len_ref, tok_ref, gain_ref, wq_ref, wk_ref, wv_ref, qg_ref, kg_ref, freq_ref,
+                n_ref, qp_ref, kvp_ref, q_ref, kv_ref, cos_ref, sin_ref):
     lane = lanes((512, 128))
+    ids = lax.axis_index("sp") * 512 + lax.broadcasted_iota(jnp.int32, (1, 512), 1)
+    positions = (ids - starts_of(ids, len_ref)).astype(f32)
+    angles = positions * freq_ref[:, 0:1]
+    cosine, sine = jnp.cos(angles), jnp.sin(angles)
+    cosine = jnp.concatenate([cosine] * 4, axis=0).T
+    sine = jnp.concatenate([-sine, sine, -sine, sine], axis=0).T
+    cos_ref[...] = cosine
+    sin_ref[...] = sine
     base = tok_ref[...].astype(f32)
     normed = (base * rms_of(base) * gain_ref[...]).astype(bf16)
     n_ref[...] = normed
-    wkv = jnp.concatenate([wk_ref[...], wv_ref[...]], axis=1)
-    cosine, sine = cos_ref[...], sin_ref[...]
+    wkv = jnp.concatenate([wk_ref[...], wv_ref[...]], axis=0)
     q = jnp.dot(normed, wq_ref[...], preferred_element_type=f32)
     qp_ref[...] = q
     q = q * lax.rsqrt(head_sums(q * q, lane) * (1.0 / 64) + eps) * twice(qg_ref[...])
     q_ref[...] = (q * cosine + turned(q, lane) * sine).astype(bf16)
-    kv = jnp.dot(normed, wkv, preferred_element_type=f32)
+    kv = nt(normed, wkv)
     kvp_ref[...] = kv
     k = kv * lax.rsqrt(head_sums(kv * kv, lane) * (1.0 / 64) + eps) * twice(kg_ref[...])
     k = k * cosine + turned(k, lane) * sine
@@ -710,23 +882,21 @@
     dk, gk = back(dkv_in, kvp_ref[...], twice(kg_ref[...]))
     dq = dq.astype(bf16)
     dkv = jnp.where(lane < 64, dk, dkv_in).astype(bf16)
-    wkv = jnp.concatenate([wk_ref[...], wv_ref[...]], axis=1)
-    dn = lax.dot_general(dq, wq_ref[...], (((1,), (1,)), ((), ())), preferred_element_type=f32)
-    dn = dn + lax.dot_general(dkv, wkv, (((1,), (1,)), ((), ())), preferred_element_type=f32)
-    dn_ref[...] = dn.astype(bf16)
+    wkv = jnp.concatenate([wk_ref[...], wv_ref[...]], axis=0)
+    dn_ref[...] = (nt(dq, wq_ref[...]) + jnp.dot(dkv, wkv, preferred_element_type=f32)).astype(bf16)
     normed = n_ref[...]
-    g_ref[0] = lax.dot_general(normed, dq, (((0,), (0,)), ((), ())), preferred_element_type=f32).astype(bf16)
-    g_ref[1] = lax.dot_general(normed, dkv, (((0,), (0,)), ((), ())), preferred_element_type=f32).astype(bf16)
+    g_ref[0] = tn(dq, normed).astype(bf16)
+    g_ref[1] = tn(dkv, normed).astype(bf16)
     gg_ref[...] = jnp.concatenate([gq, gk, jnp.zeros((1, 768), f32)], axis=1)
 
 
-def local_call(kernel, out_shape, args, name):
+def local_call(kernel, out_shape, args, name, first=None):
     return pl.pallas_call(
         kernel,
         out_shape=out_shape,
-        in_specs=[vmem] * len(args),
+        in_specs=[first or vmem] + [vmem] * (len(args) - 1),
         out_specs=tuple(vmem for _ in out_shape),
-        compiler_params=pltpu.CompilerParams(vmem_limit_bytes=32 << 20),
+        compiler_params=pltpu.CompilerParams(vmem_limit_bytes=16 << 20),
         cost_estimate=pl.CostEstimate(flops=3 << 30, bytes_accessed=16 << 20, transcendentals=0),
         name=name,
     )(*args)
@@ -737,27 +907,21 @@
 
 def body(tokens, norm_in, w_query, w_key, w_value, query_gain, key_gain, w_out, norm_mid, w_gate, w_up, w_down, cotangent, lengths):
     parts = lax.axis_size("sp")
-    sp = lax.axis_index("sp")
-    me = sp.reshape(1).astype(jnp.int32)
-    ids = sp * 512 + jnp.arange(512)
-    positions = ids - starts_of(ids, lengths)
-    index = jnp.arange(128)
-    freqs = theta ** (-((index % 32).astype(f32) * 2.0) / 64)
-    angles = positions.astype(f32)[:, None] * freqs[None, :]
-    cosine = jnp.cos(angles)
-    sine = jnp.sin(angles) * jnp.where(index % 64 < 32, -1.0, 1.0)[None, :]
+    freqs = theta ** (-(np.arange(32).astype(np.float64) * 2.0) / 64)
+    freqs = jnp.asarray(np.broadcast_to(freqs.astype(np.float32)[:, None], (32, 128)))
     qg, kg = query_gain.reshape(1, 64), key_gain.reshape(1, 64)
-    gain_in = norm_in.reshape(1, 1024)
-
-    normed, q_proj, kv_proj, q, kv = local_call(
+    wk, wv = w_key.T, w_value.T
+    wide = sds((512, 128), f32)
+
+    normed, q_proj, kv_proj, q, kv, cosine, sine = local_call(
         proj_kernel,
-        (sds((512, 1024), bf16), sds((512, 128), f32), sds((512, 128), f32), sds((512, 128), bf16), sds((512, 128), bf16)),
-        (tokens, gain_in, w_query, w_key, w_value, qg, kg, cosine, sine),
-        "project",
-    )
-    qz, kv_all = gather_keys(q, kv)
+        (sds((512, 1024), bf16), wide, wide, sds((512, 128), bf16), sds((512, 128), bf16), wide, wide),
+        (lengths, tokens, norm_in.reshape(1, 1024), w_query, wk, wv, qg, kg, freqs),
+        "project", smem,
+    )
+    qz, kv_all, ext = gather_keys(lengths, q, kv)
     kv_all = kv_all.reshape(8192, 128)
-    mix_z, mix_f, qa = attend(parts, me, lengths, qz.reshape(512, 128), kv_all)
+    mix_z, mix_f, qa = attend(parts, lengths, qz.reshape(512, 128), kv_all, ext)
     normed_mid, mid_own, mixed = make_middle(mix_z, w_out, tokens, norm_mid)
     normed_mid = normed_mid.reshape(512, 1024)
     mixed = mixed.reshape(512, 128)
@@ -774,40 +938,42 @@
         jnp.einsum("tf,df->td", d_gate, w_gate, preferred_element_type=f32)
         + jnp.einsum("tf,df->td", d_up, w_up, preferred_element_type=f32)
     ).astype(bf16)
-    g_down = jnp.einsum("tf,td->fd", act, cotangent, preferred_element_type=f32)
-    g_gate = jnp.einsum("td,tf->df", normed_mid, d_gate, preferred_element_type=f32)
-    g_up = jnp.einsum("td,tf->df", normed_mid, d_up, preferred_element_type=f32)
-
-    output, d_attn, d_middle_own, gn, d_mix_z = turn_back(d_mid_part, mlp_part, mid_own, cotangent, norm_mid, w_out)
-    g_out = jnp.einsum("tq,td->qd", mixed, d_attn.reshape(512, 1024), preferred_element_type=f32)
-    g_gate, g_up, g_down, g_out = (
-        lax.psum(g.astype(bf16), "sp").astype(f32) for g in (g_gate, g_up, g_down, g_out)
-    )
-    dq_z, dkv_all = attend_back(parts, me, lengths, qa, mix_f, d_mix_z.reshape(512, 128), kv_all)
+    grads = (
+        jnp.einsum("tf,td->fd", d_gate, normed_mid, preferred_element_type=f32).astype(bf16),
+        jnp.einsum("tf,td->fd", d_up, normed_mid, preferred_element_type=f32).astype(bf16),
+        jnp.einsum("tf,td->fd", act, cotangent, preferred_element_type=f32).astype(bf16),
+    )
+    output, d_attn, d_middle_own, gn, d_mix_z, red = turn_back(
+        d_mid_part, mlp_part, mid_own, cotangent, norm_mid, w_out, grads
+    )
+    g_out = jnp.einsum("tq,td->qd", mixed, d_attn.reshape(512, 1024), preferred_element_type=f32).astype(bf16)
+    dq_z, dkv_all, g_ff = attend_back(parts, qa, mix_f, d_mix_z.reshape(512, 128), kv_all, ext, red[:2])
     dkv, dq = scatter_keys(dkv_all, dq_z)
     dn_part, g_qkv, gg = local_call(
         proj_back_kernel,
-        (sds((512, 1024), bf16), sds((2, 1024, 128), bf16), sds((1, 1024), f32)),
-        (dq.reshape(512, 128), dkv.reshape(512, 128), q_proj, kv_proj, normed, w_query, w_key, w_value, qg, kg, cosine, sine),
+        (sds((512, 1024), bf16), sds((2, 128, 1024), bf16), sds((1, 1024), f32)),
+        (dq.reshape(512, 128), dkv.reshape(512, 128), q_proj, kv_proj, normed, w_query, wk, wv, qg, kg, cosine, sine),
         "project_back",
     )
-    grad_tokens, g_query, g_kv, vec = last_sums(dn_part, g_qkv, tokens, d_middle_own, norm_in, gn, gg)
-    g_query = g_query.reshape(1024, 128)
-    g_kv = g_kv.reshape(1024, 128)
+    grad_tokens, sums, g_down, vec = last_sums(
+        dn_part, g_qkv, g_out, red[2], tokens, d_middle_own, norm_in, gn, gg
+    )
+    sums = sums.reshape(3, 128, 1024).astype(f32)
+    g_ff = g_ff.reshape(2, 576, 1024).astype(f32)
     return (
         output.reshape(512, 1024),
         grad_tokens.reshape(512, 1024),
         vec[0],
-        g_query,
-        g_kv[:, :64],
-        g_kv[:, 64:],
+        sums[0].T,
+        sums[1, :64].T,
+        sums[1, 64:].T,
         vec[2, :64] + vec[2, 64:128],
         vec[2, 128:192],
-        g_out,
+        sums[2],
         vec[1],
-        g_gate,
-        g_up,
-        g_down,
+        g_ff[0].T,
+        g_ff[1].T,
+        g_down.reshape(576, 1024).astype(f32),
     )
 
 

time: 257 us -> 209 us (0.81)
  waiting for transfers between devices: 25.7 us -> 0 us
  between operations: 17.2 us -> 1.02 us
  Pallas kernels: 168 us -> 181 us
  other arithmetic: 13.6 us -> 3.83 us
  local copies, waits for them, and re-layouts: 19.6 us -> 12.2 us
    psum x1 -> x0, waiting for transfers between devices: 25.7 us -> none  [body(): lax.psum(g.astype(bf16), 'sp').astype(f32)]
    unnamed x77 -> x46, local copies, waits for them, and re-layouts: 16.4 us -> 4.85 us
    pallas_call x1, Pallas kernels: 16.3 us -> 25.3 us  [attend_back(): pl.pallas_call(functools.partial(bwd_kernel, parts), out_shape=(sds((rows...]
    convert_element_type x5 -> x2, other arithmetic: 10.8 us -> 3.16 us  [the longest x1 1.77 us: body(): g_down.reshape(576, 1024).astype(f32)]
    pallas_call x7, Pallas kernels: 140 us -> 146 us  [the longest x5 141 us: comm_call(): pl.pallas_call(kernel, out_shape=out_shape, in_specs=[first or vmem] + [v...]
    dot_general x3, matrix products: 5.51 us -> 2.34 us  [the longest x1 0.78 us: body(): jnp.einsum('tf,td->fd', d_up, normed_mid, preferred_element_type=f32)]
  transfers between devices with their start and end apart: 1 -> 0, of which waited for: 1 -> 0; matrix products, arithmetic and copies ran while one was open for 2% -> 0% of each run, Pallas kernels for 28% -> 0%
where the time goes in v2:
time: 209 us; the launch traced here: 208 us
  Pallas kernels  181 us (87%)
  local copies, waits for them, and re-layouts  12.2 us (6%)
  matrix products  10.3 us (5%)
  other arithmetic  3.83 us (2%)
    pallas_call x5, Pallas kernels, comm_call(): pl.pallas_call(kernel, out_shape=out_shape, in_specs=[first or vmem] + [v...  141 us
    pallas_call x1, Pallas kernels, attend_back(): pl.pallas_call(functools.partial(bwd_kernel, parts), out_shape=(sds((rows...  25.3 us
    pallas_call x1, Pallas kernels, attend(): pl.pallas_call(functools.partial(fwd_kernel, parts), out_shape=(sds((rows...  9.28 us
    pallas_call x2, Pallas kernels, local_call(): pl.pallas_call(kernel, out_shape=out_shape, in_specs=[first or vmem] + [v...  5.38 us
    unnamed x46, local copies, waits for them, and re-layouts  4.85 us

profile of v2, /device:TPU:1, one launch (start us, length us, event | category | flops | bytes accessed | tf_op | source)
XLA Modules:
  0.0 208.4 jit_solution(13517613706117851900)
XLA Ops:
  0.6 0.0 copy-start
  0.7 0.0 copy-start.19
  0.7 0.0 copy-start.9
  0.7 0.0 copy-start.11
  0.7 0.0 copy-start.12
  0.7 0.0 copy-start.13
  0.7 0.0 copy-start.15
  0.7 0.0 copy-start.16
  0.7 0.0 copy-start.17
  0.7 0.0 copy-start.18
  0.8 2.5 %fusion.3 = f32[512,576]{0,1:T(8,128)S(1)} fusion(bf16[512,1024]{1,0:T(8,128)(2,1)} %param.27, bf16[576,1024]{1,0:T(8,128)(2,1)} %param.26), kind=kOutput, calls=%fused_computation.19 | convolution fusion | flops 603979776 | bytes 3407872 | tf_op jit(solution)/shard_map/td,fd->tf/dot_general | solution.py:934
  3.3 0.0 copy-done.19
  3.3 0.1 jit_solution_.3.freq_ref
  3.4 0.0 copy-done.9
  3.4 0.0 copy-done.11
  3.4 0.0 copy-done.12
  3.4 0.0 copy-done.13
  3.4 0.0 copy-done.15
  3.4 0.0 copy-done.16
  3.4 0.0 copy-done.17
  3.4 0.0 copy-done.18
  3.5 2.9 %project.1 = (bf16[512,1024]{1,0:T(8,128)(2,1)S(1)}, f32[512,128]{1,0:T(8,128)S(1)}, f32[512,128]{1,0:T(8,128)S(1)}, bf16[512,128]{1,0:T(8,128)(2,1)S(1)}, bf16[...) custom-call(s32[4]{0:T(128)S(1)} %copy-done.16, bf16[512,1024]{1,0:T(8,128)(2,1)S(1)} %copy-done.9, ...), custom_call_target="tpu_custom_call" | custom-call | flops 3221225472 | bytes 16777216 | tf_op jit(solution)/shard_map/project/pallas_call | solution.py:894
  6.3 23.8 %gather_keys.1 = (bf16[2,256,128]{2,1,0:T(8,128)(2,1)S(1)}, bf16[4,4,2,256,128]{4,3,2,1,0:T(8,128)(2,1)S(1)}, bf16[8192,128]{1,0:T(8,128)(2,1)S(1)}) custom-call(s32[4]{0:T(128)S(1)} %copy-done.16, bf16[2,256,128]{2,1,0:T(8,128)(2,1)S(1)} %bitcast.117, bf16[2,256,128]{2,1,0:T(8,128)(2,1)S(1)} %bitcast.118), custom_call_target="tpu_custom_call" | custom-call | flops 8589934592 | bytes 33554432 | tf_op jit(solution)/shard_map/gather_keys/pallas_call | solution.py:742
  30.1 0.0 copy-start.10
  30.1 0.0 copy-start.14
  30.2 9.3 %attend.1 = (bf16[512,128]{1,0:T(8,128)(2,1)S(1)}, f32[512,128]{1,0:T(8,128)S(1)}, bf16[2,512,256]{2,1,0:T(8,128)(2,1)S(1)}) custom-call(s32[4]{0:T(128)S(1)} %copy-done.16, bf16[512,128]{1,0:T(8,128)(2,1)S(1)} %bitcast.120, bf16[8192,128]{1,0:T(8,128)(2,1)S(1)} %bitcast.100, bf16[8192,128]{1,0:T(8,128)(2,1)S(1)} %get-tuple-element.51.ext_ref), custom_call_target="tpu_custom_call" | custom-call | flops 3221225472 | bytes 4194304 | tf_op jit(solution)/shard_map/attend/pallas_call | solution.py:198
  39.4 0.0 copy-done.10
  39.4 0.0 copy-done.14
  39.4 0.0 copy-start.21
  39.5 28.4 %make_middle.1 = (bf16[8,64,1024]{2,1,0:T(8,128)(2,1)S(1)}, f32[64,1024]{1,0:T(8,128)S(1)}, bf16[2,256,128]{2,1,0:T(8,128)(2,1)S(1)}) custom-call(bf16[2,256,128]{2,1,0:T(8,128)(2,1)S(1)} %bitcast.121, bf16[128,1024]{1,0:T(8,128)(2,1)S(1)} %copy-done.10, bf16[8,64,1024]{2,1,0:T(8,128)(2,1)S(1)} %bitcast.86, f32[1,1024]{1,0:T(1,128)S(1)} %bitcast.92), custom_call_target="tpu_custom_call" | custom-call | flops 8589934592 | bytes 33554432 | tf_op jit(solution)/shard_map/make_middle/pallas_call | solution.py:742
  67.9 0.0 copy-done.21
  67.9 0.8 fusion.4
  68.7 0.0 copy-start.20
  68.7 1.3 multiply_convert_fusion
  70.0 0.0 copy-done.20
  70.0 0.0 copy-start.8
  70.0 1.0 convolution_convert_fusion.3
  71.0 0.2 copy-done.8
  71.2 0.8 convolution_convert_fusion
  72.0 0.8 convolution_convert_fusion.2
  72.8 0.8 convolution_convert_fusion.1
  73.6 1.0 fusion.5
  74.6 1.0 add_convert_fusion
  75.6 31.9 %turn_back.1 = (bf16[8,64,1024]{2,1,0:T(8,128)(2,1)S(1)}, bf16[8,64,1024]{2,1,0:T(8,128)(2,1)S(1)}, f32[64,1024]{1,0:T(8,128)S(1)}, f32[1,1024]{1,0:T(1,128)S(1)...) custom-call(bf16[8,64,1024]{2,1,0:T(8,128)(2,1)S(1)} %bitcast.112, ...), custom_call_target="tpu_custom_call" | custom-call | flops 8589934592 | bytes 33554432 | tf_op jit(solution)/shard_map/turn_back/pallas_call | solution.py:742
  107.5 0.0 copy-start.4
  107.5 1.0 copy-done.4
  108.5 25.3 %attend_back.1 = (bf16[512,128]{1,0:T(8,128)(2,1)S(1)}, bf16[8192,128]{1,0:T(8,128)(2,1)S(1)}, bf16[2,4,144,1024]{3,2,1,0:T(8,128)(2,1)S(1)}) custom-call(bf16[2,512,256]{2,1,0:T(8,128)(2,1)S(1)} %get-tuple-element.56.qa_ref, f32[512,128]{1,0:T(8,128)S(1)} %get-tuple-element.57.out_ref, bf16[512,128]{1,0:T(8,128)(2,1)S(1)} %bitcast.114, ...), custom_call_target="tpu_custom_call" | custom-call | flops 10737418240 | bytes 8388608 | tf_op jit(solution)/shard_map/attend_back/pallas_call | solution.py:212
  133.8 24.2 %scatter_keys.1 = (bf16[2,256,128]{2,1,0:T(8,128)(2,1)S(1)}, bf16[2,256,128]{2,1,0:T(8,128)(2,1)S(1)}) custom-call(bf16[4,4,2,256,128]{4,3,2,1,0:T(8,128)(2,1)S(1)} %bitcast.102, bf16[2,256,128]{2,1,0:T(8,128)(2,1)S(1)} %bitcast.119), custom_call_target="tpu_custom_call" | custom-call | flops 8589934592 | bytes 33554432 | tf_op jit(solution)/shard_map/scatter_keys/pallas_call | solution.py:742
  158.0 2.5 %project_back.1 = (bf16[512,1024]{1,0:T(8,128)(2,1)S(1)}, bf16[2,128,1024]{2,1,0:T(8,128)(2,1)S(1)}, f32[1,1024]{1,0:T(1,128)S(1)}) custom-call(bf16[512,128]{1,0:T(8,128)(2,1)S(1)} %bitcast.116, bf16[512,128]{1,0:T(8,128)(2,1)S(1)} %bitcast.115, f32[512,128]{1,0:T(8,128)S(1)} %get-tuple-element.64.qp_ref, f32[512,128]{1,0:T(8,128)S(1)} %get-tuple-element.65.kvp_ref, ...), custom_call_target="tpu_custom_call" | custom-call | flops 3221225472 | bytes 16777216 | tf_op jit(solution)/shard_map/project_back/pallas_call | solution.py:894
  160.5 0.3 convolution_convert_fusion.4
  160.8 32.9 %last_sums.1 = (bf16[8,64,1024]{2,1,0:T(8,128)(2,1)S(1)}, bf16[3,4,32,1024]{3,2,1,0:T(8,128)(2,1)S(1)}, bf16[1,4,144,1024]{3,2,1,0:T(8,128)(2,1)S(1)}, f32[8,1024]{1,0:T(8,128)S(1)}) custom-call(bf16[8,64,1024]{2,1,0:T(8,128)(2,1)S(1)} %bitcast.106, bf16[2,4,32,1024]{3,2,1,0:T(8,128)(2,1)S(1)} %bitcast.113, bf16[4,32,1024]{2,1,0:T(8,128)(2,1)S(1)} %bitcast.83, ...), custom_call_target="tpu_custom_call" | custom-call | flops 8589934592 | bytes 33554432 | tf_op jit(solution)/shard_map/last_sums/pallas_call | solution.py:742
  193.7 0.0 copy-start.2
  193.7 1.0 copy-done.2
  194.7 0.7 slice_bitcast_fusion.3
  195.4 0.6 fusion.2
  196.0 1.1 fusion.1
  197.1 2.0 copy.28
  199.1 1.4 convert_element_type.52
  200.5 0.8 slice_bitcast_fusion
  201.4 1.8 bitcast_convert_fusion
  203.1 2.7 %fusion = (f32[1,4,144,1024]{3,2,1,0:T(8,128)}, f32[1,4,144,1024]{3,2,1,0:T(8,128)}) fusion(bf16[2,4,144,1024]{3,2,1,0:T(8,128)(2,1)S(1)} %get-tuple-element.79), kind=kLoop, calls=%fused_computation.16 | loop fusion | bytes 9437184 | tf_op jit(solution)/shard_map/slice | solution.py:975
  205.9 1.0 copy.31
  206.8 0.6 copy-done.7
  207.4 1.0 copy.32
  (12 shorter events, 0.0 us)
Async XLA Ops:
  0.6 68.1 %copy-start = (bf16[1024,576]{0,1:T(8,128)(2,1)S(1)}, bf16[1024,576]{0,1:T(8,128)(2,1)}, u32[]{:S(2)}) copy-start(bf16[1024,576]{0,1:T(8,128)(2,1)} %param.25) | copy-start | bytes 3538948
  0.7 2.7 %copy-start.19 = (f32[32]{0:T(128)S(1)}, f32[32]{0:T(128)}, u32[]{:S(2)}) copy-start(f32[32]{0:T(128)} %constant.4.clone) | copy-start | bytes 388
  0.7 2.7 %copy-start.9 = (bf16[512,1024]{1,0:T(8,128)(2,1)S(1)}, bf16[512,1024]{1,0:T(8,128)(2,1)}, u32[]{:S(2)}) copy-start(bf16[512,1024]{1,0:T(8,128)(2,1)} %tok_ref.1) | copy-start | bytes 3145732
  0.7 2.7 %copy-start.11 = (bf16[1024,128]{1,0:T(8,128)(2,1)S(1)}, bf16[1024,128]{1,0:T(8,128)(2,1)}, u32[]{:S(2)}) copy-start(bf16[1024,128]{1,0:T(8,128)(2,1)} %wq_ref.3) | copy-start | bytes 786436
  0.7 2.7 %copy-start.12 = (bf16[1024,64]{0,1:T(8,128)(2,1)S(1)}, bf16[1024,64]{0,1:T(8,128)(2,1)}, u32[]{:S(2)}) copy-start(bf16[1024,64]{0,1:T(8,128)(2,1)} %param.18) | copy-start | bytes 393220
  0.7 2.7 %copy-start.13 = (bf16[1024,64]{0,1:T(8,128)(2,1)S(1)}, bf16[1024,64]{0,1:T(8,128)(2,1)}, u32[]{:S(2)}) copy-start(bf16[1024,64]{0,1:T(8,128)(2,1)} %param.19) | copy-start | bytes 393220
  0.7 2.7 %copy-start.15 = (f32[1024]{0:T(1024)S(1)}, f32[1024]{0:T(1024)}, u32[]{:S(2)}) copy-start(f32[1024]{0:T(1024)} %param.16) | copy-start | bytes 12292
  0.7 2.7 %copy-start.16 = (s32[4]{0:T(128)S(1)}, s32[4]{0:T(128)}, u32[]{:S(2)}) copy-start(s32[4]{0:T(128)} %len_ref.5) | copy-start | bytes 52
  0.7 2.7 %copy-start.17 = (f32[64]{0:T(128)S(1)}, f32[64]{0:T(128)}, u32[]{:S(2)}) copy-start(f32[64]{0:T(128)} %param.20) | copy-start | bytes 772
  0.7 2.7 %copy-start.18 = (f32[64]{0:T(128)S(1)}, f32[64]{0:T(128)}, u32[]{:S(2)}) copy-start(f32[64]{0:T(128)} %param.21) | copy-start | bytes 772
  30.1 9.3 %copy-start.10 = (bf16[128,1024]{1,0:T(8,128)(2,1)S(1)}, bf16[128,1024]{1,0:T(8,128)(2,1)}, u32[]{:S(2)}) copy-start(bf16[128,1024]{1,0:T(8,128)(2,1)} %w_ref.3) | copy-start | bytes 786436
  30.1 9.3 %copy-start.14 = (f32[1024]{0:T(1024)S(1)}, f32[1024]{0:T(1024)}, u32[]{:S(2)}) copy-start(f32[1024]{0:T(1024)} %param.23) | copy-start | bytes 12292
  39.4 28.4 %copy-start.21 = (bf16[1024,576]{0,1:T(8,128)(2,1)S(1)}, bf16[1024,576]{0,1:T(8,128)(2,1)}, u32[]{:S(2)}) copy-start(bf16[1024,576]{0,1:T(8,128)(2,1)} %param.24) | copy-start | bytes 3538948
  68.7 1.3 copy-start.20
  70.0 1.2 copy-start.8
  107.5 1.0 copy-start.4
  193.7 1.0 copy-start.2
  194.7 1.3 copy-start.1
  194.7 2.4 %copy-start.6 = (bf16[8,64,1024]{2,1,0:T(8,128)(2,1)}, bf16[8,64,1024]{2,1,0:T(8,128)(2,1)S(1)}, u32[]{:S(2)}) copy-start(bf16[8,64,1024]{2,1,0:T(8,128)(2,1)S(1)} %get-tuple-element.76) | copy-start | bytes 3145732
  199.1 2.3 %copy-start.3 = (bf16[1,4,144,1024]{3,2,1,0:T(8,128)(2,1)S(1)}, bf16[1,4,144,1024]{3,2,1,0:T(8,128)(2,1)}, u32[]{:S(2)}) copy-start(bf16[1,4,144,1024]{3,2,1,0:T(8,128)(2,1)} %copy-done.2) | copy-start | bytes 3538948
  203.1 2.7 %copy-start.5 = (bf16[8,64,1024]{2,1,0:T(8,128)(2,1)S(1)}, bf16[8,64,1024]{2,1,0:T(8,128)(2,1)}, u32[]{:S(2)}) copy-start(bf16[8,64,1024]{2,1,0:T(8,128)(2,1)} %copy-done.4) | copy-start | bytes 3145732
  205.8 1.6 copy-start.7

commit v3 on v2

--- a/solution.py
+++ b/solution.py
@@ -14,6 +14,7 @@
 CH = 512
 HALF = 256
 SCALE = 0.125
+EARLY = 4
 C2 = SCALE * math.log2(math.e)
 
 
@@ -130,15 +131,18 @@
     p = Place()
     meet([p.along_x(d) for d in ORDER] + [p.along_y(d) for d in ORDER])
     spread = SpGather(p, grads_ref, 144, sems)
-    for i in range(2):
+    for i in range(3):
         for h in range(2):
             spread.put(i, h, red_ref[i, h])
             spread.first(i, h)
     lane = lanes((HALF, 128))
     acc_ref[...] = jnp.zeros_like(acc_ref)
-    for t in range(2):
-        r0 = tile_row(me, t, parts)
-        rows_t = slice(t * HALF, (t + 1) * HALF)
+    upper_long = (me < parts // 2).astype(jnp.int32)
+    for turn in range(2):
+        t = upper_long if turn == 0 else 1 - upper_long
+        block = me + t * (parts - 1 - 2 * me)
+        r0 = block * 512 + t * HALF
+        rows_t = pl.ds(pl.multiple_of(t * HALF, HALF), HALF)
         do = do_ref[rows_t, :].astype(f32)
         prod = do * out_ref[rows_t, :]
         d0 = -jnp.sum(jnp.where(lane < 64, prod, 0.0), axis=1, keepdims=True)
@@ -149,7 +153,7 @@
         da_ref[HALF:, 128:256] = split3(jnp.broadcast_to(d1, (HALF, 128)), lane).astype(bf16)
         dqt_ref[...] = jnp.zeros_like(dqt_ref)
 
-        def step(c, masked):
+        def step(c, masked, t=t, r0=r0):
             k0 = pl.multiple_of(c * CH, CH)
             kv = kv_ref[pl.ds(k0, CH), :]
             kva = jnp.concatenate([kv, ext_ref[pl.ds(k0, CH), :]], axis=1)
@@ -169,14 +173,16 @@
             kt = kv.T[0:64, :]
             dqt_ref[...] += jnp.dot(kt, ds, preferred_element_type=f32)
 
-        block = me if t == 0 else parts - 1 - me
-        pl.loop(0, block)(lambda c: step(c, False))
+        if turn == 0:
+            pl.loop(0, EARLY)(lambda c: step(c, False))
+            for i in range(3):
+                for h in range(2):
+                    spread.second(i, h)
+            pl.loop(EARLY, block)(lambda c: step(c, False))
+        else:
+            pl.loop(0, block)(lambda c: step(c, False))
         step(block, True)
         dqt = dqt_ref[...]
-        if t == 0:
-            for i in range(2):
-                for h in range(2):
-                    spread.second(i, h)
         both = jnp.concatenate([dqt[:, :HALF], dqt[:, HALF:]], axis=0)
         dq_ref[rows_t, :] = (both.T * SCALE).astype(bf16)
     weight = jnp.where(lanes((512, 128)) < 64, SCALE, 1.0)
@@ -211,11 +217,11 @@
     rows = 2 * HALF
     return pl.pallas_call(
         functools.partial(bwd_kernel, parts),
-        out_shape=(sds((rows, 128), bf16), sds(kv.shape, bf16), sds((2, 4, 144, 1024), bf16)),
+        out_shape=(sds((rows, 128), bf16), sds(kv.shape, bf16), sds((3, 4, 144, 1024), bf16)),
         in_specs=[vmem] * 6,
         out_specs=(vmem, vmem, vmem),
         scratch_shapes=[pltpu.VMEM((rows, 256), bf16), pltpu.VMEM(kv.shape, f32), pltpu.VMEM((64, rows), f32)]
-        + SpGather.sems(2),
+        + SpGather.sems(3),
         compiler_params=pltpu.CompilerParams(collective_id=6, has_side_effects=True, vmem_limit_bytes=20 << 20),
         cost_estimate=pl.CostEstimate(flops=10 << 30, bytes_accessed=8 << 20, transcendentals=5 << 20),
         name="attend_back",
@@ -321,48 +327,6 @@
         copy.wait_send()
     for copy in second.values():
         copy.wait()
-
-
-def scatter_kernel(dkv_ref, dqz_ref, own_ref, dq_ref, r1, send, r2, ms, mr, fs, fr, ss, sr):
-    p = Place()
-    meet([p.along_x(d) for d in ORDER] + [p.along_y(d) for d in ORDER] + [p.mirror])
-    first, second = {}, {}
-    for d in ORDER:
-        for h in range(2):
-            to = lax.rem(p.fsp(h) + d, 4)
-            src = dkv_ref.at[to, :, 0] if h == 0 else dkv_ref.at[:, to, 1]
-            first[h, d] = rcopy(src, r1.at[h, d - 1], fs.at[h, d - 1], fr.at[h, d - 1], p.first(h, d))
-            first[h, d].start()
-    mirror = rcopy(dqz_ref.at[1], dq_ref.at[1], ms, mr, p.mirror)
-    mirror.start()
-    dq_ref[0] = dqz_ref[0]
-
-    def total(h, b):
-        at = spot(h, p.fsp(h), b)
-        value = dkv_ref[at[0], at[1], h].astype(f32)
-        for d in range(3):
-            value = value + r1[h, d, b].astype(f32)
-        return value
-
-    for h in range(2):
-        for d in ORDER:
-            first[h, d].wait_recv()
-        for e in ORDER:
-            b = lax.rem(p.ssp(h) + e, 4)
-            send[h, e - 1] = total(h, b).astype(bf16)
-            second[h, e] = rcopy(
-                send.at[h, e - 1], r2.at[h, e - 1], ss.at[h, e - 1], sr.at[h, e - 1], p.second(h, e)
-            )
-            second[h, e].start()
-    for h in range(2):
-        value = total(h, p.ssp(h))
-        for e in ORDER:
-            second[h, e].wait_recv()
-            value = value + r2[h, e - 1].astype(f32)
-        own_ref[h] = value.astype(bf16)
-    mirror.wait()
-    for copy in list(first.values()) + list(second.values()):
-        copy.wait_send()
 
 
 class SpScatter:
@@ -577,6 +541,61 @@
 
 def wt_peers(p):
     return [p.sibling] + [p.along_z(d) for d in ORDER]
+
+
+def scatter_kernel(dkv_ref, dqz_ref, mlp_ref, mid_ref, own_ref, dq_ref, out_ref, r1, send, r2, ms, mr, fs, fr, ss, sr,
+                   sib, sendz, rz, cs, cr, zs, zr, az, bz, ag, bg):
+    p = Place()
+    meet(wt_peers(p) + [p.along_x(d) for d in ORDER] + [p.along_y(d) for d in ORDER] + [p.mirror])
+    first, second = {}, {}
+    for d in ORDER:
+        for h in range(2):
+            to = lax.rem(p.fsp(h) + d, 4)
+            src = dkv_ref.at[to, :, 0] if h == 0 else dkv_ref.at[:, to, 1]
+            first[h, d] = rcopy(src, r1.at[h, d - 1], fs.at[h, d - 1], fr.at[h, d - 1], p.first(h, d))
+            first[h, d].start()
+    down = WtSum(p, mlp_ref, sib, sendz, rz, (cs, cr, zs, zr))
+    for zz in range(4):
+        down.start_core(zz)
+    mirror = rcopy(dqz_ref.at[1], dq_ref.at[1], ms, mr, p.mirror)
+    mirror.start()
+    dq_ref[0] = dqz_ref[0]
+    for d in ORDER:
+        down.send_z(d)
+
+    def total(h, b):
+        at = spot(h, p.fsp(h), b)
+        value = dkv_ref[at[0], at[1], h].astype(f32)
+        for d in range(3):
+            value = value + r1[h, d, b].astype(f32)
+        return value
+
+    out_ref[p.wt] = (mid_ref[...] + down.own()).astype(bf16)
+    spread = WtGather(p, out_ref, (az, bz, ag, bg))
+    spread.start()
+    for h in range(2):
+        for d in ORDER:
+            first[h, d].wait_recv()
+        for e in ORDER:
+            b = lax.rem(p.ssp(h) + e, 4)
+            send[h, e - 1] = total(h, b).astype(bf16)
+            second[h, e] = rcopy(
+                send.at[h, e - 1], r2.at[h, e - 1], ss.at[h, e - 1], sr.at[h, e - 1], p.second(h, e)
+            )
+            second[h, e].start()
+    spread.forward()
+    for h in range(2):
+        value = total(h, p.ssp(h))
+        for e in ORDER:
+            second[h, e].wait_recv()
+            value = value + r2[h, e - 1].astype(f32)
+        own_ref[h] = value.astype(bf16)
+    mirror.wait()
+    spread.arrived()
+    spread.finish()
+    down.finish()
+    for copy in list(first.values()) + list(second.values()):
+        copy.wait_send()
 
 
 def middle_kernel(mix_ref, w_ref, tok_ref, gain_ref, nm_ref, mid_ref, mixo_ref, part, sib, send, rz, ms, mr, cs, cr, zs, zr, az, bz, ag, bg):
@@ -606,42 +625,31 @@
     total.finish()
 
 
-def turn_kernel(dm_ref, mlp_ref, mid_ref, cot_ref, gain_ref, w_ref, g0_ref, g1_ref, g2_ref,
-                out_ref, da_ref, dmid_ref, gn_ref, dz_ref, red_ref,
+def turn_kernel(dm_ref, mid_ref, cot_ref, gain_ref, w_ref, g0_ref, g1_ref, g2_ref,
+                da_ref, dmid_ref, gn_ref, dz_ref, red_ref,
                 up, sib, send, rz, ms, mr, cs, cr, zs, zr, az, bz, ag, bg, *grad_refs):
     p = Place()
     meet(wt_peers(p) + [p.mirror] + [p.along_x(d) for d in ORDER] + [p.along_y(d) for d in ORDER])
-    totals = [
-        WtSum(p, ref, sib.at[i], send.at[i], rz.at[i], (cs.at[i], cr.at[i], zs.at[i], zr.at[i]))
-        for i, ref in enumerate((dm_ref, mlp_ref))
-    ]
+    total = WtSum(p, dm_ref, sib, send, rz, (cs, cr, zs, zr))
     grads = SpScatter(p, (g0_ref, g1_ref, g2_ref), 144, grad_refs)
     for zz in range(4):
-        totals[0].start_core(zz)
+        total.start_core(zz)
     for i in range(3):
         grads.first(i)
-    for zz in range(4):
-        totals[1].start_core(zz)
-    for total in totals:
-        for d in ORDER:
-            total.send_z(d)
+    for d in ORDER:
+        total.send_z(d)
     middle = mid_ref[...]
     scale = rms_of(middle)
-    d_mid = totals[0].own()
+    d_mid = total.own()
     gn_ref[...] = jnp.sum(d_mid * middle * scale, axis=0, keepdims=True)
     d_middle = cot_ref[p.wt].astype(f32) + norm_back(middle, scale, gain_ref[...], d_mid)
     dmid_ref[...] = d_middle
     da_ref[p.wt] = d_middle.astype(bf16)
-    spreads = [
-        WtGather(p, ref, (az.at[i], bz.at[i], ag.at[i], bg.at[i])) for i, ref in enumerate((da_ref, out_ref))
-    ]
-    spreads[0].start()
+    spread = WtGather(p, da_ref, (az, bz, ag, bg))
+    spread.start()
     grads.second(0)
-    out_ref[p.wt] = (middle + totals[1].own()).astype(bf16)
-    spreads[1].start()
-    grads.second(1)
-    spreads[0].forward()
-    spreads[0].arrived()
+    spread.forward()
+    spread.arrived()
     mirror = rcopy(up, dz_ref.at[1], ms, mr, p.mirror)
     for half in (1, 0):
         rows = da_ref[half * 4:half * 4 + 4].reshape(256, 1024)
@@ -651,19 +659,18 @@
             mirror.start()
         else:
             dz_ref[0] = d_mixed
+    grads.second(1)
     grads.second(2)
-    spreads[1].forward()
     for i in range(3):
         for h in range(2):
             red_ref[i, h] = grads.own(i, h).astype(bf16)
-    spreads[1].arrived()
     mirror.wait()
-    for part in spreads + totals + [grads]:
+    for part in (spread, total, grads):
         part.finish()
 
 
-def last_kernel(dn_ref, gq_ref, go_ref, red_ref, tok_ref, dmid_ref, gain_ref, gn_ref, gg_ref,
-                gt_ref, sums_ref, gd_ref, vec_ref,
+def last_kernel(dn_ref, gq_ref, go_ref, tok_ref, dmid_ref, gain_ref, gn_ref, gg_ref,
+                gt_ref, sums_ref, vec_ref,
                 sib, send, rz, cs, cr, zs, zr, az, bz, ag, bg,
                 vw, vx, vy, vs1, vr1, vs2, vr2, vs3, vr3, *more):
     p = Place()
@@ -673,10 +680,6 @@
         total.start_core(zz)
     grads = SpScatter(p, (gq_ref.at[0], gq_ref.at[1], go_ref), 32, more[:8])
     back = SpGather(p, sums_ref, 32, more[8:12])
-    down = SpGather(p, gd_ref, 144, more[12:16])
-    for h in range(2):
-        down.put(0, h, red_ref[h])
-        down.first(0, h)
     for i in range(3):
         grads.first(i)
     for d in ORDER:
@@ -719,8 +722,6 @@
             back.first(i, h)
     vx[0] = vec_total(vw, round1)
     round2 = vec_round(vx, [p.along_x(d) for d in ORDER], vs2, vr2)
-    for h in range(2):
-        down.second(0, h)
     for i in range(3):
         for h in range(2):
             back.second(i, h)
@@ -733,9 +734,11 @@
     total.finish()
     grads.finish()
     back.finish()
-    down.finish()
     for copy in round1 + round2 + round3:
         copy.wait_send()
+
+
+WT_SEMS = [DMA((4,)), DMA((4,)), DMA((3,)), DMA((3,)), DMA((3,)), DMA((3,)), DMA((4,)), DMA((4,))]
 
 
 def comm_call(kernel, number, out_shape, args, scratch, name, limit=10, first=None):
@@ -763,13 +766,14 @@
     )
 
 
-def scatter_keys(dkv, dq):
+def scatter_keys(dkv, dq, mlp, mid):
     return comm_call(
         scatter_kernel, 2,
-        (sds((2, 256, 128), bf16), sds((2, 256, 128), bf16)),
-        (dkv.reshape(4, 4, 2, 256, 128), dq.reshape(2, 256, 128)),
+        (sds((2, 256, 128), bf16), sds((2, 256, 128), bf16), sds((8, 64, 1024), bf16)),
+        (dkv.reshape(4, 4, 2, 256, 128), dq.reshape(2, 256, 128), mlp.reshape(8, 64, 1024), mid),
         [pltpu.VMEM((2, 3, 4, 256, 128), bf16), pltpu.VMEM((2, 3, 256, 128), bf16), pltpu.VMEM((2, 3, 256, 128), bf16),
-         DMA, DMA, DMA((2, 3)), DMA((2, 3)), DMA((2, 3)), DMA((2, 3))],
+         DMA, DMA, DMA((2, 3)), DMA((2, 3)), DMA((2, 3)), DMA((2, 3)),
+         pltpu.VMEM((4, 64, 1024), bf16), pltpu.VMEM((3, 64, 1024), bf16), pltpu.VMEM((3, 64, 1024), bf16)] + WT_SEMS,
         "scatter_keys",
     )
 
@@ -786,33 +790,33 @@
     )
 
 
-def turn_back(dm, mlp, mid, cot, gain, w_out, grads):
+def turn_back(dm, mid, cot, gain, w_out, grads):
     rows = pltpu.VMEM
     return comm_call(
         turn_kernel, 4,
-        (sds((8, 64, 1024), bf16), sds((8, 64, 1024), bf16), sds((64, 1024), f32), sds((1, 1024), f32),
+        (sds((8, 64, 1024), bf16), sds((64, 1024), f32), sds((1, 1024), f32),
          sds((2, 256, 128), bf16), sds((3, 2, 144, 128), bf16)),
-        (dm.reshape(8, 64, 1024), mlp.reshape(8, 64, 1024), mid, cot.reshape(8, 64, 1024), gain.reshape(1, 1024), w_out)
+        (dm.reshape(8, 64, 1024), mid, cot.reshape(8, 64, 1024), gain.reshape(1, 1024), w_out)
         + tuple(g.reshape(4, 144, 1024) for g in grads),
-        [rows((256, 128), bf16), rows((2, 4, 64, 1024), bf16), rows((2, 3, 64, 1024), bf16), rows((2, 3, 64, 1024), bf16),
-         DMA, DMA, DMA((2, 4)), DMA((2, 4)), DMA((2, 3)), DMA((2, 3)), DMA((2, 3)), DMA((2, 3)), DMA((2, 4)), DMA((2, 4))]
+        [rows((256, 128), bf16), rows((4, 64, 1024), bf16), rows((3, 64, 1024), bf16), rows((3, 64, 1024), bf16),
+         DMA, DMA] + WT_SEMS
         + SpScatter.scratch(3, 144),
         "turn_back", 16,
     )
 
 
-def last_sums(dn, gq, go, red, tokens, dmid, gain, gn, gg):
+def last_sums(dn, gq, go, tokens, dmid, gain, gn, gg):
     rows = pltpu.VMEM
     return comm_call(
         last_kernel, 5,
-        (sds((8, 64, 1024), bf16), sds((3, 4, 32, 1024), bf16), sds((1, 4, 144, 1024), bf16), sds((8, 1024), f32)),
-        (dn.reshape(8, 64, 1024), gq.reshape(2, 4, 32, 1024), go.reshape(4, 32, 1024), red, tokens.reshape(8, 64, 1024),
+        (sds((8, 64, 1024), bf16), sds((3, 4, 32, 1024), bf16), sds((8, 1024), f32)),
+        (dn.reshape(8, 64, 1024), gq.reshape(2, 4, 32, 1024), go.reshape(4, 32, 1024), tokens.reshape(8, 64, 1024),
          dmid, gain.reshape(1, 1024), gn, gg),
         [rows((4, 64, 1024), bf16), rows((3, 64, 1024), bf16), rows((3, 64, 1024), bf16),
          DMA((4,)), DMA((4,)), DMA((3,)), DMA((3,)), DMA((3,)), DMA((3,)), DMA((4,)), DMA((4,)),
          rows((8, 8, 1024), f32), rows((4, 8, 1024), f32), rows((4, 8, 1024), f32),
          DMA((7,)), DMA((7,)), DMA((3,)), DMA((3,)), DMA((3,)), DMA((3,))]
-        + SpScatter.scratch(3, 32) + SpGather.sems(3) + SpGather.sems(1),
+        + SpScatter.scratch(3, 32) + SpGather.sems(3),
         "last_sums", 10,
     )
 
@@ -902,6 +906,51 @@
     )(*args)
 
 
+def finish_kernel(sums_ref, ff_ref, out_in, gt_in, vec_ref, out_ref, gt_ref, gq_ref, gk_ref, gv_ref, go_ref, gg_ref, gu_ref, gd_ref,
+                  ni_ref, nm_ref, qg_ref, kg_ref, wide, tall, big, sems):
+    copies = []
+
+    def write(src, dst):
+        copies.append(pltpu.make_async_copy(src, dst, sems.at[len(copies)]))
+        copies[-1].start()
+
+    write(out_in, out_ref)
+    write(gt_in, gt_ref)
+    for i, ref in enumerate((gg_ref, gu_ref, gd_ref)):
+        for part in range(2):
+            rows = pl.ds(part * 288, 288)
+            big[i, rows, :] = ff_ref[i, rows, :].astype(f32)
+            write(big.at[i, rows], ref.at[rows])
+    wide[...] = sums_ref[1:3].astype(f32)
+    write(wide.at[0, 0:64], gk_ref)
+    write(wide.at[0, 64:128], gv_ref)
+    write(wide.at[1], go_ref)
+    tall[...] = sums_ref[0].astype(f32).T
+    write(tall, gq_ref)
+    ni_ref[...] = vec_ref[0:1, :]
+    nm_ref[...] = vec_ref[1:2, :]
+    qg_ref[...] = vec_ref[2:3, 0:64] + vec_ref[2:3, 64:128]
+    kg_ref[...] = vec_ref[2:3, 128:192]
+    for copy in copies:
+        copy.wait()
+
+
+def finish(sums, ff, output, grad_tokens, vec):
+    hbm = pl.BlockSpec(memory_space=pl.ANY)
+    rows = sds((576, 1024), f32)
+    return pl.pallas_call(
+        finish_kernel,
+        out_shape=(sds((512, 1024), bf16), sds((512, 1024), bf16), sds((1024, 128), f32), sds((64, 1024), f32), sds((64, 1024), f32),
+                   sds((128, 1024), f32), rows, rows, rows,
+                   sds((1, 1024), f32), sds((1, 1024), f32), sds((1, 64), f32), sds((1, 64), f32)),
+        in_specs=[vmem] * 5,
+        out_specs=tuple([hbm] * 9 + [vmem] * 4),
+        scratch_shapes=[pltpu.VMEM((2, 128, 1024), f32), pltpu.VMEM((1024, 128), f32), pltpu.VMEM((3, 576, 1024), f32), DMA((12,))],
+        compiler_params=pltpu.CompilerParams(vmem_limit_bytes=14 << 20),
+        name="finish",
+    )(sums, ff, output, grad_tokens, vec)
+
+
 theta = 1000000.0
 
 
@@ -943,37 +992,25 @@
         jnp.einsum("tf,td->fd", d_up, normed_mid, preferred_element_type=f32).astype(bf16),
         jnp.einsum("tf,td->fd", act, cotangent, preferred_element_type=f32).astype(bf16),
     )
-    output, d_attn, d_middle_own, gn, d_mix_z, red = turn_back(
-        d_mid_part, mlp_part, mid_own, cotangent, norm_mid, w_out, grads
+    d_attn, d_middle_own, gn, d_mix_z, red = turn_back(
+        d_mid_part, mid_own, cotangent, norm_mid, w_out, grads
     )
     g_out = jnp.einsum("tq,td->qd", mixed, d_attn.reshape(512, 1024), preferred_element_type=f32).astype(bf16)
-    dq_z, dkv_all, g_ff = attend_back(parts, qa, mix_f, d_mix_z.reshape(512, 128), kv_all, ext, red[:2])
-    dkv, dq = scatter_keys(dkv_all, dq_z)
+    dq_z, dkv_all, g_ff = attend_back(parts, qa, mix_f, d_mix_z.reshape(512, 128), kv_all, ext, red)
+    dkv, dq, output = scatter_keys(dkv_all, dq_z, mlp_part, mid_own)
     dn_part, g_qkv, gg = local_call(
         proj_back_kernel,
         (sds((512, 1024), bf16), sds((2, 128, 1024), bf16), sds((1, 1024), f32)),
         (dq.reshape(512, 128), dkv.reshape(512, 128), q_proj, kv_proj, normed, w_query, wk, wv, qg, kg, cosine, sine),
         "project_back",
     )
-    grad_tokens, sums, g_down, vec = last_sums(
-        dn_part, g_qkv, g_out, red[2], tokens, d_middle_own, norm_in, gn, gg
-    )
-    sums = sums.reshape(3, 128, 1024).astype(f32)
-    g_ff = g_ff.reshape(2, 576, 1024).astype(f32)
+    grad_tokens, sums, vec = last_sums(dn_part, g_qkv, g_out, tokens, d_middle_own, norm_in, gn, gg)
+    (output, grad_tokens, g_query, g_key, g_value, g_out, g_gate, g_up, g_down, g_norm_in, g_norm_mid, g_qg, g_kg) = finish(
+        sums.reshape(3, 128, 1024), g_ff.reshape(3, 576, 1024), output.reshape(512, 1024), grad_tokens.reshape(512, 1024), vec
+    )
     return (
-        output.reshape(512, 1024),
-        grad_tokens.reshape(512, 1024),
-        vec[0],
-        sums[0].T,
-        sums[1, :64].T,
-        sums[1, 64:].T,
-        vec[2, :64] + vec[2, 64:128],
-        vec[2, 128:192],
-        sums[2],
-        vec[1],
-        g_ff[0].T,
-        g_ff[1].T,
-        g_down.reshape(576, 1024).astype(f32),
+        output, grad_tokens, g_norm_in.reshape(1024), g_query, g_key.T, g_value.T, g_qg.reshape(64), g_kg.reshape(64),
+        g_out, g_norm_mid.reshape(1024), g_gate.T, g_up.T, g_down,
     )
 
 

time: 209 us -> 188 us (0.90)
  local copies, waits for them, and re-layouts: 12.2 us -> 0.39 us
  Pallas kernels: 181 us -> 176 us
  other arithmetic: 3.83 us -> 0 us
    pallas_call x5, Pallas kernels: 141 us -> 129 us  [comm_call(): pl.pallas_call(kernel, out_shape=out_shape, in_specs=[first or vmem] + [v...]
    pallas_call x0 -> x1, Pallas kernels: none -> 4.72 us  [finish(): pl.pallas_call(finish_kernel, out_shape=(sds((512, 1024), bf16), sds((512...]
    unnamed x46 -> x30, local copies, waits for them, and re-layouts: 4.85 us -> 0.32 us
    slice x4 -> x0, local copies, waits for them, and re-layouts: 4.41 us -> none  [the longest x1 2.71 us: body(): g_ff[1]]
    convert_element_type x2 -> x0, other arithmetic: 3.16 us -> none  [the longest x1 1.77 us: body(): g_down.reshape(576, 1024).astype(f32)]
    pallas_call x1, Pallas kernels: 25.3 us -> 27.9 us  [attend_back(): pl.pallas_call(functools.partial(bwd_kernel, parts), out_shape=(sds((rows...]
where the time goes in v3:
time: 188 us
  Pallas kernels  176 us (94%)
  matrix products  10.3 us (5%)
    pallas_call x5, Pallas kernels, comm_call(): pl.pallas_call(kernel, out_shape=out_shape, in_specs=[first or vmem] + [v...  129 us
    pallas_call x1, Pallas kernels, attend_back(): pl.pallas_call(functools.partial(bwd_kernel, parts), out_shape=(sds((rows...  27.9 us
    pallas_call x1, Pallas kernels, attend(): pl.pallas_call(functools.partial(fwd_kernel, parts), out_shape=(sds((rows...  9.28 us
    pallas_call x2, Pallas kernels, local_call(): pl.pallas_call(kernel, out_shape=out_shape, in_specs=[first or vmem] + [v...  5.39 us
    pallas_call x1, Pallas kernels, finish(): pl.pallas_call(finish_kernel, out_shape=(sds((512, 1024), bf16), sds((512...  4.72 us

profile of v3, /device:TPU:1, one launch (start us, length us, event | category | flops | bytes accessed | tf_op | source)
XLA Modules:
  0.0 187.9 jit_solution(10637407029839153501)
XLA Ops:
  0.6 0.0 copy-start
  0.7 0.0 copy-start.12
  0.7 0.0 copy-start.2
  0.7 0.0 copy-start.4
  0.7 0.0 copy-start.5
  0.7 0.0 copy-start.6
  0.7 0.0 copy-start.8
  0.7 0.0 copy-start.9
  0.7 0.0 copy-start.10
  0.7 0.0 copy-start.11
  0.8 2.5 %fusion = f32[512,576]{0,1:T(8,128)S(1)} fusion(bf16[512,1024]{1,0:T(8,128)(2,1)} %param.27, bf16[576,1024]{1,0:T(8,128)(2,1)} %param.26), kind=kOutput, calls=%fused_computation.10 | convolution fusion | flops 603979776 | bytes 3407872 | tf_op jit(solution)/shard_map/td,fd->tf/dot_general | solution.py:983
  3.3 0.0 copy-done.12
  3.3 0.1 jit_solution_.3.freq_ref
  3.4 0.0 copy-done.2
  3.4 0.0 copy-done.4
  3.4 0.0 copy-done.5
  3.4 0.0 copy-done.6
  3.4 0.0 copy-done.8
  3.4 0.0 copy-done.9
  3.4 0.0 copy-done.10
  3.4 0.0 copy-done.11
  3.5 2.9 %project.1 = (bf16[512,1024]{1,0:T(8,128)(2,1)S(1)}, f32[512,128]{1,0:T(8,128)S(1)}, f32[512,128]{1,0:T(8,128)S(1)}, bf16[512,128]{1,0:T(8,128)(2,1)S(1)}, bf16[...) custom-call(s32[4]{0:T(128)S(1)} %copy-done.9, bf16[512,1024]{1,0:T(8,128)(2,1)S(1)} %copy-done.2, ...), custom_call_target="tpu_custom_call" | custom-call | flops 3221225472 | bytes 16777216 | tf_op jit(solution)/shard_map/project/pallas_call | solution.py:898
  6.3 23.8 %gather_keys.1 = (bf16[2,256,128]{2,1,0:T(8,128)(2,1)S(1)}, bf16[4,4,2,256,128]{4,3,2,1,0:T(8,128)(2,1)S(1)}, bf16[8192,128]{1,0:T(8,128)(2,1)S(1)}) custom-call(s32[4]{0:T(128)S(1)} %copy-done.9, bf16[2,256,128]{2,1,0:T(8,128)(2,1)S(1)} %bitcast.101, bf16[2,256,128]{2,1,0:T(8,128)(2,1)S(1)} %bitcast.102), custom_call_target="tpu_custom_call" | custom-call | flops 8589934592 | bytes 33554432 | tf_op jit(solution)/shard_map/gather_keys/pallas_call | solution.py:745
  30.2 0.0 copy-start.3
  30.2 0.0 copy-start.7
  30.2 9.3 %attend.1 = (bf16[512,128]{1,0:T(8,128)(2,1)S(1)}, f32[512,128]{1,0:T(8,128)S(1)}, bf16[2,512,256]{2,1,0:T(8,128)(2,1)S(1)}) custom-call(s32[4]{0:T(128)S(1)} %copy-done.9, bf16[512,128]{1,0:T(8,128)(2,1)S(1)} %bitcast.103, bf16[8192,128]{1,0:T(8,128)(2,1)S(1)} %bitcast.83, bf16[8192,128]{1,0:T(8,128)(2,1)S(1)} %get-tuple-element.63.ext_ref), custom_call_target="tpu_custom_call" | custom-call | flops 3221225472 | bytes 4194304 | tf_op jit(solution)/shard_map/attend/pallas_call | solution.py:204
  39.5 0.0 copy-done.3
  39.5 0.0 copy-done.7
  39.5 0.0 copy-start.14
  39.5 28.4 %make_middle.1 = (bf16[8,64,1024]{2,1,0:T(8,128)(2,1)S(1)}, f32[64,1024]{1,0:T(8,128)S(1)}, bf16[2,256,128]{2,1,0:T(8,128)(2,1)S(1)}) custom-call(bf16[2,256,128]{2,1,0:T(8,128)(2,1)S(1)} %bitcast.104, bf16[128,1024]{1,0:T(8,128)(2,1)S(1)} %copy-done.3, bf16[8,64,1024]{2,1,0:T(8,128)(2,1)S(1)} %bitcast.69, f32[1,1024]{1,0:T(1,128)S(1)} %bitcast.75), custom_call_target="tpu_custom_call" | custom-call | flops 8589934592 | bytes 33554432 | tf_op jit(solution)/shard_map/make_middle/pallas_call | solution.py:745
  67.9 0.0 copy-done.14
  67.9 0.8 fusion.1
  68.7 0.0 copy-done
  68.7 0.0 copy-start.13
  68.7 1.2 multiply_convert_fusion
  70.0 0.0 copy-done.13
  70.0 0.0 copy-start.1
  70.0 1.0 convolution_convert_fusion.3
  71.0 0.2 copy-done.1
  71.2 0.8 convolution_convert_fusion
  72.0 0.8 convolution_convert_fusion.2
  72.8 0.8 convolution_convert_fusion.1
  73.6 1.0 fusion.2
  74.6 1.0 add_convert_fusion
  75.6 30.5 %turn_back.1 = (bf16[8,64,1024]{2,1,0:T(8,128)(2,1)S(1)}, f32[64,1024]{1,0:T(8,128)S(1)}, f32[1,1024]{1,0:T(1,128)S(1)}, bf16[2,256,128]{2,1,0:T(8,128)(2,1)S(1)}, bf16[3,2,144,128]{3,2,1,0:T(8,128)(2,1)S(1)}) custom-call(bf16[8,64,1024]{2,1,0:T(8,128)(2,1)S(1)} %bitcast.95, f32[64,1024]{1,0:T(8,128)S(1)} %get-tuple-element.68.mid_ref, ...), custom_call_target="tpu_custom_call" | custom-call | flops 8589934592 | bytes 33554432 | tf_op jit(solution)/shard_map/turn_back/pallas_call | solution.py:745
  106.1 0.3 convolution_convert_fusion.4
  106.5 27.9 %attend_back.1 = (bf16[512,128]{1,0:T(8,128)(2,1)S(1)}, bf16[8192,128]{1,0:T(8,128)(2,1)S(1)}, bf16[3,4,144,1024]{3,2,1,0:T(8,128)(2,1)S(1)}) custom-call(bf16[2,512,256]{2,1,0:T(8,128)(2,1)S(1)} %get-tuple-element.64.qa_ref, f32[512,128]{1,0:T(8,128)S(1)} %get-tuple-element.65.out_ref, bf16[512,128]{1,0:T(8,128)(2,1)S(1)} %bitcast.97, ...), custom_call_target="tpu_custom_call" | custom-call | flops 10737418240 | bytes 8388608 | tf_op jit(solution)/shard_map/attend_back/pallas_call | solution.py:218
  134.4 22.2 %scatter_keys.1 = (bf16[2,256,128]{2,1,0:T(8,128)(2,1)S(1)}, bf16[2,256,128]{2,1,0:T(8,128)(2,1)S(1)}, bf16[8,64,1024]{2,1,0:T(8,128)(2,1)S(1)}) custom-call(bf16[4,4,2,256,128]{4,3,2,1,0:T(8,128)(2,1)S(1)} %bitcast.85, bf16[2,256,128]{2,1,0:T(8,128)(2,1)S(1)} %bitcast.100, bf16[8,64,1024]{2,1,0:T(8,128)(2,1)S(1)} %bitcast.89, ...), custom_call_target="tpu_custom_call" | custom-call | flops 8589934592 | bytes 33554432 | tf_op jit(solution)/shard_map/scatter_keys/pallas_call | solution.py:745
  156.6 2.5 %project_back.1 = (bf16[512,1024]{1,0:T(8,128)(2,1)S(1)}, bf16[2,128,1024]{2,1,0:T(8,128)(2,1)S(1)}, f32[1,1024]{1,0:T(1,128)S(1)}) custom-call(bf16[512,128]{1,0:T(8,128)(2,1)S(1)} %bitcast.99, bf16[512,128]{1,0:T(8,128)(2,1)S(1)} %bitcast.98, f32[512,128]{1,0:T(8,128)S(1)} %get-tuple-element.75.qp_ref, f32[512,128]{1,0:T(8,128)S(1)} %get-tuple-element.76.kvp_ref, ...), custom_call_target="tpu_custom_call" | custom-call | flops 3221225472 | bytes 16777216 | tf_op jit(solution)/shard_map/project_back/pallas_call | solution.py:898
  159.1 23.9 %last_sums.1 = (bf16[8,64,1024]{2,1,0:T(8,128)(2,1)S(1)}, bf16[3,4,32,1024]{3,2,1,0:T(8,128)(2,1)S(1)}, f32[8,1024]{1,0:T(8,128)S(1)}) custom-call(bf16[8,64,1024]{2,1,0:T(8,128)(2,1)S(1)} %bitcast.94, bf16[2,4,32,1024]{3,2,1,0:T(8,128)(2,1)S(1)} %bitcast.96, bf16[4,32,1024]{2,1,0:T(8,128)(2,1)S(1)} %bitcast.66, bf16[8,64,1024]{2,1,0:T(8,128)(2,1)S(1)} %bitcast.70, ...), custom_call_target="tpu_custom_call" | custom-call | flops 8589934592 | bytes 33554432 | tf_op jit(solution)/shard_map/last_sums/pallas_call | solution.py:745
  183.0 4.7 %finish.1 = (bf16[512,1024]{1,0:T(8,128)(2,1)}, bf16[512,1024]{1,0:T(8,128)(2,1)}, f32[1024,128]{1,0:T(8,128)}, f32[64,1024]{1,0:T(8,128)}, f32[64,1024]{1,0:T(8...) custom-call(bf16[3,128,1024]{2,1,0:T(8,128)(2,1)S(1)} %bitcast.65, ...), custom_call_target="tpu_custom_call" | custom-call | tf_op jit(solution)/shard_map/finish/pallas_call | solution.py:941
Async XLA Ops:
  0.6 68.1 %copy-start = (bf16[1024,576]{0,1:T(8,128)(2,1)S(1)}, bf16[1024,576]{0,1:T(8,128)(2,1)}, u32[]{:S(2)}) copy-start(bf16[1024,576]{0,1:T(8,128)(2,1)} %param.25) | copy-start | bytes 3538948
  0.7 2.6 %copy-start.12 = (f32[32]{0:T(128)S(1)}, f32[32]{0:T(128)}, u32[]{:S(2)}) copy-start(f32[32]{0:T(128)} %constant.4.clone) | copy-start | bytes 388
  0.7 2.7 %copy-start.2 = (bf16[512,1024]{1,0:T(8,128)(2,1)S(1)}, bf16[512,1024]{1,0:T(8,128)(2,1)}, u32[]{:S(2)}) copy-start(bf16[512,1024]{1,0:T(8,128)(2,1)} %tok_ref.1) | copy-start | bytes 3145732
  0.7 2.7 %copy-start.4 = (bf16[1024,128]{1,0:T(8,128)(2,1)S(1)}, bf16[1024,128]{1,0:T(8,128)(2,1)}, u32[]{:S(2)}) copy-start(bf16[1024,128]{1,0:T(8,128)(2,1)} %wq_ref.3) | copy-start | bytes 786436
  0.7 2.7 %copy-start.5 = (bf16[1024,64]{0,1:T(8,128)(2,1)S(1)}, bf16[1024,64]{0,1:T(8,128)(2,1)}, u32[]{:S(2)}) copy-start(bf16[1024,64]{0,1:T(8,128)(2,1)} %param.18) | copy-start | bytes 393220
  0.7 2.7 %copy-start.6 = (bf16[1024,64]{0,1:T(8,128)(2,1)S(1)}, bf16[1024,64]{0,1:T(8,128)(2,1)}, u32[]{:S(2)}) copy-start(bf16[1024,64]{0,1:T(8,128)(2,1)} %param.19) | copy-start | bytes 393220
  0.7 2.7 %copy-start.8 = (f32[1024]{0:T(1024)S(1)}, f32[1024]{0:T(1024)}, u32[]{:S(2)}) copy-start(f32[1024]{0:T(1024)} %param.16) | copy-start | bytes 12292
  0.7 2.7 %copy-start.9 = (s32[4]{0:T(128)S(1)}, s32[4]{0:T(128)}, u32[]{:S(2)}) copy-start(s32[4]{0:T(128)} %len_ref.5) | copy-start | bytes 52
  0.7 2.7 %copy-start.10 = (f32[64]{0:T(128)S(1)}, f32[64]{0:T(128)}, u32[]{:S(2)}) copy-start(f32[64]{0:T(128)} %param.20) | copy-start | bytes 772
  0.7 2.7 %copy-start.11 = (f32[64]{0:T(128)S(1)}, f32[64]{0:T(128)}, u32[]{:S(2)}) copy-start(f32[64]{0:T(128)} %param.21) | copy-start | bytes 772
  30.2 9.3 %copy-start.3 = (bf16[128,1024]{1,0:T(8,128)(2,1)S(1)}, bf16[128,1024]{1,0:T(8,128)(2,1)}, u32[]{:S(2)}) copy-start(bf16[128,1024]{1,0:T(8,128)(2,1)} %w_ref.3) | copy-start | bytes 786436
  30.2 9.3 %copy-start.7 = (f32[1024]{0:T(1024)S(1)}, f32[1024]{0:T(1024)}, u32[]{:S(2)}) copy-start(f32[1024]{0:T(1024)} %param.23) | copy-start | bytes 12292
  39.5 28.4 %copy-start.14 = (bf16[1024,576]{0,1:T(8,128)(2,1)S(1)}, bf16[1024,576]{0,1:T(8,128)(2,1)}, u32[]{:S(2)}) copy-start(bf16[1024,576]{0,1:T(8,128)(2,1)} %param.24) | copy-start | bytes 3538948
  68.7 1.3 copy-start.13
  70.0 1.2 copy-start.1

commit v4 on v3

--- a/solution.py
+++ b/solution.py
@@ -14,7 +14,6 @@
 CH = 512
 HALF = 256
 SCALE = 0.125
-EARLY = 4
 C2 = SCALE * math.log2(math.e)
 
 
@@ -126,75 +125,6 @@
         qa_ref[t, :, 128:256] = (split3(jnp.log(total) * (-1.0 / SCALE), lane2) + columns).astype(bf16)
 
 
-def bwd_kernel(parts, qa_ref, out_ref, do_ref, kv_ref, ext_ref, red_ref, dq_ref, dkv_ref, grads_ref, da_ref, acc_ref, dqt_ref, *sems):
-    me = lax.axis_index("sp")
-    p = Place()
-    meet([p.along_x(d) for d in ORDER] + [p.along_y(d) for d in ORDER])
-    spread = SpGather(p, grads_ref, 144, sems)
-    for i in range(3):
-        for h in range(2):
-            spread.put(i, h, red_ref[i, h])
-            spread.first(i, h)
-    lane = lanes((HALF, 128))
-    acc_ref[...] = jnp.zeros_like(acc_ref)
-    upper_long = (me < parts // 2).astype(jnp.int32)
-    for turn in range(2):
-        t = upper_long if turn == 0 else 1 - upper_long
-        block = me + t * (parts - 1 - 2 * me)
-        r0 = block * 512 + t * HALF
-        rows_t = pl.ds(pl.multiple_of(t * HALF, HALF), HALF)
-        do = do_ref[rows_t, :].astype(f32)
-        prod = do * out_ref[rows_t, :]
-        d0 = -jnp.sum(jnp.where(lane < 64, prod, 0.0), axis=1, keepdims=True)
-        d1 = -jnp.sum(jnp.where(lane < 64, 0.0, prod), axis=1, keepdims=True)
-        da_ref[0:HALF, 0:128] = jnp.where(lane < 64, 0.0, pltpu.roll(do, 64, 1)).astype(bf16)
-        da_ref[HALF:, 0:128] = jnp.where(lane < 64, 0.0, do).astype(bf16)
-        da_ref[0:HALF, 128:256] = split3(jnp.broadcast_to(d0, (HALF, 128)), lane).astype(bf16)
-        da_ref[HALF:, 128:256] = split3(jnp.broadcast_to(d1, (HALF, 128)), lane).astype(bf16)
-        dqt_ref[...] = jnp.zeros_like(dqt_ref)
-
-        def step(c, masked, t=t, r0=r0):
-            k0 = pl.multiple_of(c * CH, CH)
-            kv = kv_ref[pl.ds(k0, CH), :]
-            kva = jnp.concatenate([kv, ext_ref[pl.ds(k0, CH), :]], axis=1)
-            qa = qa_ref[t]
-            da = da_ref[...]
-            s = lax.dot_general(kva, qa, (((1,), (1,)), ((), ())), preferred_element_type=f32)
-            p = jnp.exp2(s * C2)
-            if masked:
-                rows = r0 + lax.rem(lax.broadcasted_iota(jnp.int32, (1, 2 * HALF), 1), HALF)
-                keys = k0 + lax.broadcasted_iota(jnp.int32, (CH, 2 * HALF), 0)
-                p = jnp.where(keys <= rows, p, 0.0)
-            dp = lax.dot_general(kva, da, (((1,), (1,)), ((), ())), preferred_element_type=f32)
-            ds = (p * dp).astype(bf16)
-            acc_ref[pl.ds(k0, CH), :] += jnp.dot(
-                p.astype(bf16), da[:, 0:128], preferred_element_type=f32
-            ) + jnp.dot(ds, qa[:, 0:128], preferred_element_type=f32)
-            kt = kv.T[0:64, :]
-            dqt_ref[...] += jnp.dot(kt, ds, preferred_element_type=f32)
-
-        if turn == 0:
-            pl.loop(0, EARLY)(lambda c: step(c, False))
-            for i in range(3):
-                for h in range(2):
-                    spread.second(i, h)
-            pl.loop(EARLY, block)(lambda c: step(c, False))
-        else:
-            pl.loop(0, block)(lambda c: step(c, False))
-        step(block, True)
-        dqt = dqt_ref[...]
-        both = jnp.concatenate([dqt[:, :HALF], dqt[:, HALF:]], axis=0)
-        dq_ref[rows_t, :] = (both.T * SCALE).astype(bf16)
-    weight = jnp.where(lanes((512, 128)) < 64, SCALE, 1.0)
-
-    @pl.loop(0, parts)
-    def _(b):
-        rows = pl.ds(pl.multiple_of(b * 512, 512), 512)
-        dkv_ref[rows, :] = (acc_ref[rows, :] * weight).astype(bf16)
-
-    spread.finish()
-
-
 smem = pl.BlockSpec(memory_space=pltpu.SMEM)
 vmem = pl.BlockSpec(memory_space=pltpu.VMEM)
 
@@ -211,21 +141,6 @@
         cost_estimate=pl.CostEstimate(flops=3 << 30, bytes_accessed=4 << 20, transcendentals=5 << 20),
         name="attend",
     )(lengths, q, kv, ext)
-
-
-def attend_back(parts, qa, out, do, kv, ext, red):
-    rows = 2 * HALF
-    return pl.pallas_call(
-        functools.partial(bwd_kernel, parts),
-        out_shape=(sds((rows, 128), bf16), sds(kv.shape, bf16), sds((3, 4, 144, 1024), bf16)),
-        in_specs=[vmem] * 6,
-        out_specs=(vmem, vmem, vmem),
-        scratch_shapes=[pltpu.VMEM((rows, 256), bf16), pltpu.VMEM(kv.shape, f32), pltpu.VMEM((64, rows), f32)]
-        + SpGather.sems(3),
-        compiler_params=pltpu.CompilerParams(collective_id=6, has_side_effects=True, vmem_limit_bytes=20 << 20),
-        cost_estimate=pl.CostEstimate(flops=10 << 30, bytes_accessed=8 << 20, transcendentals=5 << 20),
-        name="attend_back",
-    )(qa, out, do, kv, ext, red)
 
 
 MESH = pl.DeviceIdType.MESH
@@ -541,61 +456,6 @@
 
 def wt_peers(p):
     return [p.sibling] + [p.along_z(d) for d in ORDER]
-
-
-def scatter_kernel(dkv_ref, dqz_ref, mlp_ref, mid_ref, own_ref, dq_ref, out_ref, r1, send, r2, ms, mr, fs, fr, ss, sr,
-                   sib, sendz, rz, cs, cr, zs, zr, az, bz, ag, bg):
-    p = Place()
-    meet(wt_peers(p) + [p.along_x(d) for d in ORDER] + [p.along_y(d) for d in ORDER] + [p.mirror])
-    first, second = {}, {}
-    for d in ORDER:
-        for h in range(2):
-            to = lax.rem(p.fsp(h) + d, 4)
-            src = dkv_ref.at[to, :, 0] if h == 0 else dkv_ref.at[:, to, 1]
-            first[h, d] = rcopy(src, r1.at[h, d - 1], fs.at[h, d - 1], fr.at[h, d - 1], p.first(h, d))
-            first[h, d].start()
-    down = WtSum(p, mlp_ref, sib, sendz, rz, (cs, cr, zs, zr))
-    for zz in range(4):
-        down.start_core(zz)
-    mirror = rcopy(dqz_ref.at[1], dq_ref.at[1], ms, mr, p.mirror)
-    mirror.start()
-    dq_ref[0] = dqz_ref[0]
-    for d in ORDER:
-        down.send_z(d)
-
-    def total(h, b):
-        at = spot(h, p.fsp(h), b)
-        value = dkv_ref[at[0], at[1], h].astype(f32)
-        for d in range(3):
-            value = value + r1[h, d, b].astype(f32)
-        return value
-
-    out_ref[p.wt] = (mid_ref[...] + down.own()).astype(bf16)
-    spread = WtGather(p, out_ref, (az, bz, ag, bg))
-    spread.start()
-    for h in range(2):
-        for d in ORDER:
-            first[h, d].wait_recv()
-        for e in ORDER:
-            b = lax.rem(p.ssp(h) + e, 4)
-            send[h, e - 1] = total(h, b).astype(bf16)
-            second[h, e] = rcopy(
-                send.at[h, e - 1], r2.at[h, e - 1], ss.at[h, e - 1], sr.at[h, e - 1], p.second(h, e)
-            )
-            second[h, e].start()
-    spread.forward()
-    for h in range(2):
-        value = total(h, p.ssp(h))
-        for e in ORDER:
-            second[h, e].wait_recv()
-            value = value + r2[h, e - 1].astype(f32)
-        own_ref[h] = value.astype(bf16)
-    mirror.wait()
-    spread.arrived()
-    spread.finish()
-    down.finish()
-    for copy in list(first.values()) + list(second.values()):
-        copy.wait_send()
 
 
 def middle_kernel(mix_ref, w_ref, tok_ref, gain_ref, nm_ref, mid_ref, mixo_ref, part, sib, send, rz, ms, mr, cs, cr, zs, zr, az, bz, ag, bg):
@@ -625,119 +485,6 @@
     total.finish()
 
 
-def turn_kernel(dm_ref, mid_ref, cot_ref, gain_ref, w_ref, g0_ref, g1_ref, g2_ref,
-                da_ref, dmid_ref, gn_ref, dz_ref, red_ref,
-                up, sib, send, rz, ms, mr, cs, cr, zs, zr, az, bz, ag, bg, *grad_refs):
-    p = Place()
-    meet(wt_peers(p) + [p.mirror] + [p.along_x(d) for d in ORDER] + [p.along_y(d) for d in ORDER])
-    total = WtSum(p, dm_ref, sib, send, rz, (cs, cr, zs, zr))
-    grads = SpScatter(p, (g0_ref, g1_ref, g2_ref), 144, grad_refs)
-    for zz in range(4):
-        total.start_core(zz)
-    for i in range(3):
-        grads.first(i)
-    for d in ORDER:
-        total.send_z(d)
-    middle = mid_ref[...]
-    scale = rms_of(middle)
-    d_mid = total.own()
-    gn_ref[...] = jnp.sum(d_mid * middle * scale, axis=0, keepdims=True)
-    d_middle = cot_ref[p.wt].astype(f32) + norm_back(middle, scale, gain_ref[...], d_mid)
-    dmid_ref[...] = d_middle
-    da_ref[p.wt] = d_middle.astype(bf16)
-    spread = WtGather(p, da_ref, (az, bz, ag, bg))
-    spread.start()
-    grads.second(0)
-    spread.forward()
-    spread.arrived()
-    mirror = rcopy(up, dz_ref.at[1], ms, mr, p.mirror)
-    for half in (1, 0):
-        rows = da_ref[half * 4:half * 4 + 4].reshape(256, 1024)
-        d_mixed = lax.dot_general(rows, w_ref[...], (((1,), (1,)), ((), ())), preferred_element_type=f32).astype(bf16)
-        if half == 1:
-            up[...] = d_mixed
-            mirror.start()
-        else:
-            dz_ref[0] = d_mixed
-    grads.second(1)
-    grads.second(2)
-    for i in range(3):
-        for h in range(2):
-            red_ref[i, h] = grads.own(i, h).astype(bf16)
-    mirror.wait()
-    for part in (spread, total, grads):
-        part.finish()
-
-
-def last_kernel(dn_ref, gq_ref, go_ref, tok_ref, dmid_ref, gain_ref, gn_ref, gg_ref,
-                gt_ref, sums_ref, vec_ref,
-                sib, send, rz, cs, cr, zs, zr, az, bz, ag, bg,
-                vw, vx, vy, vs1, vr1, vs2, vr2, vs3, vr3, *more):
-    p = Place()
-    meet(wt_peers(p) + [p.along_z_other(d) for d in ORDER] + [p.along_x(d) for d in ORDER] + [p.along_y(d) for d in ORDER])
-    total = WtSum(p, dn_ref, sib, send, rz, (cs, cr, zs, zr))
-    for zz in range(4):
-        total.start_core(zz)
-    grads = SpScatter(p, (gq_ref.at[0], gq_ref.at[1], go_ref), 32, more[:8])
-    back = SpGather(p, sums_ref, 32, more[8:12])
-    for i in range(3):
-        grads.first(i)
-    for d in ORDER:
-        total.send_z(d)
-
-    vw[0] = jnp.zeros((8, 1024), f32)
-    gains = jnp.zeros((1, 1024), f32)
-    for w in range(8):
-        base = tok_ref[w].astype(f32)
-        gains = gains + jnp.sum(dn_ref[w].astype(f32) * base * rms_of(base), axis=0, keepdims=True)
-    vw[0, 0:1] = gains
-    vw[0, 1:2] = gn_ref[...]
-    vw[0, 2:3] = gg_ref[...]
-
-    def vec_round(buf, devices, sends, recvs):
-        copies = []
-        for i, device in enumerate(devices):
-            copies.append(rcopy(buf.at[0], buf.at[i + 1], sends.at[i], recvs.at[i], device))
-            copies[-1].start()
-        return copies
-
-    def vec_total(buf, copies):
-        value = buf[0]
-        for i, copy in enumerate(copies):
-            copy.wait_recv()
-            value = value + buf[i + 1]
-        return value
-
-    round1 = vec_round(vw, [p.along_z(d) for d in ORDER] + [p.along_z_other(d) for d in ORDER] + [p.sibling], vs1, vr1)
-    for i in range(3):
-        grads.second(i)
-    base = tok_ref[p.wt].astype(f32)
-    d_normed = total.own()
-    gt_ref[p.wt] = (dmid_ref[...] + norm_back(base, rms_of(base), gain_ref[...], d_normed)).astype(bf16)
-    spread = WtGather(p, gt_ref, (az, bz, ag, bg))
-    spread.start()
-    for i in range(3):
-        for h in range(2):
-            back.put(i, h, grads.own(i, h).astype(bf16))
-            back.first(i, h)
-    vx[0] = vec_total(vw, round1)
-    round2 = vec_round(vx, [p.along_x(d) for d in ORDER], vs2, vr2)
-    for i in range(3):
-        for h in range(2):
-            back.second(i, h)
-    vy[0] = vec_total(vx, round2)
-    round3 = vec_round(vy, [p.along_y(d) for d in ORDER], vs3, vr3)
-    spread.forward()
-    vec_ref[...] = vec_total(vy, round3)
-    spread.arrived()
-    spread.finish()
-    total.finish()
-    grads.finish()
-    back.finish()
-    for copy in round1 + round2 + round3:
-        copy.wait_send()
-
-
 WT_SEMS = [DMA((4,)), DMA((4,)), DMA((3,)), DMA((3,)), DMA((3,)), DMA((3,)), DMA((4,)), DMA((4,))]
 
 
@@ -766,18 +513,6 @@
     )
 
 
-def scatter_keys(dkv, dq, mlp, mid):
-    return comm_call(
-        scatter_kernel, 2,
-        (sds((2, 256, 128), bf16), sds((2, 256, 128), bf16), sds((8, 64, 1024), bf16)),
-        (dkv.reshape(4, 4, 2, 256, 128), dq.reshape(2, 256, 128), mlp.reshape(8, 64, 1024), mid),
-        [pltpu.VMEM((2, 3, 4, 256, 128), bf16), pltpu.VMEM((2, 3, 256, 128), bf16), pltpu.VMEM((2, 3, 256, 128), bf16),
-         DMA, DMA, DMA((2, 3)), DMA((2, 3)), DMA((2, 3)), DMA((2, 3)),
-         pltpu.VMEM((4, 64, 1024), bf16), pltpu.VMEM((3, 64, 1024), bf16), pltpu.VMEM((3, 64, 1024), bf16)] + WT_SEMS,
-        "scatter_keys",
-    )
-
-
 def make_middle(mix, w_out, tokens, gain):
     rows = pltpu.VMEM
     return comm_call(
@@ -787,37 +522,6 @@
         [rows((8, 64, 1024), bf16), rows((4, 64, 1024), bf16), rows((3, 64, 1024), bf16), rows((3, 64, 1024), bf16),
          DMA, DMA, DMA((4,)), DMA((4,)), DMA((3,)), DMA((3,)), DMA((3,)), DMA((3,)), DMA((4,)), DMA((4,))],
         "make_middle",
-    )
-
-
-def turn_back(dm, mid, cot, gain, w_out, grads):
-    rows = pltpu.VMEM
-    return comm_call(
-        turn_kernel, 4,
-        (sds((8, 64, 1024), bf16), sds((64, 1024), f32), sds((1, 1024), f32),
-         sds((2, 256, 128), bf16), sds((3, 2, 144, 128), bf16)),
-        (dm.reshape(8, 64, 1024), mid, cot.reshape(8, 64, 1024), gain.reshape(1, 1024), w_out)
-        + tuple(g.reshape(4, 144, 1024) for g in grads),
-        [rows((256, 128), bf16), rows((4, 64, 1024), bf16), rows((3, 64, 1024), bf16), rows((3, 64, 1024), bf16),
-         DMA, DMA] + WT_SEMS
-        + SpScatter.scratch(3, 144),
-        "turn_back", 16,
-    )
-
-
-def last_sums(dn, gq, go, tokens, dmid, gain, gn, gg):
-    rows = pltpu.VMEM
-    return comm_call(
-        last_kernel, 5,
-        (sds((8, 64, 1024), bf16), sds((3, 4, 32, 1024), bf16), sds((8, 1024), f32)),
-        (dn.reshape(8, 64, 1024), gq.reshape(2, 4, 32, 1024), go.reshape(4, 32, 1024), tokens.reshape(8, 64, 1024),
-         dmid, gain.reshape(1, 1024), gn, gg),
-        [rows((4, 64, 1024), bf16), rows((3, 64, 1024), bf16), rows((3, 64, 1024), bf16),
-         DMA((4,)), DMA((4,)), DMA((3,)), DMA((3,)), DMA((3,)), DMA((3,)), DMA((4,)), DMA((4,)),
-         rows((8, 8, 1024), f32), rows((4, 8, 1024), f32), rows((4, 8, 1024), f32),
-         DMA((7,)), DMA((7,)), DMA((3,)), DMA((3,)), DMA((3,)), DMA((3,))]
-        + SpScatter.scratch(3, 32) + SpGather.sems(3),
-        "last_sums", 10,
     )
 
 
@@ -869,31 +573,6 @@
     kv_ref[...] = jnp.where(lane < 64, k, kv).astype(bf16)
 
 
-def proj_back_kernel(dq_ref, dkv_ref, qp_ref, kvp_ref, n_ref, wq_ref, wk_ref, wv_ref, qg_ref, kg_ref, cos_ref, sin_ref, dn_ref, g_ref, gg_ref):
-    lane = lanes((512, 128))
-    cosine, sine = cos_ref[...], sin_ref[...]
-
-    def back(grad, proj, gain):
-        grad = grad * cosine - turned(grad, lane) * sine
-        scale = lax.rsqrt(head_sums(proj * proj, lane) * (1.0 / 64) + eps)
-        scaled = grad * gain
-        inner = head_sums(scaled * proj, lane) * (1.0 / 64)
-        gains = jnp.sum(grad * proj * scale, axis=0, keepdims=True)
-        return scale * scaled - proj * scale * scale * scale * inner, gains
-
-    dq, gq = back(dq_ref[...].astype(f32), qp_ref[...], twice(qg_ref[...]))
-    dkv_in = dkv_ref[...].astype(f32)
-    dk, gk = back(dkv_in, kvp_ref[...], twice(kg_ref[...]))
-    dq = dq.astype(bf16)
-    dkv = jnp.where(lane < 64, dk, dkv_in).astype(bf16)
-    wkv = jnp.concatenate([wk_ref[...], wv_ref[...]], axis=0)
-    dn_ref[...] = (nt(dq, wq_ref[...]) + jnp.dot(dkv, wkv, preferred_element_type=f32)).astype(bf16)
-    normed = n_ref[...]
-    g_ref[0] = tn(dq, normed).astype(bf16)
-    g_ref[1] = tn(dkv, normed).astype(bf16)
-    gg_ref[...] = jnp.concatenate([gq, gk, jnp.zeros((1, 768), f32)], axis=1)
-
-
 def local_call(kernel, out_shape, args, name, first=None):
     return pl.pallas_call(
         kernel,
@@ -906,6 +585,305 @@
     )(*args)
 
 
+class Flow:
+    def __init__(self):
+        self.copies = []
+
+    def send(self, *args):
+        copy = rcopy(*args)
+        copy.start()
+        self.copies.append(copy)
+        return copy
+
+    def finish(self):
+        for copy in self.copies:
+            copy.wait_send()
+
+
+def backward_kernel(
+    parts,
+    dm_ref, mlp_ref, mid_ref, cot_ref, gain_ref, w_ref, g0_ref, g1_ref, g2_ref,
+    qa_ref, mixf_ref, kv_ref, ext_ref, mixed_ref,
+    qp_ref, kvp_ref, n_ref, wq_ref, wk_ref, wv_ref, qg_ref, kg_ref, cos_ref, sin_ref, tok_ref, gain_in_ref,
+    out_ref, gt_ref, sums_ref, ff_ref, vec_ref,
+    *scratch,
+):
+    scratch = list(scratch)
+
+    def take(n):
+        got = scratch[:n]
+        del scratch[:n]
+        return got
+
+    p = Place()
+    me = p.sp
+    meet(
+        wt_peers(p) + [p.along_z_other(d) for d in ORDER] + [p.mirror]
+        + [p.along_x(d) for d in ORDER] + [p.along_y(d) for d in ORDER]
+    )
+    flow = Flow()
+
+    def wt_sum(ref):
+        sib, send, rz = take(3)
+        return WtSum(p, ref, sib, send, rz, take(4))
+
+    da, da_up, dz = take(3)
+    mirror_sems = take(4)
+    d_mid_sum = wt_sum(dm_ref)
+    da_gather = WtGather(p, da, take(4))
+    mlp_sum = wt_sum(mlp_ref)
+    out_gather = WtGather(p, out_ref, take(4))
+    ff = SpScatter(p, (g0_ref, g1_ref, g2_ref), 144, take(8))
+    ff_back = SpGather(p, ff_ref, 144, take(4))
+    dab, acc, dqt, dqz, dq, dkv, dkv_own = take(7)
+    r1, send1, r2, fs, fr, ss, sr = take(7)
+    dn, gqkv, gout = take(3)
+    dn_sum = wt_sum(dn)
+    gt_gather = WtGather(p, gt_ref, take(4))
+    sums = SpScatter(p, (gout, gqkv.at[0], gqkv.at[1]), 32, take(8))
+    sums_back = SpGather(p, sums_ref, 32, take(4))
+    vw, vx, vy, vs1, vr1, vs2, vr2, vs3, vr3 = take(9)
+    assert not scratch
+
+    for zz in range(4):
+        d_mid_sum.start_core(zz)
+    ff.first(0)
+    ff.first(1)
+    for d in ORDER:
+        d_mid_sum.send_z(d)
+    for zz in range(4):
+        mlp_sum.start_core(zz)
+    middle = mid_ref[...]
+    scale = rms_of(middle)
+    d_mid = d_mid_sum.own()
+    d_middle = cot_ref[p.wt].astype(f32) + norm_back(middle, scale, gain_ref[...], d_mid)
+    da[p.wt] = d_middle.astype(bf16)
+    da_gather.start()
+    vw[0] = jnp.zeros((8, 1024), f32)
+    vw[0, 1:2] = jnp.sum(d_mid * middle * scale, axis=0, keepdims=True)
+    ff.second(0)
+    da_gather.forward()
+    da_gather.arrived()
+    for half in (1, 0):
+        rows = da[half * 4:half * 4 + 4].reshape(256, 1024)
+        d_mixed = nt(rows, w_ref[...]).astype(bf16)
+        if half == 1:
+            da_up[...] = d_mixed
+            mirror = flow.send(da_up, dz.at[1], mirror_sems[0], mirror_sems[1], p.mirror)
+        else:
+            dz[0] = d_mixed
+    ff.first(2)
+    for d in ORDER:
+        mlp_sum.send_z(d)
+    gout[...] = tn(mixed_ref[...], da[...].reshape(512, 1024)).astype(bf16).reshape(4, 32, 1024)
+    ff.second(1)
+    mirror.wait_recv()
+
+    lane = lanes((HALF, 128))
+    acc[...] = jnp.zeros_like(acc)
+    upper_long = (me < parts // 2).astype(jnp.int32)
+    for turn in range(2):
+        t = upper_long if turn == 0 else 1 - upper_long
+        block = me + t * (parts - 1 - 2 * me)
+        r0 = block * 512 + t * HALF
+        rows_t = pl.ds(pl.multiple_of(t * HALF, HALF), HALF)
+        do = dz[t].astype(f32)
+        prod = do * mixf_ref[rows_t, :]
+        d0 = -jnp.sum(jnp.where(lane < 64, prod, 0.0), axis=1, keepdims=True)
+        d1 = -jnp.sum(jnp.where(lane < 64, 0.0, prod), axis=1, keepdims=True)
+        dab[0:HALF, 0:128] = jnp.where(lane < 64, 0.0, pltpu.roll(do, 64, 1)).astype(bf16)
+        dab[HALF:, 0:128] = jnp.where(lane < 64, 0.0, do).astype(bf16)
+        dab[0:HALF, 128:256] = split3(jnp.broadcast_to(d0, (HALF, 128)), lane).astype(bf16)
+        dab[HALF:, 128:256] = split3(jnp.broadcast_to(d1, (HALF, 128)), lane).astype(bf16)
+        dqt[...] = jnp.zeros_like(dqt)
+
+        def step(c, masked, t=t, r0=r0):
+            k0 = pl.multiple_of(c * CH, CH)
+            kv = kv_ref[pl.ds(k0, CH), :]
+            kva = jnp.concatenate([kv, ext_ref[pl.ds(k0, CH), :]], axis=1)
+            qa = qa_ref[t]
+            d_out = dab[...]
+            s = nt(kva, qa)
+            pr = jnp.exp2(s * C2)
+            if masked:
+                rows = r0 + lax.rem(lax.broadcasted_iota(jnp.int32, (1, 2 * HALF), 1), HALF)
+                keys = k0 + lax.broadcasted_iota(jnp.int32, (CH, 2 * HALF), 0)
+                pr = jnp.where(keys <= rows, pr, 0.0)
+            ds = (pr * nt(kva, d_out)).astype(bf16)
+            acc[pl.ds(k0, CH), :] += jnp.dot(
+                pr.astype(bf16), d_out[:, 0:128], preferred_element_type=f32
+            ) + jnp.dot(ds, qa[:, 0:128], preferred_element_type=f32)
+            kt = kv.T[0:64, :]
+            dqt[...] += jnp.dot(kt, ds, preferred_element_type=f32)
+
+        def plain(c):
+            step(c, False)
+
+        if turn == 0:
+            pl.loop(0, 4)(plain)
+            for i in range(2):
+                for h in range(2):
+                    ff_back.put(i, h, ff.own(i, h).astype(bf16))
+                    ff_back.first(i, h)
+            ff.second(2)
+            out_ref[p.wt] = (middle + mlp_sum.own()).astype(bf16)
+            out_gather.start()
+            pl.loop(4, 8)(plain)
+            for h in range(2):
+                ff_back.put(2, h, ff.own(2, h).astype(bf16))
+                ff_back.first(2, h)
+            for h in range(2):
+                ff_back.second(0, h)
+            out_gather.forward()
+            pl.loop(8, block)(plain)
+        else:
+            pl.loop(0, block)(plain)
+        step(block, True)
+        both = jnp.concatenate([dqt[:, :HALF], dqt[:, HALF:]], axis=0)
+        dqz[t] = (both.T * SCALE).astype(bf16)
+    weight = jnp.where(lanes((512, 128)) < 64, SCALE, 1.0)
+
+    @pl.loop(0, parts)
+    def _(b):
+        rows = pl.ds(pl.multiple_of(b * 512, 512), 512)
+        dkv[lax.div(b, 4), lax.rem(b, 4)] = (acc[rows, :] * weight).astype(bf16).reshape(2, 256, 128)
+
+    mirror = flow.send(dqz.at[1], dq.at[1], mirror_sems[2], mirror_sems[3], p.mirror)
+    dq[0] = dqz[0]
+    first, second = {}, {}
+    for d in ORDER:
+        for h in range(2):
+            to = lax.rem(p.fsp(h) + d, 4)
+            src = dkv.at[to, :, 0] if h == 0 else dkv.at[:, to, 1]
+            first[h, d] = flow.send(src, r1.at[h, d - 1], fs.at[h, d - 1], fr.at[h, d - 1], p.first(h, d))
+
+    def total(h, b):
+        at = spot(h, p.fsp(h), b)
+        value = dkv[at[0], at[1], h].astype(f32)
+        for d in range(3):
+            value = value + r1[h, d, b].astype(f32)
+        return value
+
+    for h in range(2):
+        for d in ORDER:
+            first[h, d].wait_recv()
+        for e in ORDER:
+            send1[h, e - 1] = total(h, lax.rem(p.ssp(h) + e, 4)).astype(bf16)
+            second[h, e] = flow.send(
+                send1.at[h, e - 1], r2.at[h, e - 1], ss.at[h, e - 1], sr.at[h, e - 1], p.second(h, e)
+            )
+    for h in range(2):
+        ff_back.second(1, h)
+    for h in range(2):
+        value = total(h, p.ssp(h))
+        for e in ORDER:
+            second[h, e].wait_recv()
+            value = value + r2[h, e - 1].astype(f32)
+        dkv_own[h] = value.astype(bf16)
+    mirror.wait_recv()
+
+    wide = lanes((512, 128))
+    cosine, sine = cos_ref[...], sin_ref[...]
+
+    def back(grad, proj, gain):
+        grad = grad * cosine - turned(grad, wide) * sine
+        scale = lax.rsqrt(head_sums(proj * proj, wide) * (1.0 / 64) + eps)
+        scaled = grad * gain
+        inner = head_sums(scaled * proj, wide) * (1.0 / 64)
+        gains = jnp.sum(grad * proj * scale, axis=0, keepdims=True)
+        return scale * scaled - proj * scale * scale * scale * inner, gains
+
+    d_q, gq = back(dq[...].reshape(512, 128).astype(f32), qp_ref[...], twice(qg_ref[...]))
+    dkv_in = dkv_own[...].reshape(512, 128).astype(f32)
+    d_k, gk = back(dkv_in, kvp_ref[...], twice(kg_ref[...]))
+    d_q = d_q.astype(bf16)
+    d_kv = jnp.where(wide < 64, d_k, dkv_in).astype(bf16)
+    wkv = jnp.concatenate([wk_ref[...], wv_ref[...]], axis=0)
+    dn[...] = (nt(d_q, wq_ref[...]) + jnp.dot(d_kv, wkv, preferred_element_type=f32)).astype(bf16).reshape(8, 64, 1024)
+    for zz in range(4):
+        dn_sum.start_core(zz)
+    normed = n_ref[...]
+    gqkv[0] = tn(d_q, normed).astype(bf16).reshape(4, 32, 1024)
+    gqkv[1] = tn(d_kv, normed).astype(bf16).reshape(4, 32, 1024)
+    for i in range(3):
+        sums.first(i)
+    for d in ORDER:
+        dn_sum.send_z(d)
+
+    gains = jnp.zeros((1, 1024), f32)
+    for w in range(8):
+        base = tok_ref[w].astype(f32)
+        gains = gains + jnp.sum(dn[w].astype(f32) * base * rms_of(base), axis=0, keepdims=True)
+    vw[0, 0:1] = gains
+    vw[0, 2:3] = jnp.concatenate([gq, gk, jnp.zeros((1, 768), f32)], axis=1)
+
+    def vec_round(buf, devices, sends, recvs):
+        return [
+            flow.send(buf.at[0], buf.at[i + 1], sends.at[i], recvs.at[i], device) for i, device in enumerate(devices)
+        ]
+
+    def vec_total(buf, copies):
+        value = buf[0]
+        for i, copy in enumerate(copies):
+            copy.wait_recv()
+            value = value + buf[i + 1]
+        return value
+
+    round1 = vec_round(vw, [p.along_z(d) for d in ORDER] + [p.along_z_other(d) for d in ORDER] + [p.sibling], vs1, vr1)
+    for h in range(2):
+        ff_back.second(2, h)
+    for i in range(3):
+        sums.second(i)
+    base = tok_ref[p.wt].astype(f32)
+    d_normed = dn_sum.own()
+    gt_ref[p.wt] = (d_middle + norm_back(base, rms_of(base), gain_in_ref[...], d_normed)).astype(bf16)
+    gt_gather.start()
+    for i in range(3):
+        for h in range(2):
+            sums_back.put(i, h, sums.own(i, h).astype(bf16))
+            sums_back.first(i, h)
+    vx[0] = vec_total(vw, round1)
+    round2 = vec_round(vx, [p.along_x(d) for d in ORDER], vs2, vr2)
+    for i in range(3):
+        for h in range(2):
+            sums_back.second(i, h)
+    vy[0] = vec_total(vx, round2)
+    round3 = vec_round(vy, [p.along_y(d) for d in ORDER], vs3, vr3)
+    gt_gather.forward()
+    vec_ref[...] = vec_total(vy, round3)
+    out_gather.arrived()
+    gt_gather.arrived()
+    for part in (d_mid_sum, da_gather, mlp_sum, out_gather, ff, ff_back, dn_sum, gt_gather, sums, sums_back, flow):
+        part.finish()
+
+
+def backward(parts, *args):
+    rows = pltpu.VMEM
+    wt_rows = [rows((4, 64, 1024), bf16), rows((3, 64, 1024), bf16), rows((3, 64, 1024), bf16)]
+    wt_sum = wt_rows + WT_SEMS[:4]
+    wt_gather = WT_SEMS[4:]
+    half = rows((2, 256, 128), bf16)
+    return comm_call(
+        functools.partial(backward_kernel, parts), 4,
+        (sds((8, 64, 1024), bf16), sds((8, 64, 1024), bf16), sds((3, 4, 32, 1024), bf16), sds((3, 4, 144, 1024), bf16),
+         sds((8, 1024), f32)),
+        args,
+        [rows((8, 64, 1024), bf16), rows((256, 128), bf16), half] + [DMA] * 4
+        + wt_sum + wt_gather + wt_sum + wt_gather
+        + SpScatter.scratch(3, 144) + SpGather.sems(3)
+        + [rows((512, 256), bf16), rows((8192, 128), f32), rows((64, 512), f32), half, half,
+           rows((4, 4, 2, 256, 128), bf16), half]
+        + [rows((2, 3, 4, 256, 128), bf16), rows((2, 3, 256, 128), bf16), rows((2, 3, 256, 128), bf16)]
+        + [DMA((2, 3))] * 4
+        + [rows((8, 64, 1024), bf16), rows((2, 4, 32, 1024), bf16), rows((4, 32, 1024), bf16)]
+        + wt_sum + wt_gather
+        + SpScatter.scratch(3, 32) + SpGather.sems(3)
+        + [rows((8, 8, 1024), f32), rows((4, 8, 1024), f32), rows((4, 8, 1024), f32),
+           DMA((7,)), DMA((7,)), DMA((3,)), DMA((3,)), DMA((3,)), DMA((3,))],
+        "backward", 36,
+    )
+
+
 def finish_kernel(sums_ref, ff_ref, out_in, gt_in, vec_ref, out_ref, gt_ref, gq_ref, gk_ref, gv_ref, go_ref, gg_ref, gu_ref, gd_ref,
                   ni_ref, nm_ref, qg_ref, kg_ref, wide, tall, big, sems):
     copies = []
@@ -921,11 +899,12 @@
             rows = pl.ds(part * 288, 288)
             big[i, rows, :] = ff_ref[i, rows, :].astype(f32)
             write(big.at[i, rows], ref.at[rows])
-    wide[...] = sums_ref[1:3].astype(f32)
-    write(wide.at[0, 0:64], gk_ref)
-    write(wide.at[0, 64:128], gv_ref)
-    write(wide.at[1], go_ref)
-    tall[...] = sums_ref[0].astype(f32).T
+    wide[0] = sums_ref[0].astype(f32)
+    wide[1] = sums_ref[2].astype(f32)
+    write(wide.at[1, 0:64], gk_ref)
+    write(wide.at[1, 64:128], gv_ref)
+    write(wide.at[0], go_ref)
+    tall[...] = sums_ref[1].astype(f32).T
     write(tall, gq_ref)
     ni_ref[...] = vec_ref[0:1, :]
     nm_ref[...] = vec_ref[1:2, :]
@@ -992,19 +971,13 @@
         jnp.einsum("tf,td->fd", d_up, normed_mid, preferred_element_type=f32).astype(bf16),
         jnp.einsum("tf,td->fd", act, cotangent, preferred_element_type=f32).astype(bf16),
     )
-    d_attn, d_middle_own, gn, d_mix_z, red = turn_back(
-        d_mid_part, mid_own, cotangent, norm_mid, w_out, grads
-    )
-    g_out = jnp.einsum("tq,td->qd", mixed, d_attn.reshape(512, 1024), preferred_element_type=f32).astype(bf16)
-    dq_z, dkv_all, g_ff = attend_back(parts, qa, mix_f, d_mix_z.reshape(512, 128), kv_all, ext, red)
-    dkv, dq, output = scatter_keys(dkv_all, dq_z, mlp_part, mid_own)
-    dn_part, g_qkv, gg = local_call(
-        proj_back_kernel,
-        (sds((512, 1024), bf16), sds((2, 128, 1024), bf16), sds((1, 1024), f32)),
-        (dq.reshape(512, 128), dkv.reshape(512, 128), q_proj, kv_proj, normed, w_query, wk, wv, qg, kg, cosine, sine),
-        "project_back",
-    )
-    grad_tokens, sums, vec = last_sums(dn_part, g_qkv, g_out, tokens, d_middle_own, norm_in, gn, gg)
+    output, grad_tokens, sums, g_ff, vec = backward(
+        parts,
+        d_mid_part.reshape(8, 64, 1024), mlp_part.reshape(8, 64, 1024), mid_own, cotangent.reshape(8, 64, 1024),
+        norm_mid.reshape(1, 1024), w_out, *(g.reshape(4, 144, 1024) for g in grads),
+        qa, mix_f, kv_all, ext, mixed,
+        q_proj, kv_proj, normed, w_query, wk, wv, qg, kg, cosine, sine, tokens.reshape(8, 64, 1024), norm_in.reshape(1, 1024),
+    )
     (output, grad_tokens, g_query, g_key, g_value, g_out, g_gate, g_up, g_down, g_norm_in, g_norm_mid, g_qg, g_kg) = finish(
         sums.reshape(3, 128, 1024), g_ff.reshape(3, 576, 1024), output.reshape(512, 1024), grad_tokens.reshape(512, 1024), vec
     )

time: 188 us -> 186 us (0.989)
  Pallas kernels: 176 us -> 171 us
  local copies, waits for them, and re-layouts: 0.39 us -> 2.36 us
    pallas_call x1 -> x0, Pallas kernels: 27.9 us -> none  [attend_back(): pl.pallas_call(functools.partial(bwd_kernel, parts), out_shape=(sds((rows...]
    pallas_call x5 -> x3, Pallas kernels: 129 us -> 154 us  [comm_call(): pl.pallas_call(kernel, out_shape=out_shape, in_specs=[first or vmem] + [v...]
    pallas_call x2 -> x1, Pallas kernels: 5.39 us -> 2.86 us  [local_call(): pl.pallas_call(kernel, out_shape=out_shape, in_specs=[first or vmem] + [v...]
    unnamed x30 -> x34, local copies, waits for them, and re-layouts: 0.32 us -> 2.29 us
where the time goes in v4:
time: 186 us; the launch traced here: 184 us
  Pallas kernels  171 us (92%)
  matrix products  10.1 us (5%)
  local copies, waits for them, and re-layouts  2.36 us (1%)
    pallas_call x3, Pallas kernels, comm_call(): pl.pallas_call(kernel, out_shape=out_shape, in_specs=[first or vmem] + [v...  154 us
    pallas_call x1, Pallas kernels, attend(): pl.pallas_call(functools.partial(fwd_kernel, parts), out_shape=(sds((rows...  9.28 us
    pallas_call x1, Pallas kernels, finish(): pl.pallas_call(finish_kernel, out_shape=(sds((512, 1024), bf16), sds((512...  4.71 us

profile of v4, /device:TPU:1, one launch (start us, length us, event | category | flops | bytes accessed | tf_op | source)
XLA Modules:
  0.0 184.5 jit_solution(10845383752769988506)
XLA Ops:
  0.6 0.0 copy-start
  0.7 0.0 copy-start.14
  0.7 0.0 copy-start.2
  0.7 0.0 copy-start.4
  0.7 0.0 copy-start.6
  0.7 0.0 copy-start.7
  0.7 0.0 copy-start.8
  0.7 0.0 copy-start.10
  0.7 0.0 copy-start.11
  0.7 0.0 copy-start.12
  0.8 2.5 %fusion = f32[512,576]{0,1:T(8,128)S(1)} fusion(bf16[512,1024]{1,0:T(8,128)(2,1)} %param.27, bf16[576,1024]{1,0:T(8,128)(2,1)} %param.26), kind=kOutput, calls=%fused_computation.9 | convolution fusion | flops 603979776 | bytes 3407872 | tf_op jit(solution)/shard_map/td,fd->tf/dot_general | solution.py:962
  3.3 0.0 copy-done.14
  3.3 0.1 jit_solution_.3.freq_ref
  3.4 0.0 copy-done.2
  3.4 0.0 copy-done.4
  3.4 0.0 copy-done.6
  3.4 0.0 copy-done.7
  3.4 0.0 copy-done.8
  3.4 0.0 copy-done.10
  3.4 0.0 copy-done.11
  3.4 0.0 copy-done.12
  3.5 2.9 %project.1 = (bf16[512,1024]{1,0:T(8,128)(2,1)S(1)}, f32[512,128]{1,0:T(8,128)S(1)}, f32[512,128]{1,0:T(8,128)S(1)}, bf16[512,128]{1,0:T(8,128)(2,1)S(1)}, bf16[...) custom-call(s32[4]{0:T(128)S(1)} %copy-done.10, bf16[512,1024]{1,0:T(8,128)(2,1)S(1)} %copy-done.2, ...), custom_call_target="tpu_custom_call" | custom-call | flops 3221225472 | bytes 16777216 | tf_op jit(solution)/shard_map/project/pallas_call | solution.py:577
  6.3 23.8 %gather_keys.1 = (bf16[2,256,128]{2,1,0:T(8,128)(2,1)S(1)}, bf16[4,4,2,256,128]{4,3,2,1,0:T(8,128)(2,1)S(1)}, bf16[8192,128]{1,0:T(8,128)(2,1)S(1)}) custom-call(s32[4]{0:T(128)S(1)} %copy-done.10, bf16[2,256,128]{2,1,0:T(8,128)(2,1)S(1)} %bitcast.81, bf16[2,256,128]{2,1,0:T(8,128)(2,1)S(1)} %bitcast.82), custom_call_target="tpu_custom_call" | custom-call | flops 8589934592 | bytes 33554432 | tf_op jit(solution)/shard_map/gather_keys/pallas_call | solution.py:492
  30.1 0.0 copy-start.13
  30.1 0.0 copy-start.5
  30.1 0.0 copy-start.9
  30.2 9.3 %attend.1 = (bf16[512,128]{1,0:T(8,128)(2,1)S(1)}, f32[512,128]{1,0:T(8,128)S(1)}, bf16[2,512,256]{2,1,0:T(8,128)(2,1)S(1)}) custom-call(s32[4]{0:T(128)S(1)} %copy-done.10, bf16[512,128]{1,0:T(8,128)(2,1)S(1)} %bitcast.83, bf16[8192,128]{1,0:T(8,128)(2,1)S(1)} %bitcast.69, bf16[8192,128]{1,0:T(8,128)(2,1)S(1)} %get-tuple-element.51.ext_ref), custom_call_target="tpu_custom_call" | custom-call | flops 3221225472 | bytes 4194304 | tf_op jit(solution)/shard_map/attend/pallas_call | solution.py:134
  39.4 0.0 copy-done.13
  39.4 0.0 copy-done.5
  39.5 0.0 copy-done.9
  39.5 0.0 copy-start.16
  39.5 28.4 %make_middle.1 = (bf16[8,64,1024]{2,1,0:T(8,128)(2,1)S(1)}, f32[64,1024]{1,0:T(8,128)S(1)}, bf16[2,256,128]{2,1,0:T(8,128)(2,1)S(1)}) custom-call(bf16[2,256,128]{2,1,0:T(8,128)(2,1)S(1)} %bitcast.84, bf16[128,1024]{1,0:T(8,128)(2,1)S(1)} %copy-done.5, bf16[8,64,1024]{2,1,0:T(8,128)(2,1)S(1)} %bitcast.54, f32[1,1024]{1,0:T(1,128)S(1)} %bitcast.63), custom_call_target="tpu_custom_call" | custom-call | flops 8589934592 | bytes 33554432 | tf_op jit(solution)/shard_map/make_middle/pallas_call | solution.py:492
  67.9 0.0 copy-done.16
  67.9 0.9 fusion.1
  68.8 0.0 copy-done
  68.8 0.0 copy-start.15
  68.8 1.3 multiply_convert_fusion
  70.1 0.0 copy-done.15
  70.1 0.0 copy-start.3
  70.1 1.0 convolution_convert_fusion.3
  71.1 0.2 copy-done.3
  71.3 0.8 convolution_convert_fusion
  72.1 0.8 convolution_convert_fusion.2
  72.9 0.8 convolution_convert_fusion.1
  73.7 1.0 fusion.2
  74.7 1.0 add_convert_fusion
  75.7 101.8 %backward.1 = (bf16[8,64,1024]{2,1,0:T(8,128)(2,1)S(1)}, bf16[8,64,1024]{2,1,0:T(8,128)(2,1)S(1)}, bf16[3,4,32,1024]{3,2,1,0:T(8,128)(2,1)S(1)}, bf16[3,4,144,1024]{3,2,1,0:T(8,128)(2,1)}, f32[8,1024]{1,0:T(8,128)S(1)}) custom-call(bf16[8,64,1024]{2,1,0:T(8,128)(2,1)S(1)} %bitcast.75, bf16[8,64,1024]{2,1,0:T(8,128)(2,1)S(1)} %bitcast.74, ...), custom_call_target="tpu_custom_call" | custom-call | flops 8589934592 | bytes 33554432 | tf_op jit(solution)/shard_map/backward/pallas_call | solution.py:492
  177.6 0.0 copy-start.1
  177.6 2.0 %copy-done.1 = bf16[3,4,144,1024]{3,2,1,0:T(8,128)(2,1)S(1)} copy-done((bf16[3,4,144,1024]{3,2,1,0:T(8,128)(2,1)S(1)}, bf16[3,4,144,1024]{3,2,1,0:T(8,128)(2,1)}, u32[]{:S(2)}) %copy-start.1) | copy-done | bytes 3538968
  179.6 4.7 %finish.1 = (bf16[512,1024]{1,0:T(8,128)(2,1)}, bf16[512,1024]{1,0:T(8,128)(2,1)}, f32[1024,128]{1,0:T(8,128)}, f32[64,1024]{1,0:T(8,128)}, f32[64,1024]{1,0:T(8...) custom-call(bf16[3,128,1024]{2,1,0:T(8,128)(2,1)S(1)} %bitcast.53, ...), custom_call_target="tpu_custom_call" | custom-call | tf_op jit(solution)/shard_map/finish/pallas_call | solution.py:920
Async XLA Ops:
  0.6 68.1 %copy-start = (bf16[1024,576]{0,1:T(8,128)(2,1)S(1)}, bf16[1024,576]{0,1:T(8,128)(2,1)}, u32[]{:S(2)}) copy-start(bf16[1024,576]{0,1:T(8,128)(2,1)} %param.25) | copy-start | bytes 3538948
  0.7 2.6 %copy-start.14 = (f32[32]{0:T(128)S(1)}, f32[32]{0:T(128)}, u32[]{:S(2)}) copy-start(f32[32]{0:T(128)} %constant.4.clone) | copy-start | bytes 388
  0.7 2.7 %copy-start.2 = (bf16[512,1024]{1,0:T(8,128)(2,1)S(1)}, bf16[512,1024]{1,0:T(8,128)(2,1)}, u32[]{:S(2)}) copy-start(bf16[512,1024]{1,0:T(8,128)(2,1)} %tok_ref.1) | copy-start | bytes 3145732
  0.7 2.7 %copy-start.4 = (bf16[1024,128]{1,0:T(8,128)(2,1)S(1)}, bf16[1024,128]{1,0:T(8,128)(2,1)}, u32[]{:S(2)}) copy-start(bf16[1024,128]{1,0:T(8,128)(2,1)} %wq_ref.3) | copy-start | bytes 786436
  0.7 2.7 %copy-start.6 = (bf16[1024,64]{0,1:T(8,128)(2,1)S(1)}, bf16[1024,64]{0,1:T(8,128)(2,1)}, u32[]{:S(2)}) copy-start(bf16[1024,64]{0,1:T(8,128)(2,1)} %param.18) | copy-start | bytes 393220
  0.7 2.7 %copy-start.7 = (bf16[1024,64]{0,1:T(8,128)(2,1)S(1)}, bf16[1024,64]{0,1:T(8,128)(2,1)}, u32[]{:S(2)}) copy-start(bf16[1024,64]{0,1:T(8,128)(2,1)} %param.19) | copy-start | bytes 393220
  0.7 2.7 %copy-start.8 = (f32[1024]{0:T(1024)S(1)}, f32[1024]{0:T(1024)}, u32[]{:S(2)}) copy-start(f32[1024]{0:T(1024)} %param.16) | copy-start | bytes 12292
  0.7 2.7 %copy-start.10 = (s32[4]{0:T(128)S(1)}, s32[4]{0:T(128)}, u32[]{:S(2)}) copy-start(s32[4]{0:T(128)} %len_ref.5) | copy-start | bytes 52
  0.7 2.7 %copy-start.11 = (f32[64]{0:T(128)S(1)}, f32[64]{0:T(128)}, u32[]{:S(2)}) copy-start(f32[64]{0:T(128)} %param.20) | copy-start | bytes 772
  0.7 2.7 %copy-start.12 = (f32[64]{0:T(128)S(1)}, f32[64]{0:T(128)}, u32[]{:S(2)}) copy-start(f32[64]{0:T(128)} %param.21) | copy-start | bytes 772
  30.1 9.3 %copy-start.13 = (bf16[8192,128]{1,0:T(8,128)(2,1)}, bf16[8192,128]{1,0:T(8,128)(2,1)S(1)}, u32[]{:S(2)}) copy-start(bf16[8192,128]{1,0:T(8,128)(2,1)S(1)} %get-tuple-element.51.ext_ref) | copy-start | bytes 6291460
  30.1 9.3 %copy-start.5 = (bf16[128,1024]{1,0:T(8,128)(2,1)S(1)}, bf16[128,1024]{1,0:T(8,128)(2,1)}, u32[]{:S(2)}) copy-start(bf16[128,1024]{1,0:T(8,128)(2,1)} %w_ref.3) | copy-start | bytes 786436
  30.1 9.3 %copy-start.9 = (f32[1024]{0:T(1024)S(1)}, f32[1024]{0:T(1024)}, u32[]{:S(2)}) copy-start(f32[1024]{0:T(1024)} %param.23) | copy-start | bytes 12292
  39.5 28.4 %copy-start.16 = (bf16[1024,576]{0,1:T(8,128)(2,1)S(1)}, bf16[1024,576]{0,1:T(8,128)(2,1)}, u32[]{:S(2)}) copy-start(bf16[1024,576]{0,1:T(8,128)(2,1)} %param.24) | copy-start | bytes 3538948
  68.8 1.3 copy-start.15
  70.1 1.2 copy-start.3
  177.6 2.0 %copy-start.1 = (bf16[3,4,144,1024]{3,2,1,0:T(8,128)(2,1)S(1)}, bf16[3,4,144,1024]{3,2,1,0:T(8,128)(2,1)}, u32[]{:S(2)}) copy-start(bf16[3,4,144,1024]{3,2,1,0:T(8,128)(2,1)} %get-tuple-element.64) | copy-start | bytes 10616836

commit v5 on v4

--- a/solution.py
+++ b/solution.py
@@ -83,64 +83,8 @@
     return jnp.where((lane < 3) | (lane > 6) | within, 0.0, -FAR)
 
 
-def fwd_kernel(parts, len_ref, q_ref, kv_ref, ext_ref, mix_ref, out_ref, qa_ref, acc_ref):
-    me = lax.axis_index("sp")
-    lane = lanes((HALF, 128))
-    lane2 = lanes((2 * HALF, 128))
-    lanek = lanes((CH, 128))
-    for t in range(2):
-        r0 = tile_row(me, t, parts)
-        q = q_ref[t * HALF:(t + 1) * HALF, :].astype(f32)
-        qa_ref[t, 0:HALF, 0:128] = jnp.where(lane < 64, q, 0.0).astype(bf16)
-        qa_ref[t, HALF:, 0:128] = jnp.where(lane < 64, pltpu.roll(q, 64, 1), 0.0).astype(bf16)
-        columns = query_columns(r0, len_ref, HALF)
-        columns = jnp.concatenate([columns, columns], axis=0)
-        qa_ref[t, :, 128:256] = columns.astype(bf16)
-        acc_ref[...] = jnp.zeros_like(acc_ref)
-
-        def step(c, masked):
-            k0 = pl.multiple_of(c * CH, CH)
-            kv = kv_ref[pl.ds(k0, CH), :]
-            kva = jnp.concatenate([kv, ext_ref[pl.ds(k0, CH), :]], axis=1)
-            s = lax.dot_general(qa_ref[t], kva, (((1,), (1,)), ((), ())), preferred_element_type=f32)
-            p = jnp.exp2(s * C2)
-            if masked:
-                rows = r0 + lax.rem(lax.broadcasted_iota(jnp.int32, (2 * HALF, 1), 0), HALF)
-                keys = k0 + lax.broadcasted_iota(jnp.int32, (2 * HALF, CH), 1)
-                p = jnp.where(keys <= rows, p, 0.0)
-            ones = jnp.where(lanek < 64, jnp.ones_like(kv), kv)
-            acc_ref[...] += jnp.dot(p.astype(bf16), ones, preferred_element_type=f32)
-
-        block = me if t == 0 else parts - 1 - me
-        pl.loop(0, block)(lambda c: step(c, False))
-        step(block, True)
-
-        acc = acc_ref[...]
-        swapped = pltpu.roll(acc, 64, 1)
-        o = swapped / acc
-        m = jnp.where(lane < 64, o[:HALF], pltpu.roll(o[HALF:], 64, 1))
-        mix_ref[t * HALF:(t + 1) * HALF, :] = m.astype(bf16)
-        out_ref[t * HALF:(t + 1) * HALF, :] = m
-        total = jnp.where(lane2 < 64, acc, swapped)
-        qa_ref[t, :, 128:256] = (split3(jnp.log(total) * (-1.0 / SCALE), lane2) + columns).astype(bf16)
-
-
 smem = pl.BlockSpec(memory_space=pltpu.SMEM)
 vmem = pl.BlockSpec(memory_space=pltpu.VMEM)
-
-
-def attend(parts, lengths, q, kv, ext):
-    rows = 2 * HALF
-    return pl.pallas_call(
-        functools.partial(fwd_kernel, parts),
-        out_shape=(sds((rows, 128), bf16), sds((rows, 128), f32), sds((2, rows, 256), bf16)),
-        in_specs=[smem, vmem, vmem, vmem],
-        out_specs=(vmem, vmem, vmem),
-        scratch_shapes=[pltpu.VMEM((rows, 128), f32)],
-        compiler_params=pltpu.CompilerParams(vmem_limit_bytes=12 << 20),
-        cost_estimate=pl.CostEstimate(flops=3 << 30, bytes_accessed=4 << 20, transcendentals=5 << 20),
-        name="attend",
-    )(lengths, q, kv, ext)
 
 
 MESH = pl.DeviceIdType.MESH
@@ -199,49 +143,6 @@
 
 
 ORDER = (2, 1, 3)
-
-
-def gather_kernel(len_ref, q_ref, kv_ref, qz_ref, all_ref, ext_ref, ms, mr, fs, fr, ss, sr):
-    p = Place()
-    meet([p.along_x(d) for d in ORDER] + [p.along_y(d) for d in ORDER] + [p.mirror])
-    all_ref[p.x, p.y] = kv_ref[...]
-    mirror = rcopy(q_ref.at[1], qz_ref.at[1], ms, mr, p.mirror)
-    first, second = {}, {}
-    for d in ORDER:
-        for h in range(2):
-            first[h, d] = rcopy(
-                kv_ref.at[h], all_ref.at[p.x, p.y, h], fs.at[h, d - 1], fr.at[h, d - 1], p.first(h, d)
-            )
-            first[h, d].start()
-    mirror.start()
-
-    def forward(h, slot):
-        a = lax.rem(p.fsp(h) + 4 - slot, 4)
-        at = spot(h, a, p.ssp(h))
-        for e in ORDER:
-            src = kv_ref.at[h] if slot == 0 else all_ref.at[at[0], at[1], h]
-            second[h, slot, e] = rcopy(
-                src, all_ref.at[at[0], at[1], h], ss.at[h, slot, e - 1], sr.at[h, slot, e - 1], p.second(h, e)
-            )
-            second[h, slot, e].start()
-
-    for h in range(2):
-        forward(h, 0)
-    qz_ref[0] = q_ref[0]
-    @pl.loop(0, 8)
-    def _(b):
-        rows = pl.ds(pl.multiple_of(b * 1024, 1024), 1024)
-        ext_ref[rows, :] = key_columns(b * 1024, len_ref, 1024)
-
-    for d in (1, 3, 2):
-        for h in range(2):
-            first[h, d].wait_recv()
-            forward(h, d)
-    mirror.wait()
-    for copy in first.values():
-        copy.wait_send()
-    for copy in second.values():
-        copy.wait()
 
 
 class SpScatter:
@@ -365,44 +266,57 @@
             copy.wait()
 
 
+SPLIT = 2
+
+
+def sub(s):
+    return pl.ds(s * (64 // SPLIT), 64 // SPLIT)
+
+
 class WtSum:
     def __init__(self, p, part, sib, send, rz, sems):
         self.p, self.part, self.sib, self.send, self.rz = p, part, sib, send, rz
         self.cs, self.cr, self.zs, self.zr = sems
         self.second = {}
 
-    def core(self, zz):
+    def core(self, zz, s):
         return rcopy(
-            self.part.at[zz * 2 + 1 - self.p.c], self.sib.at[zz], self.cs.at[zz], self.cr.at[zz], self.p.sibling
+            self.part.at[zz * 2 + 1 - self.p.c, sub(s)], self.sib.at[zz, sub(s)],
+            self.cs.at[zz, s], self.cr.at[zz, s], self.p.sibling,
         )
 
     def start_core(self, zz):
-        self.core(zz).start()
-
-    def pair(self, zz):
-        return self.part[zz * 2 + self.p.c].astype(f32) + self.sib[zz].astype(f32)
-
-    def send_z(self, d):
-        zz = lax.rem(self.p.z + d, 4)
-        self.core(zz).wait_recv()
-        self.send[d - 1] = self.pair(zz).astype(bf16)
-        copy = rcopy(
-            self.send.at[d - 1], self.rz.at[d - 1], self.zs.at[d - 1], self.zr.at[d - 1], self.p.along_z(d)
-        )
-        copy.start()
-        self.second[d] = copy
-
-    def own(self):
-        self.core(self.p.z).wait_recv()
-        value = self.pair(self.p.z)
+        for s in range(SPLIT):
+            self.core(zz, s).start()
+
+    def pair(self, zz, s):
+        return self.part[zz * 2 + self.p.c, sub(s)].astype(f32) + self.sib[zz, sub(s)].astype(f32)
+
+    def send_z(self):
+        for s in range(SPLIT):
+            for d in ORDER:
+                zz = lax.rem(self.p.z + d, 4)
+                self.core(zz, s).wait_recv()
+                self.send[d - 1, sub(s)] = self.pair(zz, s).astype(bf16)
+                copy = rcopy(
+                    self.send.at[d - 1, sub(s)], self.rz.at[d - 1, sub(s)],
+                    self.zs.at[d - 1, s], self.zr.at[d - 1, s], self.p.along_z(d),
+                )
+                copy.start()
+                self.second[d, s] = copy
+
+    def own(self, s):
+        self.core(self.p.z, s).wait_recv()
+        value = self.pair(self.p.z, s)
         for d in (1, 3, 2):
-            self.second[d].wait_recv()
-            value = value + self.rz[d - 1].astype(f32)
+            self.second[d, s].wait_recv()
+            value = value + self.rz[d - 1, sub(s)].astype(f32)
         return value
 
     def finish(self):
         for zz in range(4):
-            self.core(zz).wait_send()
+            for s in range(SPLIT):
+                self.core(zz, s).wait_send()
         for copy in self.second.values():
             copy.wait_send()
 
@@ -413,31 +327,29 @@
         self.zs, self.zr, self.gs, self.gr = sems
         self.far, self.near = {}, {}
 
-    def start(self):
+    def start(self, s):
         p = self.p
+        block = self.out.at[p.wt, sub(s)]
         for d in ORDER:
-            self.far[d] = rcopy(
-                self.out.at[p.wt], self.out.at[p.wt], self.zs.at[d - 1], self.zr.at[d - 1], p.along_z(d)
-            )
-            self.far[d].start()
-        self.pass_on(0)
-
-    def pass_on(self, slot):
+            self.far[d, s] = rcopy(block, block, self.zs.at[d - 1, s], self.zr.at[d - 1, s], p.along_z(d))
+            self.far[d, s].start()
+        self.pass_on(0, s)
+
+    def pass_on(self, slot, s):
         p = self.p
-        row = lax.rem(p.z + 4 - slot, 4) * 2 + p.c
-        self.near[slot] = rcopy(
-            self.out.at[row], self.out.at[row], self.gs.at[slot], self.gr.at[slot], p.sibling
-        )
-        self.near[slot].start()
+        block = self.out.at[lax.rem(p.z + 4 - slot, 4) * 2 + p.c, sub(s)]
+        self.near[slot, s] = rcopy(block, block, self.gs.at[slot, s], self.gr.at[slot, s], p.sibling)
+        self.near[slot, s].start()
 
     def forward(self):
-        for d in (1, 3, 2):
-            self.far[d].wait_recv()
-            self.pass_on(d)
+        for s in range(SPLIT):
+            for d in (1, 3, 2):
+                self.far[d, s].wait_recv()
+                self.pass_on(d, s)
 
     def arrived(self):
-        for slot in (0, 1, 3, 2):
-            self.near[slot].wait_recv()
+        for copy in self.near.values():
+            copy.wait_recv()
 
     def finish(self):
         for copy in list(self.far.values()) + list(self.near.values()):
@@ -458,34 +370,184 @@
     return [p.sibling] + [p.along_z(d) for d in ORDER]
 
 
-def middle_kernel(mix_ref, w_ref, tok_ref, gain_ref, nm_ref, mid_ref, mixo_ref, part, sib, send, rz, ms, mr, cs, cr, zs, zr, az, bz, ag, bg):
+class Flow:
+    def __init__(self):
+        self.copies = []
+
+    def send(self, *args):
+        copy = rcopy(*args)
+        copy.start()
+        self.copies.append(copy)
+        return copy
+
+    def finish(self):
+        for copy in self.copies:
+            copy.wait_send()
+
+
+def forward_kernel(
+    parts,
+    len_ref, q_ref, kv_ref, tok_ref, cot_ref, w_ref, gain_ref,
+    all_ref, ext_ref, qa_ref, mixf_ref, mix_ref, nm_ref, mid_ref, cotz_ref,
+    qz, base, acc, part, sib, send, rz, ms, mr, cs, cr, zs, zr, az, bz, ag, bg, fs, fr, ss, sr,
+):
     p = Place()
-    meet(wt_peers(p) + [p.mirror])
-    mirror = rcopy(mix_ref.at[1], mixo_ref.at[1], ms, mr, p.mirror)
-    mirror.start()
-    mixo_ref[0] = mix_ref[0]
+    me = p.sp
+    meet(wt_peers(p) + [p.along_x(d) for d in ORDER] + [p.along_y(d) for d in ORDER] + [p.mirror])
+    flow = Flow()
+    first = {}
+    for d in ORDER:
+        for h in range(2):
+            first[h, d] = flow.send(
+                kv_ref.at[h], all_ref.at[p.x, p.y, h], fs.at[h, d - 1], fr.at[h, d - 1], p.first(h, d)
+            )
+    q_mirror = flow.send(q_ref.at[1], qz.at[1], ms.at[0], mr.at[0], p.mirror)
+
+    def pass_on(h, slot):
+        a = lax.rem(p.fsp(h) + 4 - slot, 4)
+        at = spot(h, a, p.ssp(h))
+        for e in ORDER:
+            src = kv_ref.at[h] if slot == 0 else all_ref.at[at[0], at[1], h]
+            flow.send(src, all_ref.at[at[0], at[1], h], ss.at[h, slot, e - 1], sr.at[h, slot, e - 1], p.second(h, e))
+
+    for h in range(2):
+        pass_on(h, 0)
+    token_mirror = rcopy(tok_ref.at[p.wt], base, ms.at[1], mr.at[1], p.mirror)
+
+    @pl.when(p.wt >= 4)
+    def _():
+        token_mirror.start()
+
+    @pl.when(p.wt < 4)
+    def _():
+        base[...] = tok_ref[p.wt]
+
+    all_ref[p.x, p.y] = kv_ref[...]
+    qz[0] = q_ref[0]
+    cotz_ref[0:4] = cot_ref[0:4]
+
+    @pl.loop(0, 8)
+    def _(b):
+        rows = pl.ds(pl.multiple_of(b * 1024, 1024), 1024)
+        ext_ref[rows, :] = key_columns(b * 1024, len_ref, 1024)
+
+    lane = lanes((HALF, 128))
+    lane2 = lanes((2 * HALF, 128))
+    lanek = lanes((CH, 128))
+    acc[...] = jnp.zeros_like(acc)
+    blocks = (me, parts - 1 - me)
+    begins = (me * 512, (parts - 1 - me) * 512 + HALF)
+
+    def prepare(t):
+        q = qz[t].astype(f32)
+        qa_ref[t, 0:HALF, 0:128] = jnp.where(lane < 64, q, 0.0).astype(bf16)
+        qa_ref[t, HALF:, 0:128] = jnp.where(lane < 64, pltpu.roll(q, 64, 1), 0.0).astype(bf16)
+        columns = query_columns(begins[t], len_ref, HALF).astype(bf16)
+        qa_ref[t, 0:HALF, 128:256] = columns
+        qa_ref[t, HALF:, 128:256] = columns
+
+    def step(t, x, y, masked):
+        k0 = pl.multiple_of((x * 4 + y) * CH, CH)
+        kv = all_ref[x, y].reshape(CH, 128)
+        kva = jnp.concatenate([kv, ext_ref[pl.ds(k0, CH), :]], axis=1)
+        pr = jnp.exp2(nt(qa_ref[t], kva) * C2)
+        if masked:
+            rows = begins[t] + lax.rem(lax.broadcasted_iota(jnp.int32, (2 * HALF, 1), 0), HALF)
+            keys = k0 + lax.broadcasted_iota(jnp.int32, (2 * HALF, CH), 1)
+            pr = jnp.where(keys <= rows, pr, 0.0)
+        ones = jnp.where(lanek < 64, jnp.ones_like(kv), kv)
+        acc[t] += jnp.dot(pr.astype(bf16), ones, preferred_element_type=f32)
+
+    def both(x, y):
+        block = x * 4 + y
+
+        @pl.when(block < blocks[0])
+        def _():
+            step(0, x, y, False)
+
+        @pl.when(block < blocks[1])
+        def _():
+            step(1, x, y, False)
+
+        @pl.when(block == blocks[1])
+        def _():
+            step(1, x, y, True)
+
+    prepare(0)
+    step(0, p.x, p.y, True)
+    for d in (1, 3, 2):
+        for h in range(2):
+            first[h, d].wait_recv()
+            pass_on(h, d)
+    q_mirror.wait_recv()
+    prepare(1)
+
+    @pl.when(me < blocks[1])
+    def _():
+        step(1, p.x, p.y, False)
+
+    def wait_for(x, y, h, slot, e):
+        block = all_ref.at[x, y, h]
+        rcopy(block, block, ss.at[h, slot, e - 1], sr.at[h, slot, e - 1], p.second(h, 1)).wait_recv()
+
+    @pl.loop(1, 4)
+    def _(d):
+        x = lax.rem(p.x + 4 - d, 4)
+        wait_for(x, p.y, 1, 0, d)
+        both(x, p.y)
+
+    @pl.loop(1, 4)
+    def _(d):
+        y = lax.rem(p.y + 4 - d, 4)
+        wait_for(p.x, y, 0, 0, d)
+        both(p.x, y)
+
+    @pl.loop(0, 9)
+    def _(k):
+        dx, dy = 1 + lax.div(k, 3), 1 + lax.rem(k, 3)
+        x, y = lax.rem(p.x + 4 - dx, 4), lax.rem(p.y + 4 - dy, 4)
+        wait_for(x, y, 0, dx, dy)
+        wait_for(x, y, 1, dy, dx)
+        both(x, y)
+
     total = WtSum(p, part, sib, send, rz, (cs, cr, zs, zr))
-    for half in range(2):
-        if half == 1:
-            mirror.wait()
-        both = jnp.dot(mixo_ref[half], w_ref[...], preferred_element_type=f32).astype(bf16)
-        part[half * 4:half * 4 + 4] = both.reshape(4, 64, 1024)
-        for zz in (half * 2, half * 2 + 1):
+    cot_mirror = flow.send(cot_ref.at[pl.ds(4, 4)], cotz_ref.at[pl.ds(4, 4)], ms.at[2], mr.at[2], p.mirror)
+    for t in range(2):
+        value = acc[t]
+        swapped = pltpu.roll(value, 64, 1)
+        o = swapped / value
+        mix = jnp.where(lane < 64, o[:HALF], pltpu.roll(o[HALF:], 64, 1))
+        mixf_ref[t] = mix
+        mix = mix.astype(bf16)
+        mix_ref[t] = mix
+        part[t * 4:t * 4 + 4] = jnp.dot(mix, w_ref[...], preferred_element_type=f32).astype(bf16).reshape(4, 64, 1024)
+        for zz in (t * 2, t * 2 + 1):
             total.start_core(zz)
-    for d in ORDER:
-        total.send_z(d)
-    middle = tok_ref[p.wt].astype(f32) + total.own()
-    mid_ref[...] = middle
-    nm_ref[p.wt] = (middle * rms_of(middle) * gain_ref[...]).astype(bf16)
+    total.send_z()
+    for t in range(2):
+        value = acc[t]
+        weights = jnp.where(lane2 < 64, value, pltpu.roll(value, 64, 1))
+        columns = qa_ref[t, :, 128:256].astype(f32)
+        qa_ref[t, :, 128:256] = (split3(jnp.log(weights) * (-1.0 / SCALE), lane2) + columns).astype(bf16)
+
+    @pl.when(p.wt >= 4)
+    def _():
+        token_mirror.wait()
+
     spread = WtGather(p, nm_ref, (az, bz, ag, bg))
-    spread.start()
+    for s in range(SPLIT):
+        middle = base[sub(s)].astype(f32) + total.own(s)
+        mid_ref[sub(s)] = middle
+        nm_ref[p.wt, sub(s)] = (middle * rms_of(middle) * gain_ref[...]).astype(bf16)
+        spread.start(s)
     spread.forward()
+    cot_mirror.wait_recv()
     spread.arrived()
-    spread.finish()
-    total.finish()
-
-
-WT_SEMS = [DMA((4,)), DMA((4,)), DMA((3,)), DMA((3,)), DMA((3,)), DMA((3,)), DMA((4,)), DMA((4,))]
+    for part in (spread, total, flow):
+        part.finish()
+
+
+WT_SEMS = [DMA((n, SPLIT)) for n in (4, 4, 3, 3, 3, 3, 4, 4)]
 
 
 def comm_call(kernel, number, out_shape, args, scratch, name, limit=10, first=None):
@@ -503,25 +565,20 @@
     )(*args)
 
 
-def gather_keys(lengths, q, kv):
+def forward(parts, lengths, q, kv, tokens, cotangent, w_out, gain):
+    rows = pltpu.VMEM
+    half = sds((2, 256, 128), bf16)
+    full = sds((8, 64, 1024), bf16)
     return comm_call(
-        gather_kernel, 1,
-        (sds((2, 256, 128), bf16), sds((4, 4, 2, 256, 128), bf16), sds((8192, 128), bf16)),
-        (lengths, q.reshape(2, 256, 128), kv.reshape(2, 256, 128)),
-        [DMA, DMA, DMA((2, 3)), DMA((2, 3)), DMA((2, 4, 3)), DMA((2, 4, 3))],
-        "gather_keys", 4, smem,
-    )
-
-
-def make_middle(mix, w_out, tokens, gain):
-    rows = pltpu.VMEM
-    return comm_call(
-        middle_kernel, 3,
-        (sds((8, 64, 1024), bf16), sds((64, 1024), f32), sds((2, 256, 128), bf16)),
-        (mix.reshape(2, 256, 128), w_out, tokens.reshape(8, 64, 1024), gain.reshape(1, 1024)),
-        [rows((8, 64, 1024), bf16), rows((4, 64, 1024), bf16), rows((3, 64, 1024), bf16), rows((3, 64, 1024), bf16),
-         DMA, DMA, DMA((4,)), DMA((4,)), DMA((3,)), DMA((3,)), DMA((3,)), DMA((3,)), DMA((4,)), DMA((4,))],
-        "make_middle",
+        functools.partial(forward_kernel, parts), 1,
+        (sds((4, 4, 2, 256, 128), bf16), sds((8192, 128), bf16), sds((2, 512, 256), bf16), sds((2, 256, 128), f32),
+         half, full, sds((64, 1024), f32), full),
+        (lengths, q.reshape(2, 256, 128), kv.reshape(2, 256, 128), tokens.reshape(8, 64, 1024),
+         cotangent.reshape(8, 64, 1024), w_out, gain.reshape(1, 1024)),
+        [rows((2, 256, 128), bf16), rows((64, 1024), bf16), rows((2, 512, 128), f32), rows((8, 64, 1024), bf16),
+         rows((4, 64, 1024), bf16), rows((3, 64, 1024), bf16), rows((3, 64, 1024), bf16), DMA((3,)), DMA((3,))]
+        + WT_SEMS + [DMA((2, 3)), DMA((2, 3)), DMA((2, 4, 3)), DMA((2, 4, 3))],
+        "forward", 16, smem,
     )
 
 
@@ -585,21 +642,6 @@
     )(*args)
 
 
-class Flow:
-    def __init__(self):
-        self.copies = []
-
-    def send(self, *args):
-        copy = rcopy(*args)
-        copy.start()
-        self.copies.append(copy)
-        return copy
-
-    def finish(self):
-        for copy in self.copies:
-            copy.wait_send()
-
-
 def backward_kernel(
     parts,
     dm_ref, mlp_ref, mid_ref, cot_ref, gain_ref, w_ref, g0_ref, g1_ref, g2_ref,
@@ -627,8 +669,8 @@
         sib, send, rz = take(3)
         return WtSum(p, ref, sib, send, rz, take(4))
 
-    da, da_up, dz = take(3)
-    mirror_sems = take(4)
+    da, dz, dmid, dmid_o, out_own = take(5)
+    mirror_sems = take(6)
     d_mid_sum = wt_sum(dm_ref)
     da_gather = WtGather(p, da, take(4))
     mlp_sum = wt_sum(mlp_ref)
@@ -649,46 +691,42 @@
         d_mid_sum.start_core(zz)
     ff.first(0)
     ff.first(1)
-    for d in ORDER:
-        d_mid_sum.send_z(d)
+    d_mid_sum.send_z()
     for zz in range(4):
         mlp_sum.start_core(zz)
-    middle = mid_ref[...]
-    scale = rms_of(middle)
-    d_mid = d_mid_sum.own()
-    d_middle = cot_ref[p.wt].astype(f32) + norm_back(middle, scale, gain_ref[...], d_mid)
-    da[p.wt] = d_middle.astype(bf16)
-    da_gather.start()
     vw[0] = jnp.zeros((8, 1024), f32)
-    vw[0, 1:2] = jnp.sum(d_mid * middle * scale, axis=0, keepdims=True)
+    for s in range(SPLIT):
+        middle = mid_ref[sub(s)]
+        scale = rms_of(middle)
+        d_mid = d_mid_sum.own(s)
+        d_middle = cot_ref[p.wt, sub(s)].astype(f32) + norm_back(middle, scale, gain_ref[...], d_mid)
+        da[p.wt, sub(s)] = d_middle.astype(bf16)
+        da_gather.start(s)
+        dmid[sub(s)] = d_middle
+        vw[0, 1:2] += jnp.sum(d_mid * middle * scale, axis=0, keepdims=True)
+    dmid_mirror = rcopy(dmid, dmid_o, mirror_sems[2], mirror_sems[3], p.mirror)
+
+    @pl.when(p.wt >= 4)
+    def _():
+        dmid_mirror.start()
+
+    mlp_sum.send_z()
     ff.second(0)
     da_gather.forward()
+    acc[...] = jnp.zeros_like(acc)
     da_gather.arrived()
-    for half in (1, 0):
-        rows = da[half * 4:half * 4 + 4].reshape(256, 1024)
-        d_mixed = nt(rows, w_ref[...]).astype(bf16)
-        if half == 1:
-            da_up[...] = d_mixed
-            mirror = flow.send(da_up, dz.at[1], mirror_sems[0], mirror_sems[1], p.mirror)
-        else:
-            dz[0] = d_mixed
+    dz[...] = nt(da[...].reshape(512, 1024), w_ref[...]).astype(bf16).reshape(2, 256, 128)
     ff.first(2)
-    for d in ORDER:
-        mlp_sum.send_z(d)
-    gout[...] = tn(mixed_ref[...], da[...].reshape(512, 1024)).astype(bf16).reshape(4, 32, 1024)
     ff.second(1)
-    mirror.wait_recv()
 
     lane = lanes((HALF, 128))
-    acc[...] = jnp.zeros_like(acc)
     upper_long = (me < parts // 2).astype(jnp.int32)
     for turn in range(2):
         t = upper_long if turn == 0 else 1 - upper_long
         block = me + t * (parts - 1 - 2 * me)
         r0 = block * 512 + t * HALF
-        rows_t = pl.ds(pl.multiple_of(t * HALF, HALF), HALF)
         do = dz[t].astype(f32)
-        prod = do * mixf_ref[rows_t, :]
+        prod = do * mixf_ref[t]
         d0 = -jnp.sum(jnp.where(lane < 64, prod, 0.0), axis=1, keepdims=True)
         d1 = -jnp.sum(jnp.where(lane < 64, 0.0, prod), axis=1, keepdims=True)
         dab[0:HALF, 0:128] = jnp.where(lane < 64, 0.0, pltpu.roll(do, 64, 1)).astype(bf16)
@@ -726,15 +764,32 @@
                     ff_back.put(i, h, ff.own(i, h).astype(bf16))
                     ff_back.first(i, h)
             ff.second(2)
-            out_ref[p.wt] = (middle + mlp_sum.own()).astype(bf16)
-            out_gather.start()
+            for s in range(SPLIT):
+                out_own[sub(s)] = (mid_ref[sub(s)] + mlp_sum.own(s)).astype(bf16)
+            out_mirror = rcopy(out_own, out_ref.at[p.wt], mirror_sems[4], mirror_sems[5], p.mirror)
+
+            @pl.when(p.wt >= 4)
+            def _():
+                out_mirror.start()
+
+            @pl.when(p.wt < 4)
+            def _():
+                out_ref[p.wt] = out_own[...]
+
+            gout[...] = tn(mixed_ref[...].reshape(512, 128), da[...].reshape(512, 1024)).astype(bf16).reshape(4, 32, 1024)
             pl.loop(4, 8)(plain)
             for h in range(2):
                 ff_back.put(2, h, ff.own(2, h).astype(bf16))
                 ff_back.first(2, h)
             for h in range(2):
                 ff_back.second(0, h)
-            out_gather.forward()
+
+            @pl.when(p.wt >= 4)
+            def _():
+                out_mirror.wait()
+
+            for s in range(SPLIT):
+                out_gather.start(s)
             pl.loop(8, block)(plain)
         else:
             pl.loop(0, block)(plain)
@@ -748,7 +803,7 @@
         rows = pl.ds(pl.multiple_of(b * 512, 512), 512)
         dkv[lax.div(b, 4), lax.rem(b, 4)] = (acc[rows, :] * weight).astype(bf16).reshape(2, 256, 128)
 
-    mirror = flow.send(dqz.at[1], dq.at[1], mirror_sems[2], mirror_sems[3], p.mirror)
+    mirror = flow.send(dqz.at[1], dq.at[1], mirror_sems[0], mirror_sems[1], p.mirror)
     dq[0] = dqz[0]
     first, second = {}, {}
     for d in ORDER:
@@ -772,6 +827,7 @@
             second[h, e] = flow.send(
                 send1.at[h, e - 1], r2.at[h, e - 1], ss.at[h, e - 1], sr.at[h, e - 1], p.second(h, e)
             )
+    out_gather.forward()
     for h in range(2):
         ff_back.second(1, h)
     for h in range(2):
@@ -807,8 +863,7 @@
     gqkv[1] = tn(d_kv, normed).astype(bf16).reshape(4, 32, 1024)
     for i in range(3):
         sums.first(i)
-    for d in ORDER:
-        dn_sum.send_z(d)
+    dn_sum.send_z()
 
     gains = jnp.zeros((1, 1024), f32)
     for w in range(8):
@@ -834,10 +889,22 @@
         ff_back.second(2, h)
     for i in range(3):
         sums.second(i)
-    base = tok_ref[p.wt].astype(f32)
-    d_normed = dn_sum.own()
-    gt_ref[p.wt] = (d_middle + norm_back(base, rms_of(base), gain_in_ref[...], d_normed)).astype(bf16)
-    gt_gather.start()
+
+    @pl.when(p.wt >= 4)
+    def _():
+        dmid_mirror.wait()
+
+    @pl.when(p.wt < 4)
+    def _():
+        dmid_o[...] = dmid[...]
+
+    for s in range(SPLIT):
+        base = tok_ref[p.wt, sub(s)].astype(f32)
+        d_normed = dn_sum.own(s)
+        gt_ref[p.wt, sub(s)] = (
+            dmid_o[sub(s)] + norm_back(base, rms_of(base), gain_in_ref[...], d_normed)
+        ).astype(bf16)
+        gt_gather.start(s)
     for i in range(3):
         for h in range(2):
             sums_back.put(i, h, sums.own(i, h).astype(bf16))
@@ -868,7 +935,7 @@
         (sds((8, 64, 1024), bf16), sds((8, 64, 1024), bf16), sds((3, 4, 32, 1024), bf16), sds((3, 4, 144, 1024), bf16),
          sds((8, 1024), f32)),
         args,
-        [rows((8, 64, 1024), bf16), rows((256, 128), bf16), half] + [DMA] * 4
+        [rows((8, 64, 1024), bf16), half, rows((64, 1024), f32), rows((64, 1024), f32), rows((64, 1024), bf16)] + [DMA] * 6
         + wt_sum + wt_gather + wt_sum + wt_gather
         + SpScatter.scratch(3, 144) + SpGather.sems(3)
         + [rows((512, 256), bf16), rows((8192, 128), f32), rows((64, 512), f32), half, half,
@@ -885,7 +952,7 @@
 
 
 def finish_kernel(sums_ref, ff_ref, out_in, gt_in, vec_ref, out_ref, gt_ref, gq_ref, gk_ref, gv_ref, go_ref, gg_ref, gu_ref, gd_ref,
-                  ni_ref, nm_ref, qg_ref, kg_ref, wide, tall, big, sems):
+                  ni_ref, nm_ref, qg_ref, kg_ref, wide, tall, big, ff, sems, load_sems):
     copies = []
 
     def write(src, dst):
@@ -894,10 +961,14 @@
 
     write(out_in, out_ref)
     write(gt_in, gt_ref)
+    loads = [pltpu.make_async_copy(ff_ref.at[i], ff.at[i], load_sems.at[i]) for i in range(3)]
+    for load in loads:
+        load.start()
     for i, ref in enumerate((gg_ref, gu_ref, gd_ref)):
+        loads[i].wait()
         for part in range(2):
             rows = pl.ds(part * 288, 288)
-            big[i, rows, :] = ff_ref[i, rows, :].astype(f32)
+            big[i, rows, :] = ff[i, rows, :].astype(f32)
             write(big.at[i, rows], ref.at[rows])
     wide[0] = sums_ref[0].astype(f32)
     wide[1] = sums_ref[2].astype(f32)
@@ -922,10 +993,10 @@
         out_shape=(sds((512, 1024), bf16), sds((512, 1024), bf16), sds((1024, 128), f32), sds((64, 1024), f32), sds((64, 1024), f32),
                    sds((128, 1024), f32), rows, rows, rows,
                    sds((1, 1024), f32), sds((1, 1024), f32), sds((1, 64), f32), sds((1, 64), f32)),
-        in_specs=[vmem] * 5,
+        in_specs=[vmem, hbm, vmem, vmem, vmem],
         out_specs=tuple([hbm] * 9 + [vmem] * 4),
-        scratch_shapes=[pltpu.VMEM((2, 128, 1024), f32), pltpu.VMEM((1024, 128), f32), pltpu.VMEM((3, 576, 1024), f32), DMA((12,))],
-        compiler_params=pltpu.CompilerParams(vmem_limit_bytes=14 << 20),
+        scratch_shapes=[pltpu.VMEM((2, 128, 1024), f32), pltpu.VMEM((1024, 128), f32), pltpu.VMEM((3, 576, 1024), f32), pltpu.VMEM((3, 576, 1024), bf16), DMA((12,)), DMA((3,))],
+        compiler_params=pltpu.CompilerParams(vmem_limit_bytes=18 << 20),
         name="finish",
     )(sums, ff, output, grad_tokens, vec)
 
@@ -947,12 +1018,12 @@
         (lengths, tokens, norm_in.reshape(1, 1024), w_query, wk, wv, qg, kg, freqs),
         "project", smem,
     )
-    qz, kv_all, ext = gather_keys(lengths, q, kv)
+    kv_all, ext, qa, mix_f, mixed, normed_mid, mid_own, cot = forward(
+        parts, lengths, q, kv, tokens, cotangent, w_out, norm_mid
+    )
     kv_all = kv_all.reshape(8192, 128)
-    mix_z, mix_f, qa = attend(parts, lengths, qz.reshape(512, 128), kv_all, ext)
-    normed_mid, mid_own, mixed = make_middle(mix_z, w_out, tokens, norm_mid)
     normed_mid = normed_mid.reshape(512, 1024)
-    mixed = mixed.reshape(512, 128)
+    cotangent = cot.reshape(512, 1024)
 
     gate = jnp.dot(normed_mid, w_gate, preferred_element_type=f32)
     up_proj = jnp.dot(normed_mid, w_up, preferred_element_type=f32)
@@ -973,7 +1044,7 @@
     )
     output, grad_tokens, sums, g_ff, vec = backward(
         parts,
-        d_mid_part.reshape(8, 64, 1024), mlp_part.reshape(8, 64, 1024), mid_own, cotangent.reshape(8, 64, 1024),
+        d_mid_part.reshape(8, 64, 1024), mlp_part.reshape(8, 64, 1024), mid_own, cot,
         norm_mid.reshape(1, 1024), w_out, *(g.reshape(4, 144, 1024) for g in grads),
         qa, mix_f, kv_all, ext, mixed,
         q_proj, kv_proj, normed, w_query, wk, wv, qg, kg, cosine, sine, tokens.reshape(8, 64, 1024), norm_in.reshape(1, 1024),

time: 186 us -> 182 us (0.978)
  Pallas kernels: 171 us -> 162 us
  local copies, waits for them, and re-layouts: 2.36 us -> 11 us
    pallas_call x1 -> x0, Pallas kernels: 9.28 us -> none  [attend(): pl.pallas_call(functools.partial(fwd_kernel, parts), out_shape=(sds((rows...]
    unnamed x34 -> x46, local copies, waits for them, and re-layouts: 2.29 us -> 10.2 us
    pallas_call x3 -> x2, Pallas kernels: 154 us -> 154 us  [comm_call(): pl.pallas_call(kernel, out_shape=out_shape, in_specs=[first or vmem] + [v...]
where the time goes in v5:
time: 182 us
  Pallas kernels  162 us (89%)
  local copies, waits for them, and re-layouts  11 us (6%)
  matrix products  8.31 us (5%)
    pallas_call x2, Pallas kernels, comm_call(): pl.pallas_call(kernel, out_shape=out_shape, in_specs=[first or vmem] + [v...  154 us
    unnamed x46, local copies, waits for them, and re-layouts  10.2 us
    pallas_call x1, Pallas kernels, finish(): pl.pallas_call(finish_kernel, out_shape=(sds((512, 1024), bf16), sds((512...  4.93 us

profile of v5, /device:TPU:1, one launch (start us, length us, event | category | flops | bytes accessed | tf_op | source)
XLA Modules:
  0.0 181.9 jit_solution(2521425891907644442)
XLA Ops:
  0.6 0.0 copy-start
  0.7 0.8 jit_solution_.3.freq_ref
  1.5 0.0 copy-start.3
  1.5 1.2 copy-done.3
  2.7 0.0 copy-start.5
  2.7 0.9 copy-done.5
  3.7 0.0 copy-start.8
  3.7 0.9 copy-done.8
  4.6 0.0 copy-start.10
  4.6 0.9 copy-done.10
  5.5 0.0 copy-start.12
  5.5 0.7 copy-done.12
  6.2 0.0 copy-start.15
  6.2 0.7 copy-done.15
  6.8 0.0 copy-start.16
  6.8 0.7 copy-done.16
  7.5 0.0 copy-start.18
  7.5 0.7 copy-done.18
  8.1 0.0 copy-start.2
  8.1 0.0 copy-start.7
  8.1 0.0 copy-start.14
  8.1 2.9 %project.1 = (bf16[512,1024]{1,0:T(8,128)(2,1)S(1)}, f32[512,128]{1,0:T(8,128)S(1)}, f32[512,128]{1,0:T(8,128)S(1)}, bf16[512,128]{1,0:T(8,128)(2,1)S(1)}, bf16[...) custom-call(s32[4]{0:T(128)S(1)} %copy-done.15, bf16[512,1024]{1,0:T(8,128)(2,1)S(1)} %copy-done.3, ...), custom_call_target="tpu_custom_call" | custom-call | flops 3221225472 | bytes 16777216 | tf_op jit(solution)/shard_map/project/pallas_call | solution.py:634
  11.0 0.0 copy-done.2
  11.0 0.0 copy-done.7
  11.0 0.0 copy-done.14
  11.0 0.0 copy-start.22
  11.0 50.8 %forward.1 = (bf16[4,4,2,256,128]{4,3,2,1,0:T(8,128)(2,1)S(1)}, bf16[8192,128]{1,0:T(8,128)(2,1)S(1)}, bf16[2,512,256]{2,1,0:T(8,128)(2,1)S(1)}, f32[2,256,128]{...) custom-call(s32[4]{0:T(128)S(1)} %copy-done.15, ...), custom_call_target="tpu_custom_call" | custom-call | flops 8589934592 | bytes 33554432 | tf_op jit(solution)/shard_map/forward/pallas_call | solution.py:554
  61.8 0.0 copy-start.20
  61.8 0.0 copy-done.22
  61.9 0.0 copy-start.21
  61.9 0.8 fusion.1
  62.7 0.5 copy-done.20
  63.2 0.7 copy-done.21
  63.9 0.8 fusion
  64.7 0.0 copy-done
  64.8 1.3 multiply_convert_fusion
  66.0 1.0 convolution_convert_fusion.3
  67.0 0.8 convolution_convert_fusion
  67.8 0.8 convolution_convert_fusion.2
  68.6 0.8 convolution_convert_fusion.1
  69.4 1.0 fusion.2
  70.4 0.0 copy-start.4
  70.5 0.0 copy-start.6
  70.5 0.0 copy-start.9
  70.5 0.0 copy-start.11
  70.5 0.0 copy-start.13
  70.5 0.0 copy-start.17
  70.5 0.0 copy-start.19
  70.5 1.0 add_convert_fusion
  71.5 0.1 copy-done.4
  71.7 0.0 copy-done.6
  71.7 0.0 copy-done.9
  71.7 0.0 copy-done.11
  71.8 0.0 copy-done.13
  71.8 0.0 copy-done.17
  71.8 0.0 copy-done.19
  71.8 103.0 %backward.1 = (bf16[8,64,1024]{2,1,0:T(8,128)(2,1)S(1)}, bf16[8,64,1024]{2,1,0:T(8,128)(2,1)S(1)}, bf16[3,4,32,1024]{3,2,1,0:T(8,128)(2,1)S(1)}, bf16[3,4,144,1024]{3,2,1,0:T(8,128)(2,1)}, f32[8,1024]{1,0:T(8,128)S(1)}) custom-call(bf16[8,64,1024]{2,1,0:T(8,128)(2,1)S(1)} %bitcast.78, bf16[8,64,1024]{2,1,0:T(8,128)(2,1)S(1)} %bitcast.73, ...), custom_call_target="tpu_custom_call" | custom-call | flops 8589934592 | bytes 33554432 | tf_op jit(solution)/shard_map/backward/pallas_call | solution.py:554
  174.8 0.0 copy-start.1
  174.8 2.0 %copy-done.1 = bf16[3,4,144,1024]{3,2,1,0:T(8,128)(2,1)S(1)} copy-done((bf16[3,4,144,1024]{3,2,1,0:T(8,128)(2,1)S(1)}, bf16[3,4,144,1024]{3,2,1,0:T(8,128)(2,1)}, u32[]{:S(2)}) %copy-start.1) | copy-done | bytes 3538968
  176.8 4.9 %finish.1 = (bf16[512,1024]{1,0:T(8,128)(2,1)}, bf16[512,1024]{1,0:T(8,128)(2,1)}, f32[1024,128]{1,0:T(8,128)}, f32[64,1024]{1,0:T(8,128)}, f32[64,1024]{1,0:T(8...) custom-call(bf16[3,128,1024]{2,1,0:T(8,128)(2,1)S(1)} %bitcast.51, ...), custom_call_target="tpu_custom_call" | custom-call | tf_op jit(solution)/shard_map/finish/pallas_call | solution.py:991
Async XLA Ops:
  0.6 64.1 %copy-start = (bf16[1024,576]{0,1:T(8,128)(2,1)S(1)}, bf16[1024,576]{0,1:T(8,128)(2,1)}, u32[]{:S(2)}) copy-start(bf16[1024,576]{0,1:T(8,128)(2,1)} %param.25) | copy-start | bytes 3538948
  1.5 1.2 copy-start.3
  2.7 0.9 copy-start.5
  3.7 0.9 copy-start.8
  4.6 0.9 copy-start.10
  5.5 0.7 copy-start.12
  6.2 0.7 copy-start.15
  6.8 0.7 copy-start.16
  7.5 0.7 copy-start.18
  8.1 2.9 %copy-start.2 = (bf16[512,1024]{1,0:T(8,128)(2,1)S(1)}, bf16[512,1024]{1,0:T(8,128)(2,1)}, u32[]{:S(2)}) copy-start(bf16[512,1024]{1,0:T(8,128)(2,1)} %param.27) | copy-start | bytes 3145732
  8.1 2.9 %copy-start.7 = (bf16[128,1024]{1,0:T(8,128)(2,1)S(1)}, bf16[128,1024]{1,0:T(8,128)(2,1)}, u32[]{:S(2)}) copy-start(bf16[128,1024]{1,0:T(8,128)(2,1)} %w_ref.3) | copy-start | bytes 786436
  8.1 2.9 %copy-start.14 = (f32[1024]{0:T(1024)S(1)}, f32[1024]{0:T(1024)}, u32[]{:S(2)}) copy-start(f32[1024]{0:T(1024)} %param.23) | copy-start | bytes 12292
  11.0 50.8 %copy-start.22 = (bf16[1024,576]{0,1:T(8,128)(2,1)S(1)}, bf16[1024,576]{0,1:T(8,128)(2,1)}, u32[]{:S(2)}) copy-start(bf16[1024,576]{0,1:T(8,128)(2,1)} %param.24) | copy-start | bytes 3538948
  61.8 1.3 copy-start.20
  61.9 2.0 %copy-start.21 = (bf16[576,1024]{1,0:T(8,128)(2,1)S(1)}, bf16[576,1024]{1,0:T(8,128)(2,1)}, u32[]{:S(2)}) copy-start(bf16[576,1024]{1,0:T(8,128)(2,1)} %param.26) | copy-start | bytes 3538948
  70.4 1.2 copy-start.4
  70.5 1.3 copy-start.6
  70.5 1.3 copy-start.9
  70.5 1.3 copy-start.11
  70.5 1.3 copy-start.13
  70.5 1.3 copy-start.17
  70.5 1.3 copy-start.19
  174.8 2.0 %copy-start.1 = (bf16[3,4,144,1024]{3,2,1,0:T(8,128)(2,1)S(1)}, bf16[3,4,144,1024]{3,2,1,0:T(8,128)(2,1)}, u32[]{:S(2)}) copy-start(bf16[3,4,144,1024]{3,2,1,0:T(8,128)(2,1)} %get-tuple-element.62) | copy-start | bytes 10616836

commit v6 on v5

--- a/solution.py
+++ b/solution.py
@@ -387,7 +387,7 @@
 
 def forward_kernel(
     parts,
-    len_ref, q_ref, kv_ref, tok_ref, cot_ref, w_ref, gain_ref,
+    len_ref, q_ref, kv_ref, tok_ref, cot_ref, w_ref, pack_ref,
     all_ref, ext_ref, qa_ref, mixf_ref, mix_ref, nm_ref, mid_ref, cotz_ref,
     qz, base, acc, part, sib, send, rz, ms, mr, cs, cr, zs, zr, az, bz, ag, bg, fs, fr, ss, sr,
 ):
@@ -538,7 +538,7 @@
     for s in range(SPLIT):
         middle = base[sub(s)].astype(f32) + total.own(s)
         mid_ref[sub(s)] = middle
-        nm_ref[p.wt, sub(s)] = (middle * rms_of(middle) * gain_ref[...]).astype(bf16)
+        nm_ref[p.wt, sub(s)] = (middle * rms_of(middle) * pack_ref[1:2]).astype(bf16)
         spread.start(s)
     spread.forward()
     cot_mirror.wait_recv()
@@ -565,7 +565,7 @@
     )(*args)
 
 
-def forward(parts, lengths, q, kv, tokens, cotangent, w_out, gain):
+def forward(parts, lengths, q, kv, tokens, cotangent, w_out, pack):
     rows = pltpu.VMEM
     half = sds((2, 256, 128), bf16)
     full = sds((8, 64, 1024), bf16)
@@ -574,7 +574,7 @@
         (sds((4, 4, 2, 256, 128), bf16), sds((8192, 128), bf16), sds((2, 512, 256), bf16), sds((2, 256, 128), f32),
          half, full, sds((64, 1024), f32), full),
         (lengths, q.reshape(2, 256, 128), kv.reshape(2, 256, 128), tokens.reshape(8, 64, 1024),
-         cotangent.reshape(8, 64, 1024), w_out, gain.reshape(1, 1024)),
+         cotangent.reshape(8, 64, 1024), w_out, pack),
         [rows((2, 256, 128), bf16), rows((64, 1024), bf16), rows((2, 512, 128), f32), rows((8, 64, 1024), bf16),
          rows((4, 64, 1024), bf16), rows((3, 64, 1024), bf16), rows((3, 64, 1024), bf16), DMA((3,)), DMA((3,))]
         + WT_SEMS + [DMA((2, 3)), DMA((2, 3)), DMA((2, 4, 3)), DMA((2, 4, 3))],
@@ -592,10 +592,6 @@
     return jnp.where(lane < 64, s0, s1)
 
 
-def twice(gain):
-    return jnp.concatenate([gain, gain], axis=1)
-
-
 def nt(a, b):
     return lax.dot_general(a, b, (((1,), (1,)), ((), ())), preferred_element_type=f32)
 
@@ -604,49 +600,55 @@
     return lax.dot_general(a, b, (((0,), (0,)), ((), ())), preferred_element_type=f32)
 
 
-def proj_kernel(len_ref, tok_ref, gain_ref, wq_ref, wk_ref, wv_ref, qg_ref, kg_ref, freq_ref,
-                n_ref, qp_ref, kvp_ref, q_ref, kv_ref, cos_ref, sin_ref):
+FREQS = [float(np.float32(1000000.0 ** (-2.0 * i / 64))) for i in range(32)]
+
+
+def proj_kernel(len_ref, tok_ref, pack_ref, wq_ref, wkv_ref, n_ref, qp_ref, kvp_ref, q_ref, kv_ref, cos_ref, sin_ref):
     lane = lanes((512, 128))
     ids = lax.axis_index("sp") * 512 + lax.broadcasted_iota(jnp.int32, (1, 512), 1)
     positions = (ids - starts_of(ids, len_ref)).astype(f32)
-    angles = positions * freq_ref[:, 0:1]
+    row = lax.broadcasted_iota(jnp.int32, (32, 512), 0)
+    freqs = jnp.zeros((32, 512), f32)
+    for i, freq in enumerate(FREQS):
+        freqs = jnp.where(row == i, freq, freqs)
+    angles = positions * freqs
     cosine, sine = jnp.cos(angles), jnp.sin(angles)
     cosine = jnp.concatenate([cosine] * 4, axis=0).T
     sine = jnp.concatenate([-sine, sine, -sine, sine], axis=0).T
     cos_ref[...] = cosine
     sin_ref[...] = sine
     base = tok_ref[...].astype(f32)
-    normed = (base * rms_of(base) * gain_ref[...]).astype(bf16)
+    normed = (base * rms_of(base) * pack_ref[0:1]).astype(bf16)
     n_ref[...] = normed
-    wkv = jnp.concatenate([wk_ref[...], wv_ref[...]], axis=0)
     q = jnp.dot(normed, wq_ref[...], preferred_element_type=f32)
     qp_ref[...] = q
-    q = q * lax.rsqrt(head_sums(q * q, lane) * (1.0 / 64) + eps) * twice(qg_ref[...])
+    q = q * lax.rsqrt(head_sums(q * q, lane) * (1.0 / 64) + eps) * pack_ref[2:3, 0:128]
     q_ref[...] = (q * cosine + turned(q, lane) * sine).astype(bf16)
-    kv = nt(normed, wkv)
+    kv = nt(normed, wkv_ref[...])
     kvp_ref[...] = kv
-    k = kv * lax.rsqrt(head_sums(kv * kv, lane) * (1.0 / 64) + eps) * twice(kg_ref[...])
+    k = kv * lax.rsqrt(head_sums(kv * kv, lane) * (1.0 / 64) + eps) * pack_ref[2:3, 128:256]
     k = k * cosine + turned(k, lane) * sine
     kv_ref[...] = jnp.where(lane < 64, k, kv).astype(bf16)
 
 
-def local_call(kernel, out_shape, args, name, first=None):
+def project(*args):
+    wide = sds((512, 128), f32)
+    out_shape = (sds((512, 1024), bf16), wide, wide, sds((512, 128), bf16), sds((512, 128), bf16), wide, wide)
     return pl.pallas_call(
-        kernel,
+        proj_kernel,
         out_shape=out_shape,
-        in_specs=[first or vmem] + [vmem] * (len(args) - 1),
+        in_specs=[smem] + [vmem] * 4,
         out_specs=tuple(vmem for _ in out_shape),
-        compiler_params=pltpu.CompilerParams(vmem_limit_bytes=16 << 20),
-        cost_estimate=pl.CostEstimate(flops=3 << 30, bytes_accessed=16 << 20, transcendentals=0),
-        name=name,
+        compiler_params=pltpu.CompilerParams(vmem_limit_bytes=12 << 20),
+        name="project",
     )(*args)
 
 
 def backward_kernel(
     parts,
-    dm_ref, mlp_ref, mid_ref, cot_ref, gain_ref, w_ref, g0_ref, g1_ref, g2_ref,
+    dm_ref, mlp_ref, mid_ref, cot_ref, pack_ref, w_ref, g0_ref, g1_ref, g2_ref,
     qa_ref, mixf_ref, kv_ref, ext_ref, mixed_ref,
-    qp_ref, kvp_ref, n_ref, wq_ref, wk_ref, wv_ref, qg_ref, kg_ref, cos_ref, sin_ref, tok_ref, gain_in_ref,
+    qp_ref, kvp_ref, n_ref, wq_ref, wkv_ref, cos_ref, sin_ref, tok_ref,
     out_ref, gt_ref, sums_ref, ff_ref, vec_ref,
     *scratch,
 ):
@@ -689,17 +691,17 @@
 
     for zz in range(4):
         d_mid_sum.start_core(zz)
-    ff.first(0)
-    ff.first(1)
+    for i in range(3):
+        ff.first(i)
     d_mid_sum.send_z()
-    for zz in range(4):
-        mlp_sum.start_core(zz)
     vw[0] = jnp.zeros((8, 1024), f32)
+    acc[...] = jnp.zeros_like(acc)
+    dqt[...] = jnp.zeros_like(dqt)
     for s in range(SPLIT):
         middle = mid_ref[sub(s)]
         scale = rms_of(middle)
         d_mid = d_mid_sum.own(s)
-        d_middle = cot_ref[p.wt, sub(s)].astype(f32) + norm_back(middle, scale, gain_ref[...], d_mid)
+        d_middle = cot_ref[p.wt, sub(s)].astype(f32) + norm_back(middle, scale, pack_ref[1:2], d_mid)
         da[p.wt, sub(s)] = d_middle.astype(bf16)
         da_gather.start(s)
         dmid[sub(s)] = d_middle
@@ -710,91 +712,94 @@
     def _():
         dmid_mirror.start()
 
+    da_gather.forward()
+    da_gather.arrived()
+    for zz in range(4):
+        mlp_sum.start_core(zz)
+    dz[...] = nt(da[...].reshape(512, 1024), w_ref[...]).astype(bf16).reshape(2, 256, 128)
     mlp_sum.send_z()
-    ff.second(0)
-    da_gather.forward()
-    acc[...] = jnp.zeros_like(acc)
-    da_gather.arrived()
-    dz[...] = nt(da[...].reshape(512, 1024), w_ref[...]).astype(bf16).reshape(2, 256, 128)
-    ff.first(2)
-    ff.second(1)
 
     lane = lanes((HALF, 128))
-    upper_long = (me < parts // 2).astype(jnp.int32)
-    for turn in range(2):
-        t = upper_long if turn == 0 else 1 - upper_long
-        block = me + t * (parts - 1 - 2 * me)
-        r0 = block * 512 + t * HALF
+    for t in range(2):
         do = dz[t].astype(f32)
         prod = do * mixf_ref[t]
         d0 = -jnp.sum(jnp.where(lane < 64, prod, 0.0), axis=1, keepdims=True)
         d1 = -jnp.sum(jnp.where(lane < 64, 0.0, prod), axis=1, keepdims=True)
-        dab[0:HALF, 0:128] = jnp.where(lane < 64, 0.0, pltpu.roll(do, 64, 1)).astype(bf16)
-        dab[HALF:, 0:128] = jnp.where(lane < 64, 0.0, do).astype(bf16)
-        dab[0:HALF, 128:256] = split3(jnp.broadcast_to(d0, (HALF, 128)), lane).astype(bf16)
-        dab[HALF:, 128:256] = split3(jnp.broadcast_to(d1, (HALF, 128)), lane).astype(bf16)
-        dqt[...] = jnp.zeros_like(dqt)
-
-        def step(c, masked, t=t, r0=r0):
-            k0 = pl.multiple_of(c * CH, CH)
-            kv = kv_ref[pl.ds(k0, CH), :]
-            kva = jnp.concatenate([kv, ext_ref[pl.ds(k0, CH), :]], axis=1)
-            qa = qa_ref[t]
-            d_out = dab[...]
-            s = nt(kva, qa)
-            pr = jnp.exp2(s * C2)
-            if masked:
-                rows = r0 + lax.rem(lax.broadcasted_iota(jnp.int32, (1, 2 * HALF), 1), HALF)
-                keys = k0 + lax.broadcasted_iota(jnp.int32, (CH, 2 * HALF), 0)
-                pr = jnp.where(keys <= rows, pr, 0.0)
-            ds = (pr * nt(kva, d_out)).astype(bf16)
-            acc[pl.ds(k0, CH), :] += jnp.dot(
-                pr.astype(bf16), d_out[:, 0:128], preferred_element_type=f32
-            ) + jnp.dot(ds, qa[:, 0:128], preferred_element_type=f32)
-            kt = kv.T[0:64, :]
-            dqt[...] += jnp.dot(kt, ds, preferred_element_type=f32)
-
-        def plain(c):
-            step(c, False)
-
-        if turn == 0:
-            pl.loop(0, 4)(plain)
-            for i in range(2):
-                for h in range(2):
-                    ff_back.put(i, h, ff.own(i, h).astype(bf16))
-                    ff_back.first(i, h)
-            ff.second(2)
-            for s in range(SPLIT):
-                out_own[sub(s)] = (mid_ref[sub(s)] + mlp_sum.own(s)).astype(bf16)
-            out_mirror = rcopy(out_own, out_ref.at[p.wt], mirror_sems[4], mirror_sems[5], p.mirror)
-
-            @pl.when(p.wt >= 4)
-            def _():
-                out_mirror.start()
-
-            @pl.when(p.wt < 4)
-            def _():
-                out_ref[p.wt] = out_own[...]
-
-            gout[...] = tn(mixed_ref[...].reshape(512, 128), da[...].reshape(512, 1024)).astype(bf16).reshape(4, 32, 1024)
-            pl.loop(4, 8)(plain)
-            for h in range(2):
-                ff_back.put(2, h, ff.own(2, h).astype(bf16))
-                ff_back.first(2, h)
-            for h in range(2):
-                ff_back.second(0, h)
-
-            @pl.when(p.wt >= 4)
-            def _():
-                out_mirror.wait()
-
-            for s in range(SPLIT):
-                out_gather.start(s)
-            pl.loop(8, block)(plain)
-        else:
-            pl.loop(0, block)(plain)
-        step(block, True)
-        both = jnp.concatenate([dqt[:, :HALF], dqt[:, HALF:]], axis=0)
+        dab[t, 0:HALF, 0:128] = jnp.where(lane < 64, 0.0, pltpu.roll(do, 64, 1)).astype(bf16)
+        dab[t, HALF:, 0:128] = jnp.where(lane < 64, 0.0, do).astype(bf16)
+        dab[t, 0:HALF, 128:256] = split3(jnp.broadcast_to(d0, (HALF, 128)), lane).astype(bf16)
+        dab[t, HALF:, 128:256] = split3(jnp.broadcast_to(d1, (HALF, 128)), lane).astype(bf16)
+    upper_long = (me < parts // 2).astype(jnp.int32)
+    blocks = [me + t * (parts - 1 - 2 * me) for t in (upper_long, 1 - upper_long)]
+
+    def step(k, masked):
+        short = (k > blocks[0]).astype(jnp.int32)
+        t = upper_long + short * (1 - 2 * upper_long)
+        c = k - short * (blocks[0] + 1)
+        k0 = pl.multiple_of(c * CH, CH)
+        kv = kv_ref[pl.ds(k0, CH), :]
+        kva = jnp.concatenate([kv, ext_ref[pl.ds(k0, CH), :]], axis=1)
+        qa = qa_ref[t]
+        d_out = dab[t]
+        pr = jnp.exp2(nt(kva, qa) * C2)
+        if masked:
+            r0 = c * 512 + t * HALF
+            rows = r0 + lax.rem(lax.broadcasted_iota(jnp.int32, (1, 2 * HALF), 1), HALF)
+            keys = k0 + lax.broadcasted_iota(jnp.int32, (CH, 2 * HALF), 0)
+            pr = jnp.where(keys <= rows, pr, 0.0)
+        ds = (pr * nt(kva, d_out)).astype(bf16)
+        acc[pl.ds(k0, CH), :] += jnp.dot(
+            pr.astype(bf16), d_out[:, 0:128], preferred_element_type=f32
+        ) + jnp.dot(ds, qa[:, 0:128], preferred_element_type=f32)
+        kt = kv.T[0:64, :]
+        dqt[t] += jnp.dot(kt, ds, preferred_element_type=f32)
+
+    def plain(k):
+        step(k, False)
+
+    def either(k):
+        pl.when(k == blocks[0])(lambda: step(k, True))
+        pl.when(k != blocks[0])(lambda: step(k, False))
+
+    ff.second(0)
+    ff.second(1)
+    pl.loop(0, 3)(plain)
+    ff.second(2)
+    pl.loop(3, 6)(plain)
+    for i in range(3):
+        for h in range(2):
+            ff_back.put(i, h, ff.own(i, h).astype(bf16))
+            ff_back.first(i, h)
+    pl.loop(6, 8)(plain)
+    for s in range(SPLIT):
+        out_own[sub(s)] = (mid_ref[sub(s)] + mlp_sum.own(s)).astype(bf16)
+    out_mirror = rcopy(out_own, out_ref.at[p.wt], mirror_sems[4], mirror_sems[5], p.mirror)
+
+    @pl.when(p.wt >= 4)
+    def _():
+        out_mirror.start()
+
+    @pl.when(p.wt < 4)
+    def _():
+        out_ref[p.wt] = out_own[...]
+
+    gout[...] = tn(mixed_ref[...].reshape(512, 128), da[...].reshape(512, 1024)).astype(bf16).reshape(4, 32, 1024)
+    sums.first(0)
+    pl.loop(8, 12)(either)
+    for h in range(2):
+        ff_back.second(0, h)
+    sums.second(0)
+
+    @pl.when(p.wt >= 4)
+    def _():
+        out_mirror.wait()
+
+    for s in range(SPLIT):
+        out_gather.start(s)
+    pl.loop(12, 16)(either)
+    step(16, True)
+    for t in range(2):
+        both = jnp.concatenate([dqt[t, :, :HALF], dqt[t, :, HALF:]], axis=0)
         dqz[t] = (both.T * SCALE).astype(bf16)
     weight = jnp.where(lanes((512, 128)) < 64, SCALE, 1.0)
 
@@ -806,32 +811,36 @@
     mirror = flow.send(dqz.at[1], dq.at[1], mirror_sems[0], mirror_sems[1], p.mirror)
     dq[0] = dqz[0]
     first, second = {}, {}
-    for d in ORDER:
+    for e in (2, 1, 3, 0):
+        for d in ORDER:
+            for h in range(2):
+                at = spot(h, lax.rem(p.fsp(h) + d, 4), lax.rem(p.ssp(h) + e, 4))
+                first[h, d, e] = flow.send(
+                    dkv.at[at[0], at[1], h], r1.at[h, d - 1, e], fs.at[h, d - 1, e], fr.at[h, d - 1, e], p.first(h, d)
+                )
+
+    def total(h, e):
+        at = spot(h, p.fsp(h), lax.rem(p.ssp(h) + e, 4))
+        value = dkv[at[0], at[1], h].astype(f32)
+        for d in ORDER:
+            first[h, d, e].wait_recv()
+            value = value + r1[h, d - 1, e].astype(f32)
+        return value
+
+    out_gather.forward()
+    for e in ORDER:
         for h in range(2):
-            to = lax.rem(p.fsp(h) + d, 4)
-            src = dkv.at[to, :, 0] if h == 0 else dkv.at[:, to, 1]
-            first[h, d] = flow.send(src, r1.at[h, d - 1], fs.at[h, d - 1], fr.at[h, d - 1], p.first(h, d))
-
-    def total(h, b):
-        at = spot(h, p.fsp(h), b)
-        value = dkv[at[0], at[1], h].astype(f32)
-        for d in range(3):
-            value = value + r1[h, d, b].astype(f32)
-        return value
-
-    for h in range(2):
-        for d in ORDER:
-            first[h, d].wait_recv()
-        for e in ORDER:
-            send1[h, e - 1] = total(h, lax.rem(p.ssp(h) + e, 4)).astype(bf16)
+            send1[h, e - 1] = total(h, e).astype(bf16)
             second[h, e] = flow.send(
                 send1.at[h, e - 1], r2.at[h, e - 1], ss.at[h, e - 1], sr.at[h, e - 1], p.second(h, e)
             )
-    out_gather.forward()
+    own = [total(h, 0) for h in range(2)]
     for h in range(2):
         ff_back.second(1, h)
+        sums_back.put(0, h, sums.own(0, h).astype(bf16))
+        sums_back.first(0, h)
     for h in range(2):
-        value = total(h, p.ssp(h))
+        value = own[h]
         for e in ORDER:
             second[h, e].wait_recv()
             value = value + r2[h, e - 1].astype(f32)
@@ -849,19 +858,18 @@
         gains = jnp.sum(grad * proj * scale, axis=0, keepdims=True)
         return scale * scaled - proj * scale * scale * scale * inner, gains
 
-    d_q, gq = back(dq[...].reshape(512, 128).astype(f32), qp_ref[...], twice(qg_ref[...]))
+    d_q, gq = back(dq[...].reshape(512, 128).astype(f32), qp_ref[...], pack_ref[2:3, 0:128])
     dkv_in = dkv_own[...].reshape(512, 128).astype(f32)
-    d_k, gk = back(dkv_in, kvp_ref[...], twice(kg_ref[...]))
+    d_k, gk = back(dkv_in, kvp_ref[...], pack_ref[2:3, 128:256])
     d_q = d_q.astype(bf16)
     d_kv = jnp.where(wide < 64, d_k, dkv_in).astype(bf16)
-    wkv = jnp.concatenate([wk_ref[...], wv_ref[...]], axis=0)
-    dn[...] = (nt(d_q, wq_ref[...]) + jnp.dot(d_kv, wkv, preferred_element_type=f32)).astype(bf16).reshape(8, 64, 1024)
+    dn[...] = (nt(d_q, wq_ref[...]) + jnp.dot(d_kv, wkv_ref[...], preferred_element_type=f32)).astype(bf16).reshape(8, 64, 1024)
     for zz in range(4):
         dn_sum.start_core(zz)
     normed = n_ref[...]
     gqkv[0] = tn(d_q, normed).astype(bf16).reshape(4, 32, 1024)
     gqkv[1] = tn(d_kv, normed).astype(bf16).reshape(4, 32, 1024)
-    for i in range(3):
+    for i in (1, 2):
         sums.first(i)
     dn_sum.send_z()
 
@@ -885,10 +893,11 @@
         return value
 
     round1 = vec_round(vw, [p.along_z(d) for d in ORDER] + [p.along_z_other(d) for d in ORDER] + [p.sibling], vs1, vr1)
+    for i in (1, 2):
+        sums.second(i)
     for h in range(2):
+        sums_back.second(0, h)
         ff_back.second(2, h)
-    for i in range(3):
-        sums.second(i)
 
     @pl.when(p.wt >= 4)
     def _():
@@ -902,16 +911,16 @@
         base = tok_ref[p.wt, sub(s)].astype(f32)
         d_normed = dn_sum.own(s)
         gt_ref[p.wt, sub(s)] = (
-            dmid_o[sub(s)] + norm_back(base, rms_of(base), gain_in_ref[...], d_normed)
+            dmid_o[sub(s)] + norm_back(base, rms_of(base), pack_ref[0:1], d_normed)
         ).astype(bf16)
         gt_gather.start(s)
-    for i in range(3):
+    for i in (1, 2):
         for h in range(2):
             sums_back.put(i, h, sums.own(i, h).astype(bf16))
             sums_back.first(i, h)
     vx[0] = vec_total(vw, round1)
     round2 = vec_round(vx, [p.along_x(d) for d in ORDER], vs2, vr2)
-    for i in range(3):
+    for i in (1, 2):
         for h in range(2):
             sums_back.second(i, h)
     vy[0] = vec_total(vx, round2)
@@ -938,16 +947,16 @@
         [rows((8, 64, 1024), bf16), half, rows((64, 1024), f32), rows((64, 1024), f32), rows((64, 1024), bf16)] + [DMA] * 6
         + wt_sum + wt_gather + wt_sum + wt_gather
         + SpScatter.scratch(3, 144) + SpGather.sems(3)
-        + [rows((512, 256), bf16), rows((8192, 128), f32), rows((64, 512), f32), half, half,
+        + [rows((2, 512, 256), bf16), rows((8192, 128), f32), rows((2, 64, 512), f32), half, half,
            rows((4, 4, 2, 256, 128), bf16), half]
         + [rows((2, 3, 4, 256, 128), bf16), rows((2, 3, 256, 128), bf16), rows((2, 3, 256, 128), bf16)]
-        + [DMA((2, 3))] * 4
+        + [DMA((2, 3, 4)), DMA((2, 3, 4)), DMA((2, 3)), DMA((2, 3))]
         + [rows((8, 64, 1024), bf16), rows((2, 4, 32, 1024), bf16), rows((4, 32, 1024), bf16)]
         + wt_sum + wt_gather
         + SpScatter.scratch(3, 32) + SpGather.sems(3)
         + [rows((8, 8, 1024), f32), rows((4, 8, 1024), f32), rows((4, 8, 1024), f32),
            DMA((7,)), DMA((7,)), DMA((3,)), DMA((3,)), DMA((3,)), DMA((3,))],
-        "backward", 36,
+        "backward", 30,
     )
 
 
@@ -1001,25 +1010,15 @@
     )(sums, ff, output, grad_tokens, vec)
 
 
-theta = 1000000.0
-
-
 def body(tokens, norm_in, w_query, w_key, w_value, query_gain, key_gain, w_out, norm_mid, w_gate, w_up, w_down, cotangent, lengths):
     parts = lax.axis_size("sp")
-    freqs = theta ** (-(np.arange(32).astype(np.float64) * 2.0) / 64)
-    freqs = jnp.asarray(np.broadcast_to(freqs.astype(np.float32)[:, None], (32, 128)))
-    qg, kg = query_gain.reshape(1, 64), key_gain.reshape(1, 64)
-    wk, wv = w_key.T, w_value.T
-    wide = sds((512, 128), f32)
-
-    normed, q_proj, kv_proj, q, kv, cosine, sine = local_call(
-        proj_kernel,
-        (sds((512, 1024), bf16), wide, wide, sds((512, 128), bf16), sds((512, 128), bf16), wide, wide),
-        (lengths, tokens, norm_in.reshape(1, 1024), w_query, wk, wv, qg, kg, freqs),
-        "project", smem,
-    )
+    gains = jnp.concatenate([query_gain, query_gain, key_gain, key_gain, jnp.zeros((768,), f32)])
+    pack = jnp.concatenate([norm_in[None], norm_mid[None], gains[None], jnp.zeros((5, 1024), f32)], axis=0)
+    wkv = jnp.concatenate([w_key.T, w_value.T], axis=0)
+
+    normed, q_proj, kv_proj, q, kv, cosine, sine = project(lengths, tokens, pack, w_query, wkv)
     kv_all, ext, qa, mix_f, mixed, normed_mid, mid_own, cot = forward(
-        parts, lengths, q, kv, tokens, cotangent, w_out, norm_mid
+        parts, lengths, q, kv, tokens, cotangent, w_out, pack
     )
     kv_all = kv_all.reshape(8192, 128)
     normed_mid = normed_mid.reshape(512, 1024)
@@ -1045,9 +1044,9 @@
     output, grad_tokens, sums, g_ff, vec = backward(
         parts,
         d_mid_part.reshape(8, 64, 1024), mlp_part.reshape(8, 64, 1024), mid_own, cot,
-        norm_mid.reshape(1, 1024), w_out, *(g.reshape(4, 144, 1024) for g in grads),
+        pack, w_out, *(g.reshape(4, 144, 1024) for g in grads),
         qa, mix_f, kv_all, ext, mixed,
-        q_proj, kv_proj, normed, w_query, wk, wv, qg, kg, cosine, sine, tokens.reshape(8, 64, 1024), norm_in.reshape(1, 1024),
+        q_proj, kv_proj, normed, w_query, wkv, cosine, sine, tokens.reshape(8, 64, 1024),
     )
     (output, grad_tokens, g_query, g_key, g_value, g_out, g_gate, g_up, g_down, g_norm_in, g_norm_mid, g_qg, g_kg) = finish(
         sums.reshape(3, 128, 1024), g_ff.reshape(3, 576, 1024), output.reshape(512, 1024), grad_tokens.reshape(512, 1024), vec

time: 182 us -> 176 us (0.967); the launches traced: 182 us -> 174 us
  local copies, waits for them, and re-layouts: 11 us -> 5.48 us
  Pallas kernels: 162 us -> 157 us
    unnamed x46 -> x22, local copies, waits for them, and re-layouts: 10.2 us -> 4.53 us
    pallas_call x2, Pallas kernels: 154 us -> 150 us  [comm_call(): pl.pallas_call(kernel, out_shape=out_shape, in_specs=[first or vmem] + [v...]
where the time goes in v6:
time: 176 us; the launch traced here: 174 us
  Pallas kernels  157 us (89%)
  matrix products  8.26 us (5%)
  local copies, waits for them, and re-layouts  5.48 us (3%)
  other arithmetic  1.76 us (1%)
    pallas_call x2, Pallas kernels, comm_call(): pl.pallas_call(kernel, out_shape=out_shape, in_specs=[first or vmem] + [v...  150 us
    pallas_call x1, Pallas kernels, finish(): pl.pallas_call(finish_kernel, out_shape=(sds((512, 1024), bf16), sds((512...  4.95 us
    unnamed x22, local copies, waits for them, and re-layouts  4.53 us

profile of v6, /device:TPU:1, one launch (start us, length us, event | category | flops | bytes accessed | tf_op | source)
XLA Modules:
  0.0 173.8 jit_solution(17238213539375410243)
XLA Ops:
  0.6 0.0 copy-start
  0.7 0.0 copy-start.6
  0.7 0.0 copy-start.8
  0.7 0.1 pad.5.clone
  0.8 0.9 concatenate.9
  1.6 0.8 maximum_maximum_fusion.pack_ref
  2.4 1.0 pad_maximum_fusion.wkv_ref
  3.4 0.0 copy-start.1
  3.4 1.2 copy-done.1
  4.6 0.0 copy-start.3
  4.6 0.9 copy-done.3
  5.6 0.0 copy-start.5
  5.6 0.7 copy-done.5
  6.2 0.0 copy-start.2
  6.2 2.8 %project.1 = (bf16[512,1024]{1,0:T(8,128)(2,1)S(1)}, f32[512,128]{1,0:T(8,128)S(1)}, f32[512,128]{1,0:T(8,128)S(1)}, bf16[512,128]{1,0:T(8,128)(2,1)S(1)}, bf16[...) custom-call(s32[4]{0:T(128)S(1)} %copy-done.5, bf16[512,1024]{1,0:T(8,128)(2,1)S(1)} %copy-done.1, ...), custom_call_target="tpu_custom_call" | custom-call | tf_op jit(solution)/shard_map/project/pallas_call | solution.py:637
  9.0 0.0 copy-done.6
  9.0 0.0 copy-done.8
  9.0 0.0 copy-done.2
  9.1 0.0 copy-start.7
  9.1 1.2 copy-done.7
  10.3 0.0 copy-start.10
  10.3 50.7 %forward.1 = (bf16[4,4,2,256,128]{4,3,2,1,0:T(8,128)(2,1)S(1)}, bf16[8192,128]{1,0:T(8,128)(2,1)S(1)}, bf16[2,512,256]{2,1,0:T(8,128)(2,1)S(1)}, f32[2,256,128]{...) custom-call(s32[4]{0:T(128)S(1)} %copy-done.6, ...), custom_call_target="tpu_custom_call" | custom-call | flops 8589934592 | bytes 33554432 | tf_op jit(solution)/shard_map/forward/pallas_call | solution.py:554
  61.0 0.0 copy-done.10
  61.0 0.0 copy-start.9
  61.0 0.8 fusion.1
  61.8 0.4 copy-done.9
  62.3 0.8 fusion
  63.1 0.0 copy-done
  63.1 1.3 multiply_convert_fusion
  64.4 1.0 convolution_convert_fusion.3
  65.4 0.8 convolution_convert_fusion
  66.2 0.8 convolution_convert_fusion.2
  67.0 0.8 convolution_convert_fusion.1
  67.8 1.0 fusion.2
  68.8 0.0 copy-start.4
  68.8 1.0 add_convert_fusion
  69.8 0.0 copy-done.4
  69.8 98.9 %backward.1 = (bf16[8,64,1024]{2,1,0:T(8,128)(2,1)S(1)}, bf16[8,64,1024]{2,1,0:T(8,128)(2,1)S(1)}, bf16[3,4,32,1024]{3,2,1,0:T(8,128)(2,1)S(1)}, bf16[3,4,144,1024]{3,2,1,0:T(8,128)(2,1)S(1)}, f32[8,1024]{1,0:T(8,128)S(1)}) custom-call(bf16[8,64,1024]{2,1,0:T(8,128)(2,1)S(1)} %bitcast.63, bf16[8,64,1024]{2,1,0:T(8,128)(2,1)S(1)} %bitcast.62, ...), custom_call_target="tpu_custom_call" | custom-call | flops 8589934592 | bytes 33554432 | tf_op jit(solution)/shard_map/backward/pallas_call | solution.py:554
  168.7 4.9 %finish.1 = (bf16[512,1024]{1,0:T(8,128)(2,1)}, bf16[512,1024]{1,0:T(8,128)(2,1)}, f32[1024,128]{1,0:T(8,128)}, f32[64,1024]{1,0:T(8,128)}, f32[64,1024]{1,0:T(8...) custom-call(bf16[3,128,1024]{2,1,0:T(8,128)(2,1)S(1)} %bitcast.52, ...), custom_call_target="tpu_custom_call" | custom-call | tf_op jit(solution)/shard_map/finish/pallas_call | solution.py:1000
  (2 shorter events, 0.0 us)
Async XLA Ops:
  0.6 62.4 %copy-start = (bf16[1024,576]{0,1:T(8,128)(2,1)S(1)}, bf16[1024,576]{0,1:T(8,128)(2,1)}, u32[]{:S(2)}) copy-start(bf16[1024,576]{0,1:T(8,128)(2,1)} %param.24) | copy-start | bytes 3538948
  0.7 8.4 %copy-start.6 = (s32[4]{0:T(128)S(1)}, s32[4]{0:T(128)}, u32[]{:S(2)}) copy-start(s32[4]{0:T(128)} %len_ref.3) | copy-start | bytes 52
  0.7 8.4 %copy-start.8 = (bf16[128,1024]{1,0:T(8,128)(2,1)S(1)}, bf16[128,1024]{1,0:T(8,128)(2,1)}, u32[]{:S(2)}) copy-start(bf16[128,1024]{1,0:T(8,128)(2,1)} %w_ref.3) | copy-start | bytes 786436
  3.4 1.2 copy-start.1
  4.6 0.9 copy-start.3
  5.6 0.7 copy-start.5
  6.2 2.8 %copy-start.2 = (bf16[512,1024]{1,0:T(8,128)(2,1)S(1)}, bf16[512,1024]{1,0:T(8,128)(2,1)}, u32[]{:S(2)}) copy-start(bf16[512,1024]{1,0:T(8,128)(2,1)} %tok_ref.1) | copy-start | bytes 3145732
  9.1 1.2 copy-start.7
  10.3 50.7 %copy-start.10 = (bf16[1024,576]{0,1:T(8,128)(2,1)S(1)}, bf16[1024,576]{0,1:T(8,128)(2,1)}, u32[]{:S(2)}) copy-start(bf16[1024,576]{0,1:T(8,128)(2,1)} %param.23) | copy-start | bytes 3538948
  61.0 1.3 copy-start.9
  68.8 1.0 copy-start.4

commit v7 on v6

--- a/solution.py
+++ b/solution.py
@@ -145,46 +145,42 @@
 ORDER = (2, 1, 3)
 
 
+def to_blocks(value, rows, put):
+    for x in range(4):
+        for y in range(4):
+            for h in range(2):
+                block = value(x)[:, h * 512 + y * 128:h * 512 + y * 128 + 128]
+                put(h, *spot(h, x, y), block)
+
+
 class SpScatter:
-    def __init__(self, p, srcs, rows, refs):
-        self.p, self.srcs, self.rows = p, srcs, rows
-        self.ra, self.rb, self.send, self.r2, self.fs, self.fr, self.ss, self.sr = refs
+    def __init__(self, p, srcs, refs):
+        self.p, self.srcs = p, srcs
+        self.r1, self.send, self.r2, self.fs, self.fr, self.ss, self.sr = refs
         self.one, self.two = {}, {}
 
     @staticmethod
     def scratch(n, rows):
         return [
-            pltpu.VMEM((n, 3, rows, 512), bf16), pltpu.VMEM((n, 3, 4, rows, 128), bf16),
-            pltpu.VMEM((n, 2, 3, rows, 128), bf16), pltpu.VMEM((n, 2, 3, rows, 128), bf16),
+            pltpu.VMEM((n, 2, 3, 4, rows, 128), bf16), pltpu.VMEM((n, 2, 3, rows, 128), bf16),
+            pltpu.VMEM((n, 2, 3, rows, 128), bf16),
             DMA((n, 2, 3)), DMA((n, 2, 3)), DMA((n, 2, 3)), DMA((n, 2, 3)),
         ]
 
     def first(self, i):
         p = self.p
         for d in ORDER:
-            to = lax.rem(p.x + d, 4)
-            self.one[i, 0, d] = rcopy(
-                self.srcs[i].at[to, :, pl.ds(0, 512)], self.ra.at[i, d - 1],
-                self.fs.at[i, 0, d - 1], self.fr.at[i, 0, d - 1], p.along_x(d),
-            )
-            self.one[i, 0, d].start()
-            to = lax.rem(p.y + d, 4)
-            self.one[i, 1, d] = rcopy(
-                self.srcs[i].at[:, :, pl.ds(columns_at(1, to), 128)], self.rb.at[i, d - 1],
-                self.fs.at[i, 1, d - 1], self.fr.at[i, 1, d - 1], p.along_y(d),
-            )
-            self.one[i, 1, d].start()
+            for h in range(2):
+                self.one[i, h, d] = rcopy(
+                    self.srcs[i].at[h, lax.rem(p.fsp(h) + d, 4)], self.r1.at[i, h, d - 1],
+                    self.fs.at[i, h, d - 1], self.fr.at[i, h, d - 1], p.first(h, d),
+                )
+                self.one[i, h, d].start()
 
     def part(self, i, h, b):
-        p = self.p
-        if h == 0:
-            value = self.srcs[i][p.x, :, pl.ds(columns_at(0, b), 128)].astype(f32)
-            for d in range(3):
-                value = value + self.ra[i, d, :, pl.ds(columns_at(0, b), 128)].astype(f32)
-            return value
-        value = self.srcs[i][b, :, pl.ds(columns_at(1, p.y), 128)].astype(f32)
+        value = self.srcs[i][h, self.p.fsp(h), b].astype(f32)
         for d in range(3):
-            value = value + self.rb[i, d, b].astype(f32)
+            value = value + self.r1[i, h, d, b].astype(f32)
         return value
 
     def second(self, i):
@@ -212,13 +208,9 @@
             copy.wait_send()
 
 
-def columns_at(h, b):
-    return pl.multiple_of(h * 512 + b * 128, 128)
-
-
 class SpGather:
-    def __init__(self, p, out, rows, sems):
-        self.p, self.out, self.rows = p, out, rows
+    def __init__(self, p, out, sems):
+        self.p, self.out = p, out
         self.fs, self.fr, self.ss, self.sr = sems
         self.one, self.two = {}, {}
 
@@ -226,17 +218,11 @@
     def sems(n):
         return [DMA((n, 2, 3)) for _ in range(4)]
 
-    def spot(self, h):
-        p = self.p
-        return p.x, pl.ds(columns_at(h, p.y), 128)
-
     def put(self, i, h, value):
-        x, columns = self.spot(h)
-        self.out[i, x, :, columns] = value
+        self.out[i, h, self.p.fsp(h), self.p.ssp(h)] = value
 
     def first(self, i, h):
-        x, columns = self.spot(h)
-        block = self.out.at[i, x, :, columns]
+        block = self.out.at[i, h, self.p.fsp(h), self.p.ssp(h)]
         for e in ORDER:
             self.one[i, h, e] = rcopy(
                 block, block, self.fs.at[i, h, e - 1], self.fr.at[i, h, e - 1], self.p.second(h, e)
@@ -244,20 +230,14 @@
             self.one[i, h, e].start()
 
     def second(self, i, h):
-        x, columns = self.spot(h)
         for e in ORDER:
             self.one[i, h, e].wait_recv()
-        block = self.out.at[i, x, :, pl.ds(0, 512)] if h == 0 else self.out.at[i, :, :, columns]
+        block = self.out.at[i, h, self.p.fsp(h)]
         for d in ORDER:
             self.two[i, h, d] = rcopy(
                 block, block, self.ss.at[i, h, d - 1], self.sr.at[i, h, d - 1], self.p.first(h, d)
             )
             self.two[i, h, d].start()
-
-    def arrived(self, i):
-        for h in range(2):
-            for d in ORDER:
-                self.two[i, h, d].wait_recv()
 
     def finish(self):
         for copy in self.one.values():
@@ -677,23 +657,29 @@
     da_gather = WtGather(p, da, take(4))
     mlp_sum = wt_sum(mlp_ref)
     out_gather = WtGather(p, out_ref, take(4))
-    ff = SpScatter(p, (g0_ref, g1_ref, g2_ref), 144, take(8))
-    ff_back = SpGather(p, ff_ref, 144, take(4))
+    (ffb,) = take(1)
+    ff = SpScatter(p, [ffb.at[i] for i in range(3)], take(7))
+    ff_back = SpGather(p, ff_ref, take(4))
     dab, acc, dqt, dqz, dq, dkv, dkv_own = take(7)
     r1, send1, r2, fs, fr, ss, sr = take(7)
     dn, gqkv, gout = take(3)
     dn_sum = wt_sum(dn)
     gt_gather = WtGather(p, gt_ref, take(4))
-    sums = SpScatter(p, (gout, gqkv.at[0], gqkv.at[1]), 32, take(8))
-    sums_back = SpGather(p, sums_ref, 32, take(4))
+    sums = SpScatter(p, (gout, gqkv.at[0], gqkv.at[1]), take(7))
+    sums_back = SpGather(p, sums_ref, take(4))
     vw, vx, vy, vs1, vr1, vs2, vr2, vs3, vr3 = take(9)
     assert not scratch
 
     for zz in range(4):
         d_mid_sum.start_core(zz)
-    for i in range(3):
+    for i, ref in enumerate((g0_ref, g1_ref, g2_ref)):
+        def put(h, u, v, block, i=i):
+            ffb[i, h, u, v] = block
+
+        to_blocks(lambda x, ref=ref: ref[x], 144, put)
         ff.first(i)
-    d_mid_sum.send_z()
+        if i == 0:
+            d_mid_sum.send_z()
     vw[0] = jnp.zeros((8, 1024), f32)
     acc[...] = jnp.zeros_like(acc)
     dqt[...] = jnp.zeros_like(dqt)
@@ -783,7 +769,12 @@
     def _():
         out_ref[p.wt] = out_own[...]
 
-    gout[...] = tn(mixed_ref[...].reshape(512, 128), da[...].reshape(512, 1024)).astype(bf16).reshape(4, 32, 1024)
+
+    def put_out(h, u, v, block):
+        gout[h, u, v] = block
+
+    g_out = tn(mixed_ref[...].reshape(512, 128), da[...].reshape(512, 1024)).astype(bf16)
+    to_blocks(lambda x: g_out[x * 32:x * 32 + 32], 32, put_out)
     sums.first(0)
     pl.loop(8, 12)(either)
     for h in range(2):
@@ -867,8 +858,12 @@
     for zz in range(4):
         dn_sum.start_core(zz)
     normed = n_ref[...]
-    gqkv[0] = tn(d_q, normed).astype(bf16).reshape(4, 32, 1024)
-    gqkv[1] = tn(d_kv, normed).astype(bf16).reshape(4, 32, 1024)
+    for i, grad in enumerate((d_q, d_kv)):
+        def put_in(h, u, v, block, i=i):
+            gqkv[i, h, u, v] = block
+
+        g_in = tn(grad, normed).astype(bf16)
+        to_blocks(lambda x, g_in=g_in: g_in[x * 32:x * 32 + 32], 32, put_in)
     for i in (1, 2):
         sums.first(i)
     dn_sum.send_z()
@@ -941,17 +936,17 @@
     half = rows((2, 256, 128), bf16)
     return comm_call(
         functools.partial(backward_kernel, parts), 4,
-        (sds((8, 64, 1024), bf16), sds((8, 64, 1024), bf16), sds((3, 4, 32, 1024), bf16), sds((3, 4, 144, 1024), bf16),
+        (sds((8, 64, 1024), bf16), sds((8, 64, 1024), bf16), sds((3, 2, 4, 4, 32, 128), bf16), sds((3, 2, 4, 4, 144, 128), bf16),
          sds((8, 1024), f32)),
         args,
         [rows((8, 64, 1024), bf16), half, rows((64, 1024), f32), rows((64, 1024), f32), rows((64, 1024), bf16)] + [DMA] * 6
         + wt_sum + wt_gather + wt_sum + wt_gather
-        + SpScatter.scratch(3, 144) + SpGather.sems(3)
+        + [rows((3, 2, 4, 4, 144, 128), bf16)] + SpScatter.scratch(3, 144) + SpGather.sems(3)
         + [rows((2, 512, 256), bf16), rows((8192, 128), f32), rows((2, 64, 512), f32), half, half,
            rows((4, 4, 2, 256, 128), bf16), half]
         + [rows((2, 3, 4, 256, 128), bf16), rows((2, 3, 256, 128), bf16), rows((2, 3, 256, 128), bf16)]
         + [DMA((2, 3, 4)), DMA((2, 3, 4)), DMA((2, 3)), DMA((2, 3))]
-        + [rows((8, 64, 1024), bf16), rows((2, 4, 32, 1024), bf16), rows((4, 32, 1024), bf16)]
+        + [rows((8, 64, 1024), bf16), rows((2, 2, 4, 4, 32, 128), bf16), rows((2, 4, 4, 32, 128), bf16)]
         + wt_sum + wt_gather
         + SpScatter.scratch(3, 32) + SpGather.sems(3)
         + [rows((8, 8, 1024), f32), rows((4, 8, 1024), f32), rows((4, 8, 1024), f32),
@@ -973,18 +968,26 @@
     loads = [pltpu.make_async_copy(ff_ref.at[i], ff.at[i], load_sems.at[i]) for i in range(3)]
     for load in loads:
         load.start()
+
+    def assemble(out, blocks, x, rows):
+        for h in range(2):
+            for y in range(4):
+                columns = slice(h * 512 + y * 128, h * 512 + y * 128 + 128)
+                out[x * rows:(x + 1) * rows, columns] = blocks[(h,) + spot(h, x, y)].astype(f32)
+
     for i, ref in enumerate((gg_ref, gu_ref, gd_ref)):
         loads[i].wait()
-        for part in range(2):
-            rows = pl.ds(part * 288, 288)
-            big[i, rows, :] = ff[i, rows, :].astype(f32)
+        for x in range(4):
+            assemble(big.at[i], ff.at[i], x, 144)
+            rows = pl.ds(x * 144, 144)
             write(big.at[i, rows], ref.at[rows])
-    wide[0] = sums_ref[0].astype(f32)
-    wide[1] = sums_ref[2].astype(f32)
-    write(wide.at[1, 0:64], gk_ref)
-    write(wide.at[1, 64:128], gv_ref)
+    for i in range(3):
+        for x in range(4):
+            assemble(wide.at[i], sums_ref.at[i], x, 32)
+    write(wide.at[2, 0:64], gk_ref)
+    write(wide.at[2, 64:128], gv_ref)
     write(wide.at[0], go_ref)
-    tall[...] = sums_ref[1].astype(f32).T
+    tall[...] = wide[1].T
     write(tall, gq_ref)
     ni_ref[...] = vec_ref[0:1, :]
     nm_ref[...] = vec_ref[1:2, :]
@@ -1004,7 +1007,7 @@
                    sds((1, 1024), f32), sds((1, 1024), f32), sds((1, 64), f32), sds((1, 64), f32)),
         in_specs=[vmem, hbm, vmem, vmem, vmem],
         out_specs=tuple([hbm] * 9 + [vmem] * 4),
-        scratch_shapes=[pltpu.VMEM((2, 128, 1024), f32), pltpu.VMEM((1024, 128), f32), pltpu.VMEM((3, 576, 1024), f32), pltpu.VMEM((3, 576, 1024), bf16), DMA((12,)), DMA((3,))],
+        scratch_shapes=[pltpu.VMEM((3, 128, 1024), f32), pltpu.VMEM((1024, 128), f32), pltpu.VMEM((3, 576, 1024), f32), pltpu.VMEM((3, 2, 4, 4, 144, 128), bf16), DMA((18,)), DMA((3,))],
         compiler_params=pltpu.CompilerParams(vmem_limit_bytes=18 << 20),
         name="finish",
     )(sums, ff, output, grad_tokens, vec)
@@ -1049,7 +1052,7 @@
         q_proj, kv_proj, normed, w_query, wkv, cosine, sine, tokens.reshape(8, 64, 1024),
     )
     (output, grad_tokens, g_query, g_key, g_value, g_out, g_gate, g_up, g_down, g_norm_in, g_norm_mid, g_qg, g_kg) = finish(
-        sums.reshape(3, 128, 1024), g_ff.reshape(3, 576, 1024), output.reshape(512, 1024), grad_tokens.reshape(512, 1024), vec
+        sums, g_ff, output.reshape(512, 1024), grad_tokens.reshape(512, 1024), vec
     )
     return (
         output, grad_tokens, g_norm_in.reshape(1024), g_query, g_key.T, g_value.T, g_qg.reshape(64), g_kg.reshape(64),

time: 176 us -> 175 us (level)
  no operation moved by 1% of the time
where the time goes in v7:
time: 175 us; the launch traced here: 174 us
  Pallas kernels  158 us (90%)
  matrix products  8.26 us (5%)
  local copies, waits for them, and re-layouts  5.48 us (3%)
  other arithmetic  1.76 us (1%)
    pallas_call x2, Pallas kernels, comm_call(): pl.pallas_call(kernel, out_shape=out_shape, in_specs=[first or vmem] + [v...  150 us
    pallas_call x1, Pallas kernels, finish(): pl.pallas_call(finish_kernel, out_shape=(sds((512, 1024), bf16), sds((512...  4.98 us
    unnamed x22, local copies, waits for them, and re-layouts  4.53 us

profile of v7, /device:TPU:1, one launch (start us, length us, event | category | flops | bytes accessed | tf_op | source)
XLA Modules:
  0.0 174.2 jit_solution(7738434419271900450)
XLA Ops:
  0.6 0.0 copy-start
  0.7 0.0 copy-start.6
  0.7 0.0 copy-start.8
  0.7 0.1 pad.5.clone
  0.8 0.9 concatenate.9
  1.6 0.8 maximum_maximum_fusion.pack_ref
  2.4 1.0 pad_maximum_fusion.wkv_ref
  3.4 0.0 copy-start.1
  3.4 1.2 copy-done.1
  4.6 0.0 copy-start.3
  4.6 0.9 copy-done.3
  5.6 0.0 copy-start.5
  5.6 0.7 copy-done.5
  6.2 0.0 copy-start.2
  6.2 2.8 %project.1 = (bf16[512,1024]{1,0:T(8,128)(2,1)S(1)}, f32[512,128]{1,0:T(8,128)S(1)}, f32[512,128]{1,0:T(8,128)S(1)}, bf16[512,128]{1,0:T(8,128)(2,1)S(1)}, bf16[...) custom-call(s32[4]{0:T(128)S(1)} %copy-done.5, bf16[512,1024]{1,0:T(8,128)(2,1)S(1)} %copy-done.1, ...), custom_call_target="tpu_custom_call" | custom-call | tf_op jit(solution)/shard_map/project/pallas_call | solution.py:617
  9.0 0.0 copy-done.6
  9.0 0.0 copy-done.8
  9.0 0.0 copy-done.2
  9.1 0.0 copy-start.7
  9.1 1.2 copy-done.7
  10.3 0.0 copy-start.10
  10.3 50.7 %forward.1 = (bf16[4,4,2,256,128]{4,3,2,1,0:T(8,128)(2,1)S(1)}, bf16[8192,128]{1,0:T(8,128)(2,1)S(1)}, bf16[2,512,256]{2,1,0:T(8,128)(2,1)S(1)}, f32[2,256,128]{...) custom-call(s32[4]{0:T(128)S(1)} %copy-done.6, ...), custom_call_target="tpu_custom_call" | custom-call | flops 8589934592 | bytes 33554432 | tf_op jit(solution)/shard_map/forward/pallas_call | solution.py:534
  61.0 0.0 copy-done.10
  61.0 0.0 copy-start.9
  61.0 0.8 fusion.1
  61.8 0.4 copy-done.9
  62.3 0.8 fusion
  63.1 0.0 copy-done
  63.1 1.3 multiply_convert_fusion
  64.4 1.0 convolution_convert_fusion.3
  65.4 0.8 convolution_convert_fusion
  66.2 0.8 convolution_convert_fusion.2
  67.0 0.8 convolution_convert_fusion.1
  67.8 1.0 fusion.2
  68.8 0.0 copy-start.4
  68.8 1.0 add_convert_fusion
  69.8 0.0 copy-done.4
  69.8 99.2 %backward.1 = (bf16[8,64,1024]{2,1,0:T(8,128)(2,1)S(1)}, bf16[8,64,1024]{2,1,0:T(8,128)(2,1)S(1)}, bf16[3,2,4,4,32,128]{5,4,3,2,1,0:T(8,128)(2,1)S(1)}, bf16[3,2...) custom-call(bf16[8,64,1024]{2,1,0:T(8,128)(2,1)S(1)} %bitcast.59, bf16[8,64,1024]{2,1,0:T(8,128)(2,1)S(1)} %bitcast.58, ...), custom_call_target="tpu_custom_call" | custom-call | flops 8589934592 | bytes 33554432 | tf_op jit(solution)/shard_map/backward/pallas_call | solution.py:534
  169.0 5.0 %finish.1 = (bf16[512,1024]{1,0:T(8,128)(2,1)}, bf16[512,1024]{1,0:T(8,128)(2,1)}, f32[1024,128]{1,0:T(8,128)}, f32[64,1024]{1,0:T(8,128)}, f32[64,1024]{1,0:T(8...) custom-call(bf16[3,2,4,4,32,128]{5,4,3,2,1,0:T(8,128)(2,1)S(1)} %get, ...), custom_call_target="tpu_custom_call" | custom-call | tf_op jit(solution)/shard_map/finish/pallas_call | solution.py:1003
  (2 shorter events, 0.0 us)
Async XLA Ops:
  0.6 62.4 %copy-start = (bf16[1024,576]{0,1:T(8,128)(2,1)S(1)}, bf16[1024,576]{0,1:T(8,128)(2,1)}, u32[]{:S(2)}) copy-start(bf16[1024,576]{0,1:T(8,128)(2,1)} %param.24) | copy-start | bytes 3538948
  0.7 8.4 %copy-start.6 = (s32[4]{0:T(128)S(1)}, s32[4]{0:T(128)}, u32[]{:S(2)}) copy-start(s32[4]{0:T(128)} %len_ref.3) | copy-start | bytes 52
  0.7 8.4 %copy-start.8 = (bf16[128,1024]{1,0:T(8,128)(2,1)S(1)}, bf16[128,1024]{1,0:T(8,128)(2,1)}, u32[]{:S(2)}) copy-start(bf16[128,1024]{1,0:T(8,128)(2,1)} %w_ref.3) | copy-start | bytes 786436
  3.4 1.2 copy-start.1
  4.6 0.9 copy-start.3
  5.6 0.7 copy-start.5
  6.2 2.8 %copy-start.2 = (bf16[512,1024]{1,0:T(8,128)(2,1)S(1)}, bf16[512,1024]{1,0:T(8,128)(2,1)}, u32[]{:S(2)}) copy-start(bf16[512,1024]{1,0:T(8,128)(2,1)} %tok_ref.1) | copy-start | bytes 3145732
  9.1 1.2 copy-start.7
  10.3 50.7 %copy-start.10 = (bf16[1024,576]{0,1:T(8,128)(2,1)S(1)}, bf16[1024,576]{0,1:T(8,128)(2,1)}, u32[]{:S(2)}) copy-start(bf16[1024,576]{0,1:T(8,128)(2,1)} %param.23) | copy-start | bytes 3538948
  61.0 1.3 copy-start.9
  68.8 1.0 copy-start.4

commit v8 on v7

--- a/solution.py
+++ b/solution.py
@@ -212,11 +212,11 @@
     def __init__(self, p, out, sems):
         self.p, self.out = p, out
         self.fs, self.fr, self.ss, self.sr = sems
-        self.one, self.two = {}, {}
+        self.one, self.two, self.further = {}, {}, {}
 
     @staticmethod
     def sems(n):
-        return [DMA((n, 2, 3)) for _ in range(4)]
+        return [DMA((n, 2, k)) for k in (3, 3, 4, 4)]
 
     def put(self, i, h, value):
         self.out[i, h, self.p.fsp(h), self.p.ssp(h)] = value
@@ -239,10 +239,31 @@
             )
             self.two[i, h, d].start()
 
+    def relayed(self, i, h):
+        for e in ORDER:
+            self.one[i, h, e].wait_recv()
+        block = self.out.at[i, h, self.p.fsp(h)]
+        for slot, d in enumerate((1, 3)):
+            self.two[i, h, slot] = rcopy(
+                block, block, self.ss.at[i, h, slot], self.sr.at[i, h, slot], self.p.first(h, d)
+            )
+            self.two[i, h, slot].start()
+
+    def relay(self, i, h):
+        for slot, d in enumerate((1, 3)):
+            self.two[i, h, slot].wait_recv()
+            block = self.out.at[i, h, lax.rem(self.p.fsp(h) + 4 - d, 4), pl.ds(2 * slot, 2)]
+            self.further[i, h, slot] = rcopy(
+                block, block, self.ss.at[i, h, 2 + slot], self.sr.at[i, h, 2 + slot], self.p.first(h, d)
+            )
+            self.further[i, h, slot].start()
+
     def finish(self):
         for copy in self.one.values():
             copy.wait_send()
         for copy in self.two.values():
+            copy.wait_send() if self.further else copy.wait()
+        for copy in self.further.values():
             copy.wait()
 
 
@@ -751,12 +772,14 @@
     ff.second(1)
     pl.loop(0, 3)(plain)
     ff.second(2)
-    pl.loop(3, 6)(plain)
+    pl.loop(3, 5)(plain)
     for i in range(3):
         for h in range(2):
             ff_back.put(i, h, ff.own(i, h).astype(bf16))
             ff_back.first(i, h)
-    pl.loop(6, 8)(plain)
+    pl.loop(5, 8)(plain)
+    for h in range(2):
+        ff_back.relayed(0, h)
     for s in range(SPLIT):
         out_own[sub(s)] = (mid_ref[sub(s)] + mlp_sum.own(s)).astype(bf16)
     out_mirror = rcopy(out_own, out_ref.at[p.wt], mirror_sems[4], mirror_sems[5], p.mirror)
@@ -768,7 +791,6 @@
     @pl.when(p.wt < 4)
     def _():
         out_ref[p.wt] = out_own[...]
-
 
     def put_out(h, u, v, block):
         gout[h, u, v] = block
@@ -778,7 +800,9 @@
     sums.first(0)
     pl.loop(8, 12)(either)
     for h in range(2):
-        ff_back.second(0, h)
+        ff_back.relayed(1, h)
+    for h in range(2):
+        ff_back.relay(0, h)
     sums.second(0)
 
     @pl.when(p.wt >= 4)
@@ -827,7 +851,8 @@
             )
     own = [total(h, 0) for h in range(2)]
     for h in range(2):
-        ff_back.second(1, h)
+        ff_back.relayed(2, h)
+        ff_back.relay(1, h)
         sums_back.put(0, h, sums.own(0, h).astype(bf16))
         sums_back.first(0, h)
     for h in range(2):
@@ -891,8 +916,8 @@
     for i in (1, 2):
         sums.second(i)
     for h in range(2):
+        ff_back.relay(2, h)
         sums_back.second(0, h)
-        ff_back.second(2, h)
 
     @pl.when(p.wt >= 4)
     def _():

time: 175 us -> 174 us (level)
  Pallas kernels: 158 us -> 156 us
where the time goes in v8:
time: 174 us; the launch traced here: 173 us
  Pallas kernels  156 us (90%)
  matrix products  8.26 us (5%)
  local copies, waits for them, and re-layouts  5.48 us (3%)
  other arithmetic  1.76 us (1%)
    pallas_call x2, Pallas kernels, comm_call(): pl.pallas_call(kernel, out_shape=out_shape, in_specs=[first or vmem] + [v...  149 us
    pallas_call x1, Pallas kernels, finish(): pl.pallas_call(finish_kernel, out_shape=(sds((512, 1024), bf16), sds((512...  4.98 us
    unnamed x22, local copies, waits for them, and re-layouts  4.53 us

profile of v8, /device:TPU:1, one launch (start us, length us, event | category | flops | bytes accessed | tf_op | source)
XLA Modules:
  0.0 173.0 jit_solution(2490732262707651875)
XLA Ops:
  0.6 0.0 copy-start
  0.7 0.0 copy-start.6
  0.7 0.0 copy-start.8
  0.7 0.1 pad.5.clone
  0.8 0.9 concatenate.9
  1.6 0.8 maximum_maximum_fusion.pack_ref
  2.4 1.0 pad_maximum_fusion.wkv_ref
  3.4 0.0 copy-start.1
  3.4 1.2 copy-done.1
  4.6 0.0 copy-start.3
  4.6 0.9 copy-done.3
  5.6 0.0 copy-start.5
  5.6 0.7 copy-done.5
  6.2 0.0 copy-start.2
  6.2 2.8 %project.1 = (bf16[512,1024]{1,0:T(8,128)(2,1)S(1)}, f32[512,128]{1,0:T(8,128)S(1)}, f32[512,128]{1,0:T(8,128)S(1)}, bf16[512,128]{1,0:T(8,128)(2,1)S(1)}, bf16[...) custom-call(s32[4]{0:T(128)S(1)} %copy-done.5, bf16[512,1024]{1,0:T(8,128)(2,1)S(1)} %copy-done.1, ...), custom_call_target="tpu_custom_call" | custom-call | tf_op jit(solution)/shard_map/project/pallas_call | solution.py:638
  9.0 0.0 copy-done.6
  9.0 0.0 copy-done.8
  9.0 0.0 copy-done.2
  9.1 0.0 copy-start.7
  9.1 1.2 copy-done.7
  10.3 0.0 copy-start.10
  10.3 50.7 %forward.1 = (bf16[4,4,2,256,128]{4,3,2,1,0:T(8,128)(2,1)S(1)}, bf16[8192,128]{1,0:T(8,128)(2,1)S(1)}, bf16[2,512,256]{2,1,0:T(8,128)(2,1)S(1)}, f32[2,256,128]{...) custom-call(s32[4]{0:T(128)S(1)} %copy-done.6, ...), custom_call_target="tpu_custom_call" | custom-call | flops 8589934592 | bytes 33554432 | tf_op jit(solution)/shard_map/forward/pallas_call | solution.py:555
  61.0 0.0 copy-done.10
  61.0 0.0 copy-start.9
  61.0 0.8 fusion.1
  61.8 0.4 copy-done.9
  62.3 0.8 fusion
  63.1 0.0 copy-done
  63.1 1.3 multiply_convert_fusion
  64.4 1.0 convolution_convert_fusion.3
  65.4 0.8 convolution_convert_fusion
  66.2 0.8 convolution_convert_fusion.2
  67.0 0.8 convolution_convert_fusion.1
  67.8 1.0 fusion.2
  68.8 0.0 copy-start.4
  68.8 1.0 add_convert_fusion
  69.8 0.0 copy-done.4
  69.8 98.0 %backward.1 = (bf16[8,64,1024]{2,1,0:T(8,128)(2,1)S(1)}, bf16[8,64,1024]{2,1,0:T(8,128)(2,1)S(1)}, bf16[3,2,4,4,32,128]{5,4,3,2,1,0:T(8,128)(2,1)S(1)}, bf16[3,2...) custom-call(bf16[8,64,1024]{2,1,0:T(8,128)(2,1)S(1)} %bitcast.59, bf16[8,64,1024]{2,1,0:T(8,128)(2,1)S(1)} %bitcast.58, ...), custom_call_target="tpu_custom_call" | custom-call | flops 8589934592 | bytes 33554432 | tf_op jit(solution)/shard_map/backward/pallas_call | solution.py:555
  167.8 5.0 %finish.1 = (bf16[512,1024]{1,0:T(8,128)(2,1)}, bf16[512,1024]{1,0:T(8,128)(2,1)}, f32[1024,128]{1,0:T(8,128)}, f32[64,1024]{1,0:T(8,128)}, f32[64,1024]{1,0:T(8...) custom-call(bf16[3,2,4,4,32,128]{5,4,3,2,1,0:T(8,128)(2,1)S(1)} %get, ...), custom_call_target="tpu_custom_call" | custom-call | tf_op jit(solution)/shard_map/finish/pallas_call | solution.py:1028
  (2 shorter events, 0.0 us)
Async XLA Ops:
  0.6 62.4 %copy-start = (bf16[1024,576]{0,1:T(8,128)(2,1)S(1)}, bf16[1024,576]{0,1:T(8,128)(2,1)}, u32[]{:S(2)}) copy-start(bf16[1024,576]{0,1:T(8,128)(2,1)} %param.24) | copy-start | bytes 3538948
  0.7 8.4 %copy-start.6 = (s32[4]{0:T(128)S(1)}, s32[4]{0:T(128)}, u32[]{:S(2)}) copy-start(s32[4]{0:T(128)} %len_ref.3) | copy-start | bytes 52
  0.7 8.4 %copy-start.8 = (bf16[128,1024]{1,0:T(8,128)(2,1)S(1)}, bf16[128,1024]{1,0:T(8,128)(2,1)}, u32[]{:S(2)}) copy-start(bf16[128,1024]{1,0:T(8,128)(2,1)} %w_ref.3) | copy-start | bytes 786436
  3.4 1.2 copy-start.1
  4.6 0.9 copy-start.3
  5.6 0.7 copy-start.5
  6.2 2.8 %copy-start.2 = (bf16[512,1024]{1,0:T(8,128)(2,1)S(1)}, bf16[512,1024]{1,0:T(8,128)(2,1)}, u32[]{:S(2)}) copy-start(bf16[512,1024]{1,0:T(8,128)(2,1)} %tok_ref.1) | copy-start | bytes 3145732
  9.1 1.2 copy-start.7
  10.3 50.7 %copy-start.10 = (bf16[1024,576]{0,1:T(8,128)(2,1)S(1)}, bf16[1024,576]{0,1:T(8,128)(2,1)}, u32[]{:S(2)}) copy-start(bf16[1024,576]{0,1:T(8,128)(2,1)} %param.23) | copy-start | bytes 3538948
  61.0 1.3 copy-start.9
  68.8 1.0 copy-start.4

commit v9 on v8

--- a/solution.py
+++ b/solution.py
@@ -773,13 +773,16 @@
     pl.loop(0, 3)(plain)
     ff.second(2)
     pl.loop(3, 5)(plain)
-    for i in range(3):
+    for i in range(2):
         for h in range(2):
             ff_back.put(i, h, ff.own(i, h).astype(bf16))
             ff_back.first(i, h)
     pl.loop(5, 8)(plain)
     for h in range(2):
         ff_back.relayed(0, h)
+    for h in range(2):
+        ff_back.put(2, h, ff.own(2, h).astype(bf16))
+        ff_back.first(2, h)
     for s in range(SPLIT):
         out_own[sub(s)] = (mid_ref[sub(s)] + mlp_sum.own(s)).astype(bf16)
     out_mirror = rcopy(out_own, out_ref.at[p.wt], mirror_sems[4], mirror_sems[5], p.mirror)
@@ -801,8 +804,6 @@
     pl.loop(8, 12)(either)
     for h in range(2):
         ff_back.relayed(1, h)
-    for h in range(2):
-        ff_back.relay(0, h)
     sums.second(0)
 
     @pl.when(p.wt >= 4)
@@ -843,6 +844,8 @@
         return value
 
     out_gather.forward()
+    for h in range(2):
+        ff_back.relay(0, h)
     for e in ORDER:
         for h in range(2):
             send1[h, e - 1] = total(h, e).astype(bf16)
@@ -916,7 +919,6 @@
     for i in (1, 2):
         sums.second(i)
     for h in range(2):
-        ff_back.relay(2, h)
         sums_back.second(0, h)
 
     @pl.when(p.wt >= 4)
@@ -934,6 +936,8 @@
             dmid_o[sub(s)] + norm_back(base, rms_of(base), pack_ref[0:1], d_normed)
         ).astype(bf16)
         gt_gather.start(s)
+    for h in range(2):
+        ff_back.relay(2, h)
     for i in (1, 2):
         for h in range(2):
             sums_back.put(i, h, sums.own(i, h).astype(bf16))

time: 174 us -> 175 us (level)
  Pallas kernels: 156 us -> 159 us
    pallas_call x2, Pallas kernels: 149 us -> 151 us  [comm_call(): pl.pallas_call(kernel, out_shape=out_shape, in_specs=[first or vmem] + [v...]
where the time goes in v9:
time: 175 us
  Pallas kernels  159 us (91%)
  matrix products  8.26 us (5%)
  local copies, waits for them, and re-layouts  5.48 us (3%)
  other arithmetic  1.76 us (1%)
    pallas_call x2, Pallas kernels, comm_call(): pl.pallas_call(kernel, out_shape=out_shape, in_specs=[first or vmem] + [v...  151 us
    pallas_call x1, Pallas kernels, finish(): pl.pallas_call(finish_kernel, out_shape=(sds((512, 1024), bf16), sds((512...  4.98 us
    unnamed x22, local copies, waits for them, and re-layouts  4.53 us

profile of v9, /device:TPU:1, one launch (start us, length us, event | category | flops | bytes accessed | tf_op | source)
XLA Modules:
  0.0 175.1 jit_solution(15481681357139036384)
XLA Ops:
  0.6 0.0 copy-start
  0.7 0.0 copy-start.6
  0.7 0.0 copy-start.8
  0.7 0.1 pad.5.clone
  0.8 0.9 concatenate.9
  1.6 0.8 maximum_maximum_fusion.pack_ref
  2.4 1.0 pad_maximum_fusion.wkv_ref
  3.4 0.0 copy-start.1
  3.4 1.2 copy-done.1
  4.6 0.0 copy-start.3
  4.6 0.9 copy-done.3
  5.6 0.0 copy-start.5
  5.6 0.7 copy-done.5
  6.2 0.0 copy-start.2
  6.2 2.8 %project.1 = (bf16[512,1024]{1,0:T(8,128)(2,1)S(1)}, f32[512,128]{1,0:T(8,128)S(1)}, f32[512,128]{1,0:T(8,128)S(1)}, bf16[512,128]{1,0:T(8,128)(2,1)S(1)}, bf16[...) custom-call(s32[4]{0:T(128)S(1)} %copy-done.5, bf16[512,1024]{1,0:T(8,128)(2,1)S(1)} %copy-done.1, ...), custom_call_target="tpu_custom_call" | custom-call | tf_op jit(solution)/shard_map/project/pallas_call | solution.py:638
  9.0 0.0 copy-done.6
  9.0 0.0 copy-done.8
  9.0 0.0 copy-done.2
  9.1 0.0 copy-start.7
  9.1 1.2 copy-done.7
  10.3 0.0 copy-start.10
  10.3 50.7 %forward.1 = (bf16[4,4,2,256,128]{4,3,2,1,0:T(8,128)(2,1)S(1)}, bf16[8192,128]{1,0:T(8,128)(2,1)S(1)}, bf16[2,512,256]{2,1,0:T(8,128)(2,1)S(1)}, f32[2,256,128]{...) custom-call(s32[4]{0:T(128)S(1)} %copy-done.6, ...), custom_call_target="tpu_custom_call" | custom-call | flops 8589934592 | bytes 33554432 | tf_op jit(solution)/shard_map/forward/pallas_call | solution.py:555
  61.0 0.0 copy-done.10
  61.0 0.0 copy-start.9
  61.0 0.8 fusion.1
  61.8 0.4 copy-done.9
  62.3 0.8 fusion
  63.1 0.0 copy-done
  63.1 1.3 multiply_convert_fusion
  64.4 1.0 convolution_convert_fusion.3
  65.4 0.8 convolution_convert_fusion
  66.2 0.8 convolution_convert_fusion.2
  67.0 0.8 convolution_convert_fusion.1
  67.8 1.0 fusion.2
  68.8 0.0 copy-start.4
  68.8 1.0 add_convert_fusion
  69.8 0.0 copy-done.4
  69.8 100.1 %backward.1 = (bf16[8,64,1024]{2,1,0:T(8,128)(2,1)S(1)}, bf16[8,64,1024]{2,1,0:T(8,128)(2,1)S(1)}, bf16[3,2,4,4,32,128]{5,4,3,2,1,0:T(8,128)(2,1)S(1)}, bf16[3,2...) custom-call(bf16[8,64,1024]{2,1,0:T(8,128)(2,1)S(1)} %bitcast.59, bf16[8,64,1024]{2,1,0:T(8,128)(2,1)S(1)} %bitcast.58, ...), custom_call_target="tpu_custom_call" | custom-call | flops 8589934592 | bytes 33554432 | tf_op jit(solution)/shard_map/backward/pallas_call | solution.py:555
  169.9 5.0 %finish.1 = (bf16[512,1024]{1,0:T(8,128)(2,1)}, bf16[512,1024]{1,0:T(8,128)(2,1)}, f32[1024,128]{1,0:T(8,128)}, f32[64,1024]{1,0:T(8,128)}, f32[64,1024]{1,0:T(8...) custom-call(bf16[3,2,4,4,32,128]{5,4,3,2,1,0:T(8,128)(2,1)S(1)} %get, ...), custom_call_target="tpu_custom_call" | custom-call | tf_op jit(solution)/shard_map/finish/pallas_call | solution.py:1032
  (2 shorter events, 0.0 us)
Async XLA Ops:
  0.6 62.4 %copy-start = (bf16[1024,576]{0,1:T(8,128)(2,1)S(1)}, bf16[1024,576]{0,1:T(8,128)(2,1)}, u32[]{:S(2)}) copy-start(bf16[1024,576]{0,1:T(8,128)(2,1)} %param.24) | copy-start | bytes 3538948
  0.7 8.4 %copy-start.6 = (s32[4]{0:T(128)S(1)}, s32[4]{0:T(128)}, u32[]{:S(2)}) copy-start(s32[4]{0:T(128)} %len_ref.3) | copy-start | bytes 52
  0.7 8.4 %copy-start.8 = (bf16[128,1024]{1,0:T(8,128)(2,1)S(1)}, bf16[128,1024]{1,0:T(8,128)(2,1)}, u32[]{:S(2)}) copy-start(bf16[128,1024]{1,0:T(8,128)(2,1)} %w_ref.3) | copy-start | bytes 786436
  3.4 1.2 copy-start.1
  4.6 0.9 copy-start.3
  5.6 0.7 copy-start.5
  6.2 2.8 %copy-start.2 = (bf16[512,1024]{1,0:T(8,128)(2,1)S(1)}, bf16[512,1024]{1,0:T(8,128)(2,1)}, u32[]{:S(2)}) copy-start(bf16[512,1024]{1,0:T(8,128)(2,1)} %tok_ref.1) | copy-start | bytes 3145732
  9.1 1.2 copy-start.7
  10.3 50.7 %copy-start.10 = (bf16[1024,576]{0,1:T(8,128)(2,1)S(1)}, bf16[1024,576]{0,1:T(8,128)(2,1)}, u32[]{:S(2)}) copy-start(bf16[1024,576]{0,1:T(8,128)(2,1)} %param.23) | copy-start | bytes 3538948
  61.0 1.3 copy-start.9
  68.8 1.0 copy-start.4
